TPU v7x, 32 devices: a whole 2x2x4 slice. The times are simulated.
32 devices in a mesh: section: 2 (over x), dp: 4 (over z), mp: 4 (over y, core).
Axes of the slice: x: 2, y: 2, z: 4, core: 2. Of those that a mesh axis runs over, the one named last changes fastest.
Arguments:
- ends_in: bfloat16 [2, 8192, 768], P('section', 'dp'), may hold values from -6 to 6
- seq_lengths: int32 [8, 8], P('dp'), may hold values from 1 to 512, 1024 in all within a row
- norm_gains: bfloat16 [2, 768, 2], P('section', 'dp'), may hold values from 0.099609375 to 1.8984375
- qk_weight: bfloat16 [2, 768, 2, 768], P('section', 'dp', None, 'mp'), may hold values from -0.21875 to 0.21875
- value_weight: bfloat16 [768, 1152], P('dp'), may hold values from -0.21875 to 0.21875
- out_weight: bfloat16 [2, 768, 768], P('section', 'mp', 'dp'), may hold values from -2.5 to 2.5
- fc_weight: bfloat16 [2, 768, 3072], P('section', 'dp', 'mp'), may hold values from -0.21875 to 0.21875
- proj_weight: bfloat16 [2, 3072, 768], P('section', 'mp', 'dp'), may hold values from -0.109375 to 0.109375
Outputs:
- ends_out: bfloat16 [2, 8192, 768], P('section', 'dp')
- grad_attn_gain: float32 [2, 768], P('section', 'dp')
- grad_mlp_gain: float32 [2, 768], P('section', 'dp')
- grad_qk: float32 [2, 768, 2, 768], P('section', 'dp', None, 'mp')
- grad_value: float32 [768, 1152], P('dp')
- grad_out: float32 [2, 768, 768], P('section', 'mp', 'dp')
- grad_fc: float32 [2, 768, 3072], P('section', 'dp', 'mp')
- grad_proj: float32 [2, 3072, 768], P('section', 'mp', 'dp')
Inputs may be any that keep to these rules, and one draw needn't show every extreme that they name: `seq_lengths`: row b holds the lengths of the 8 sequences of micro-batch b; they sum to 1024, the longest is exactly 512.
All inputs are finite; a program needn't handle non-finite values.
Results may differ from a plain program's by a relative error of at most 0.03.
Values may be sent and summed in bfloat16 or wider, within the bound.
A program may use at most 192 MiB of HBM per device.

v0:
```python
import math

import jax
import jax.numpy as jnp
from jax import lax
from jax.sharding import PartitionSpec as P

D = 768
HEADS = 12
MB_TOK = 1024


EPSILON = 1e-05


def from_behind(value, axis, steps):
    count = lax.axis_size(axis)
    initial, last = (max(0, -steps), min(count, count - steps))
    return lax.ppermute(value, axis, [(source, source + steps) for source in range(initial, last)])


def inner_rows(left, right):
    return lax.dot_general(
        left, right, (((0,), (0,)), ((), ())), preferred_element_type=jnp.float32
    )


def times_back(left, right):
    return lax.dot_general(
        left, right, (((1,), (1,)), ((), ())), preferred_element_type=jnp.float32
    )


def normalize(in_rows, gain_row):
    row_mean = jnp.mean(in_rows, axis=1, keepdims=True)
    centred = in_rows - row_mean
    row_var = jnp.mean(centred * centred, axis=1, keepdims=True)
    factor = lax.rsqrt(row_var + EPSILON)
    plain_rows = centred * factor
    return (plain_rows * gain_row, plain_rows, factor)


def norm_back(grad_rows, plain_rows, factor, gain_row):
    scaled = grad_rows * gain_row
    inner_sum = (
        scaled
        - jnp.mean(scaled, axis=1, keepdims=True)
        - plain_rows * jnp.mean(scaled * plain_rows, axis=1, keepdims=True)
    )
    return (factor * inner_sum, jnp.sum(grad_rows * plain_rows, axis=0))


def segment_ids(lengths, row_count):
    seq_ends = jnp.cumsum(lengths)
    places = jnp.arange(row_count, dtype=jnp.int32)
    return jnp.sum((places[:, None] >= seq_ends[None, :]).astype(jnp.int32), axis=1)


def block_scores(query_block, key_heads, segment, block_start, scaling):
    block_rows = query_block.shape[0]
    seg_block = lax.dynamic_slice_in_dim(segment, block_start, block_rows, 0)
    pos_block = block_start + jnp.arange(block_rows, dtype=jnp.int32)
    places = jnp.arange(segment.shape[0], dtype=jnp.int32)
    allowed = (seg_block[:, None] == segment[None, :]) & (places[None, :] <= pos_block[:, None])
    scores = scaling * jnp.einsum(
        "qhd,khd->hqk", query_block, key_heads, preferred_element_type=jnp.float32
    )
    return jnp.where(allowed[None], scores, -1e30)


def attend_forward(query_vals, key_vals, value_vals, segment, head_count):
    row_count = query_vals.shape[0]
    head_width = query_vals.shape[1] // head_count
    block_rows = min(512, row_count)
    scaling = 1.0 / math.sqrt(head_width)
    query_heads = query_vals.reshape(row_count, head_count, head_width)
    key_heads = key_vals.reshape(row_count, head_count, head_width)
    value_heads = value_vals.reshape(row_count, head_count, head_width)

    def one_block(block_start):
        query_block = lax.dynamic_slice_in_dim(query_heads, block_start, block_rows, 0)
        scores = block_scores(query_block, key_heads, segment, block_start, scaling)
        row_max = jnp.max(scores, axis=2, keepdims=True)
        expo_vals = jnp.exp(scores - row_max)
        row_total = jnp.sum(expo_vals, axis=2, keepdims=True)
        prob_vals = (expo_vals / row_total).astype(jnp.bfloat16)
        attn_block = jnp.einsum(
            "hqk,khd->qhd", prob_vals, value_heads, preferred_element_type=jnp.float32
        )
        return (attn_block.astype(jnp.bfloat16), (row_max + jnp.log(row_total))[:, :, 0])

    block_starts = jnp.arange(row_count // block_rows, dtype=jnp.int32) * block_rows
    attn_blocks, log_sums = lax.map(one_block, block_starts)
    return (attn_blocks.reshape(row_count, head_count * head_width), log_sums)


def attend_backward(query_vals, key_vals, value_vals, grad_attn, log_sums, segment, head_count):
    row_count = query_vals.shape[0]
    head_width = query_vals.shape[1] // head_count
    block_rows = min(512, row_count)
    scaling = 1.0 / math.sqrt(head_width)
    query_heads = query_vals.reshape(row_count, head_count, head_width)
    key_heads = key_vals.reshape(row_count, head_count, head_width)
    value_heads = value_vals.reshape(row_count, head_count, head_width)
    grad_heads = grad_attn.reshape(row_count, head_count, head_width)

    def one_block(running, block_item):
        grad_key_sum, grad_value_sum = running
        block_start, block_logs = block_item
        query_block = lax.dynamic_slice_in_dim(query_heads, block_start, block_rows, 0)
        grad_block = lax.dynamic_slice_in_dim(grad_heads, block_start, block_rows, 0)
        scores = block_scores(query_block, key_heads, segment, block_start, scaling)
        prob_vals = jnp.exp(scores - block_logs[:, :, None])
        grad_probs = jnp.einsum(
            "qhd,khd->hqk", grad_block, value_heads, preferred_element_type=jnp.float32
        )
        inner_sum = jnp.sum(prob_vals * grad_probs, axis=2, keepdims=True)
        grad_scores = (prob_vals * (grad_probs - inner_sum)).astype(jnp.bfloat16)
        grad_query_block = (
            scaling
            * jnp.einsum("hqk,khd->qhd", grad_scores, key_heads, preferred_element_type=jnp.float32)
        ).astype(jnp.bfloat16)
        grad_key_sum = grad_key_sum + scaling * jnp.einsum(
            "hqk,qhd->khd", grad_scores, query_block, preferred_element_type=jnp.float32
        )
        grad_value_sum = grad_value_sum + jnp.einsum(
            "hqk,qhd->khd",
            prob_vals.astype(jnp.bfloat16),
            grad_block,
            preferred_element_type=jnp.float32,
        )
        return ((grad_key_sum, grad_value_sum), grad_query_block)

    block_starts = jnp.arange(row_count // block_rows, dtype=jnp.int32) * block_rows
    zero_heads = jnp.zeros((row_count, head_count, head_width), jnp.float32)
    (grad_key_sum, grad_value_sum), grad_query_blocks = lax.scan(
        one_block, (zero_heads, zero_heads), (block_starts, log_sums)
    )
    return (
        grad_query_blocks.reshape(row_count, -1),
        grad_key_sum.reshape(row_count, -1),
        grad_value_sum.reshape(row_count, -1),
    )


def layer_forward(in_rows, segment, weights, reused_values, reused, head_count):
    gain_pair, w_qk, w_value, w_out, w_up, w_down = weights
    head_cols = w_value.shape[1]
    normed, plain_one, factor_one = normalize(in_rows, gain_pair[:, 0].astype(jnp.float32))
    normed_low = normed.astype(jnp.bfloat16)
    query_keys = jnp.dot(
        normed_low, w_qk.reshape(w_qk.shape[0], 2 * head_cols), preferred_element_type=jnp.float32
    ).astype(jnp.bfloat16)
    query_vals = query_keys[:, :head_cols]
    key_vals = query_keys[:, head_cols:]
    fresh_vals = jnp.dot(normed_low, w_value, preferred_element_type=jnp.float32).astype(
        jnp.bfloat16
    )
    value_vals = jnp.where(reused, reused_values, fresh_vals)
    attn_mixed, log_sums = attend_forward(query_vals, key_vals, value_vals, segment, head_count)
    attn_part = jnp.dot(attn_mixed, w_out, preferred_element_type=jnp.float32)
    middle = in_rows + lax.psum(attn_part.astype(jnp.bfloat16), "mp").astype(jnp.float32)
    normed_two, plain_two, factor_two = normalize(middle, gain_pair[:, 1].astype(jnp.float32))
    normed_two_low = normed_two.astype(jnp.bfloat16)
    hidden = jnp.dot(normed_two_low, w_up, preferred_element_type=jnp.float32)
    acted_vals = jax.nn.gelu(hidden).astype(jnp.bfloat16)
    mlp_part = jnp.dot(acted_vals, w_down, preferred_element_type=jnp.float32)
    result = middle + lax.psum(mlp_part.astype(jnp.bfloat16), "mp").astype(jnp.float32)
    kept_vals = (
        plain_one,
        factor_one,
        normed_low,
        query_vals,
        key_vals,
        value_vals,
        attn_mixed,
        log_sums,
        plain_two,
        factor_two,
        normed_two_low,
        hidden,
        acted_vals,
    )
    return (result, kept_vals)


def layer_backward(grad_rows, kept_vals, weights, grad_values_in, reused, head_count, segment):
    gain_pair, w_qk, w_value, w_out, w_up, w_down = weights
    (
        plain_one,
        factor_one,
        normed_low,
        query_vals,
        key_vals,
        value_vals,
        attn_mixed,
        log_sums,
        plain_two,
        factor_two,
        normed_two_low,
        hidden,
        acted_vals,
    ) = kept_vals
    head_cols = w_value.shape[1]
    grad_low = grad_rows.astype(jnp.bfloat16)
    grad_down = inner_rows(acted_vals, grad_low)
    grad_acted = times_back(grad_low, w_down)
    grad_hidden = jax.vjp(jax.nn.gelu, hidden)[1](grad_acted)[0].astype(jnp.bfloat16)
    grad_up = inner_rows(normed_two_low, grad_hidden)
    grad_normed_two = lax.psum(times_back(grad_hidden, w_up).astype(jnp.bfloat16), "mp").astype(
        jnp.float32
    )
    middle_part, gain_two = norm_back(
        grad_normed_two, plain_two, factor_two, gain_pair[:, 1].astype(jnp.float32)
    )
    grad_middle = grad_rows + middle_part
    grad_middle_low = grad_middle.astype(jnp.bfloat16)
    grad_out = inner_rows(attn_mixed, grad_middle_low)
    grad_attn = times_back(grad_middle_low, w_out).astype(jnp.bfloat16)
    grad_query, grad_keys, grad_values = attend_backward(
        query_vals, key_vals, value_vals, grad_attn, log_sums, segment, head_count
    )
    grad_values_low = (grad_values + grad_values_in).astype(jnp.bfloat16)
    grad_own = jnp.where(reused, jnp.zeros_like(grad_values_low), grad_values_low)
    grad_query_keys = jnp.concatenate([grad_query, grad_keys.astype(jnp.bfloat16)], axis=1)
    grad_qk = inner_rows(normed_low, grad_query_keys).reshape(normed_low.shape[1], 2, head_cols)
    grad_value = inner_rows(normed_low, grad_own)
    grad_normed_part = times_back(
        grad_query_keys, w_qk.reshape(w_qk.shape[0], 2 * head_cols)
    ) + times_back(grad_own, w_value)
    grad_normed = lax.psum(grad_normed_part.astype(jnp.bfloat16), "mp").astype(jnp.float32)
    input_part, gain_one = norm_back(
        grad_normed, plain_one, factor_one, gain_pair[:, 0].astype(jnp.float32)
    )
    grad_input = grad_middle + input_part
    grad_gain_pair = jnp.stack([gain_one, gain_two], axis=1)
    return (
        grad_input,
        grad_values_low,
        (grad_gain_pair, grad_qk, grad_value, grad_up),
        (grad_out, grad_down),
    )


def shards(
    ends_in, seq_lengths, norm_gains, qk_weight, value_weight, out_weight, fc_weight, proj_weight
):
    section_idx = lax.axis_index("section")
    first_section = section_idx == 0
    per_group = HEADS // lax.axis_size("mp")
    head_width = D // HEADS
    head_cols = qk_weight.shape[3]
    start_head = lax.axis_index("mp") * per_group
    reused = jnp.logical_and(section_idx == 1, start_head >= HEADS // 2)
    value_offset = jnp.where(
        first_section,
        start_head * head_width,
        D + jnp.minimum(start_head, HEADS // 2 - per_group) * head_width,
    )
    value_piece = lax.dynamic_slice_in_dim(value_weight, value_offset, head_cols, 1)
    gain_pair, w_qk, w_value, w_up = (
        lax.all_gather(norm_gains[0], "dp", axis=0, tiled=True),
        lax.all_gather(qk_weight[0], "dp", axis=0, tiled=True),
        lax.all_gather(value_piece, "dp", axis=0, tiled=True),
        lax.all_gather(fc_weight[0], "dp", axis=0, tiled=True),
    )
    w_out, w_down = (
        lax.all_gather(out_weight[0], "dp", axis=1, tiled=True),
        lax.all_gather(proj_weight[0], "dp", axis=1, tiled=True),
    )
    weights = (gain_pair, w_qk, w_value, w_out, w_up, w_down)
    local_rows = ends_in[0]
    batches = seq_lengths.shape[0]
    segments = [segment_ids(seq_lengths[index], MB_TOK) for index in range(batches)]
    arrived = (jnp.zeros((MB_TOK, D), jnp.bfloat16), jnp.zeros((MB_TOK, head_cols), jnp.bfloat16))
    saved = []
    outputs = []
    for step_index in range(batches + 1):
        own_index = min(step_index, batches - 1)
        late_index = max(step_index - 1, 0)
        own_rows = local_rows[own_index * MB_TOK : (own_index + 1) * MB_TOK].astype(jnp.float32)
        in_rows = jnp.where(first_section, own_rows, arrived[0].astype(jnp.float32))
        segment = jnp.where(first_section, segments[own_index], segments[late_index])
        result, kept_vals = layer_forward(in_rows, segment, weights, arrived[1], reused, per_group)
        saved.append((kept_vals, segment))
        outputs.append(result)
        if step_index < batches:
            arrived = from_behind((result.astype(jnp.bfloat16), kept_vals[5]), "section", 1)
    returned = (jnp.zeros((MB_TOK, D), jnp.bfloat16), jnp.zeros((MB_TOK, head_cols), jnp.bfloat16))
    grads_in = [None] * batches
    row_sums = None
    col_sums = None
    for step_index in range(batches + 1):
        kept_vals, segment = saved[batches - step_index]
        late_index = max(batches - 1 - step_index, 0)
        own_grad = local_rows[late_index * MB_TOK : (late_index + 1) * MB_TOK].astype(jnp.float32)
        grad_rows = jnp.where(first_section, returned[0].astype(jnp.float32), own_grad)
        grad_values_in = jnp.where(first_section, returned[1].astype(jnp.float32), 0.0)
        grad_input, grad_values_low, row_terms, col_terms = layer_backward(
            grad_rows, kept_vals, weights, grad_values_in, reused, per_group, segment
        )
        valid_flag = jnp.where(first_section, float(step_index >= 1), float(step_index < batches))
        row_terms = tuple((term_part * valid_flag for term_part in row_terms))
        col_terms = tuple((term_part * valid_flag for term_part in col_terms))
        if row_sums is None:
            row_sums = tuple(row_terms)
            col_sums = tuple(col_terms)
        else:
            row_sums = tuple(
                (old_part + new_part for old_part, new_part in zip(row_sums, row_terms))
            )
            col_sums = tuple(
                (old_part + new_part for old_part, new_part in zip(col_sums, col_terms))
            )
        if step_index >= 1:
            grads_in[batches - step_index] = grad_input
        if step_index < batches:
            send_values = jnp.where(reused, grad_values_low, jnp.zeros_like(grad_values_low))
            returned = from_behind((grad_input.astype(jnp.bfloat16), send_values), "section", -1)
    row_grads = (
        lax.psum_scatter(
            row_sums[0].astype(jnp.bfloat16), "dp", scatter_dimension=0, tiled=True
        ).astype(jnp.float32),
        lax.psum_scatter(
            row_sums[1].astype(jnp.bfloat16), "dp", scatter_dimension=0, tiled=True
        ).astype(jnp.float32),
        lax.psum_scatter(
            row_sums[2].astype(jnp.bfloat16), "dp", scatter_dimension=0, tiled=True
        ).astype(jnp.float32),
        lax.psum_scatter(
            row_sums[3].astype(jnp.bfloat16), "dp", scatter_dimension=0, tiled=True
        ).astype(jnp.float32),
    )
    col_grads = (
        lax.psum_scatter(
            col_sums[0].astype(jnp.bfloat16), "dp", scatter_dimension=1, tiled=True
        ).astype(jnp.float32),
        lax.psum_scatter(
            col_sums[1].astype(jnp.bfloat16), "dp", scatter_dimension=1, tiled=True
        ).astype(jnp.float32),
    )
    grad_gain_rows, grad_qk_rows, grad_value_rows, grad_up_rows = row_grads
    grad_out_cols, grad_down_cols = col_grads
    value_zeros = jnp.zeros((grad_value_rows.shape[0], value_weight.shape[1]), jnp.float32)
    value_placed = lax.dynamic_update_slice_in_dim(value_zeros, grad_value_rows, value_offset, 1)
    grad_value_all = lax.psum(value_placed.astype(jnp.bfloat16), ("section", "mp")).astype(
        jnp.float32
    )
    ends_out = jnp.where(
        first_section, jnp.concatenate(grads_in, axis=0), jnp.concatenate(outputs[1:], axis=0)
    ).astype(jnp.bfloat16)[None]
    attn_gain_grad = grad_gain_rows[:, 0][None]
    mlp_gain_grad = grad_gain_rows[:, 1][None]
    return (
        ends_out,
        attn_gain_grad,
        mlp_gain_grad,
        grad_qk_rows[None],
        grad_value_all,
        grad_out_cols[None],
        grad_up_rows[None],
        grad_down_cols[None],
    )


def solution(mesh):
    in_specs = (
        P("section", "dp", None),
        P("dp", None),
        P("section", "dp", None),
        P("section", "dp", None, "mp"),
        P("dp", None),
        P("section", "mp", "dp"),
        P("section", "dp", "mp"),
        P("section", "mp", "dp"),
    )
    out_specs = (
        P("section", "dp", None),
        P("section", "dp"),
        P("section", "dp"),
        P("section", "dp", None, "mp"),
        P("dp", None),
        P("section", "mp", "dp"),
        P("section", "dp", "mp"),
        P("section", "mp", "dp"),
    )
    return jax.shard_map(shards, mesh=mesh, in_specs=in_specs, out_specs=out_specs, check_vma=False)
```

profile of v0, /device:TPU:0, one launch (start us, length us, event | category | flops | bytes accessed | tf_op | source)
XLA Modules:
  0.0 1369.5 jit_solution(9097712118380652623)
XLA Ops:
  9.1 16.8 %all_gather.20 = bf16[768,192]{1,0:T(8,128)(2,1)} all-gather(bf16[192,192]{1,0:T(8,128)(2,1)S(1)} %constant_dynamic-slice_fusion), channel_id=1, replica_groups=mesh['section'=2,'dp'=4,'mp'=4] {'dp'}, dimensions={0}, use_global_device_ids=true | all-gather | bytes 368640 | tf_op jit(solution)/shard_map/all_gather | solution.py:264
  30.8 15.8 %all-gather = bf16[1,768,2]{2,0,1:T(2,128)(2,1)S(1)} all-gather(bf16[1,192,2]{2,0,1:T(2,128)(2,1)} %copy.73), channel_id=2, replica_groups=mesh['section'=2,'dp'=4,'mp'=4] {'dp'}, dimensions={1}, use_global_device_ids=true | all-gather | bytes 3840 | tf_op jit(solution)/shard_map/all_gather | solution.py:262
  47.4 19.1 %all-gather.1 = bf16[1,768,2,192]{3,2,0,1:T(2,128)(2,1)} all-gather(bf16[1,192,2,192]{3,2,0,1:T(2,128)(2,1)} %bitcast.532), channel_id=3, replica_groups=mesh['section'=2,'dp'=4,'mp'=4] {'dp'}, dimensions={1}, use_global_device_ids=true | all-gather | bytes 737280 | tf_op jit(solution)/shard_map/all_gather | solution.py:263
  79.2 26.4 %while.81 = (s32[]{:T(128)}, bf16[2,512,3,64]{1,3,2,0:T(8,128)(2,1)}, f32[2,3,512]{2,1,0:T(4,128)}, s32[2]{0:T(128)}, s32[1024]{0:T(1024)S(1)}, /*index=5*/bf16[...) while((s32[]{:T(128)}, ...), condition=%wide.region_7.8_spmd, body=%wide.region_4.7_spmd.sunk | while | flops 423197696 | bytes 22217896 | solution.py:93
  109.7 17.6 %all-gather.2 = bf16[1,192,768]{1,0,2:T(2,128)(2,1)} all-gather(bf16[1,192,192]{1,0,2:T(2,128)(2,1)} %copy.78), channel_id=4, replica_groups=mesh['section'=2,'dp'=4,'mp'=4] {'dp'}, dimensions={2}, use_global_device_ids=true | all-gather | bytes 368640 | tf_op jit(solution)/shard_map/all_gather | solution.py:268
  134.5 41.4 %all-reduce.14.cloned.1.call-done = bf16[1024,768]{1,0:T(8,128)(2,1)} async-done(((bf16[1024,768]{1,0:T(8,128)(2,1)}), bf16[1024,768]{1,0:T(8,128)(2,1)}) %all-reduce.14.cloned.1.call-update) | async-done | bytes 1572880 | tf_op jit(solution)/shard_map/psum | solution.py:162
  178.9 5.2 fusion.259
  184.2 11.8 all-gather.10.cloned.1.call-done
  196.0 5.4 convolution_convert_fusion.7
  201.5 42.2 %all-reduce.16.cloned.1.call-done = bf16[1024,768]{1,0:T(8,128)(2,1)} async-done(((bf16[1024,768]{1,0:T(8,128)(2,1)}), bf16[1024,768]{1,0:T(8,128)(2,1)}) %all-reduce.16.cloned.1.call-update) | async-done | bytes 1572880 | tf_op jit(solution)/shard_map/psum | solution.py:168
  247.4 4.5 collective-permute-start
  254.5 31.4 %collective-permute-done = bf16[1024,768]{1,0:T(8,128)(2,1)} collective-permute-done((bf16[1024,768]{1,0:T(8,128)(2,1)}, bf16[1024,768]{1,0:T(8,128)(2,1)}, u32[]{:S(2)}, u32[]{:S(2)}) %collective-permute-start) | collective-permute-done | bytes 1572896 | tf_op jit(solution)/shard_map/ppermute | solution.py:19
  296.6 26.4 %while.82 = (s32[]{:T(128)}, bf16[2,512,3,64]{1,3,2,0:T(8,128)(2,1)}, f32[2,3,512]{2,1,0:T(4,128)}, s32[2]{0:T(128)}, s32[1024]{0:T(1024)S(1)}, /*index=5*/bf16[...) while((s32[]{:T(128)}, ...), condition=%wide.region_19.20_spmd, body=%wide.region_16.19_spmd.sunk | while | flops 423197696 | bytes 22217896 | solution.py:93
  328.7 44.5 %all-reduce.18.cloned.1.call-done = bf16[1024,768]{1,0:T(8,128)(2,1)} async-done(((bf16[1024,768]{1,0:T(8,128)(2,1)}), bf16[1024,768]{1,0:T(8,128)(2,1)}) %all-reduce.18.cloned.1.call-update) | async-done | bytes 1572880 | tf_op jit(solution)/shard_map/psum | solution.py:162
  384.5 43.0 %all-reduce.20.cloned.1.call-done = bf16[1024,768]{1,0:T(8,128)(2,1)} async-done(((bf16[1024,768]{1,0:T(8,128)(2,1)}), bf16[1024,768]{1,0:T(8,128)(2,1)}) %all-reduce.20.cloned.1.call-update) | async-done | bytes 1572880 | tf_op jit(solution)/shard_map/psum | solution.py:168
  431.4 4.5 collective-permute-start.2
  437.4 32.5 %collective-permute-done.2 = bf16[1024,768]{1,0:T(8,128)(2,1)} collective-permute-done((bf16[1024,768]{1,0:T(8,128)(2,1)}, bf16[1024,768]{1,0:T(8,128)(2,1)}, u32[]{:S(2)}, u32[]{:S(2)}) %collective-permute-start.2) | collective-permute-done | bytes 1572896 | tf_op jit(solution)/shard_map/ppermute | solution.py:19
  480.7 24.4 %while.83 = (s32[]{:T(128)}, bf16[2,512,3,64]{1,3,2,0:T(8,128)(2,1)}, f32[2,3,512]{2,1,0:T(4,128)}, s32[2]{0:T(128)}, s32[1024]{0:T(1024)S(1)}, /*index=5*/bf16[...) while((s32[]{:T(128)}, ...), condition=%wide.region_29.30_spmd, body=%wide.region_26.29_spmd.sunk | while | flops 423197696 | bytes 23790788 | solution.py:93
  510.5 43.8 %all-reduce.22.cloned.1.call-done = bf16[1024,768]{1,0:T(8,128)(2,1)} async-done(((bf16[1024,768]{1,0:T(8,128)(2,1)}), bf16[1024,768]{1,0:T(8,128)(2,1)}) %all-reduce.22.cloned.1.call-update) | async-done | bytes 1572880 | tf_op jit(solution)/shard_map/psum | solution.py:162
  567.4 43.0 %all-reduce.24.cloned.1.call-done = bf16[1024,768]{1,0:T(8,128)(2,1)} async-done(((bf16[1024,768]{1,0:T(8,128)(2,1)}), bf16[1024,768]{1,0:T(8,128)(2,1)}) %all-reduce.24.cloned.1.call-update) | async-done | bytes 1572880 | tf_op jit(solution)/shard_map/psum | solution.py:210
  610.4 4.5 fusion.160
  619.8 41.3 %while.84 = (s32[]{:T(128)}, f32[1024,3,64]{0,2,1:T(8,128)}, f32[1024,3,64]{0,2,1:T(8,128)}, bf16[2,512,3,64]{1,3,2,0:T(8,128)(2,1)}, s32[2]{0:T(128)}, /*index=...) while((s32[]{:T(128)}, f32[1024,3,64]{0,2,1:T(8,128)}, ...), condition=%wide.region_38.39_spmd.clone, body=%wide.region_36.38_spmd.clone.sunk | while | flops 1032977408 | bytes 113896376 | solution.py:136
  656.9 4.2 fusion.474
  669.1 43.0 %all-reduce.26.cloned.1.call-done = bf16[1024,768]{1,0:T(8,128)(2,1)} async-done(((bf16[1024,768]{1,0:T(8,128)(2,1)}), bf16[1024,768]{1,0:T(8,128)(2,1)}) %all-reduce.26.cloned.1.call-update) | async-done | bytes 1572880 | tf_op jit(solution)/shard_map/psum | solution.py:231
  712.2 16.3 %fusion.166 = (f32[768]{0:T(1024)}, f32[1024]{0:T(1024)S(1)}, f32[1024]{0:T(1024)S(1)}) fusion(bf16[1024,768]{1,0:T(8,128)(2,1)} %all-reduce.26.cloned.1.call-done, f32[1024]{0:T(1024)S(1)} %copy-done.123, f32[1024]{0:T(1024)S(1)} %copy-done.109, bf16[1024,768]{1,0:T(8,128)(2,1)} %collective-permute-done.2, bf16[1,2048,768]{2,1,0:T(8,128)(2,1)S(1)} %copy-done.9, ...), kind=kLoop, calls=%fused_computation.217 | loop fusion | flops 9434368 | bytes 4741121 | tf_op jit(solution)/shard_map/reduce_sum | solution.py:50
  732.8 36.6 %collective-permute-done.4 = bf16[1024,768]{1,0:T(8,128)(2,1)S(1)} collective-permute-done((bf16[1024,768]{1,0:T(8,128)(2,1)S(1)}, bf16[1024,768]{1,0:T(8,128)(2,1)S(1)}, u32[]{:S(2)}, u32[]{:S(2)}) %collective-permute-start.4) | collective-permute-done | bytes 1572896 | tf_op jit(solution)/shard_map/ppermute | solution.py:19
  777.7 41.1 %all-reduce.28.cloned.1.call-done = bf16[1024,768]{1,0:T(8,128)(2,1)} async-done(((bf16[1024,768]{1,0:T(8,128)(2,1)}), bf16[1024,768]{1,0:T(8,128)(2,1)}) %all-reduce.28.cloned.1.call-update) | async-done | bytes 1572880 | tf_op jit(solution)/shard_map/psum | solution.py:210
  818.8 4.5 fusion.171
  829.3 43.8 %while.85 = (s32[]{:T(128)}, f32[1024,3,64]{0,2,1:T(8,128)}, f32[1024,3,64]{0,2,1:T(8,128)}, bf16[2,512,3,64]{1,3,2,0:T(8,128)(2,1)}, s32[2]{0:T(128)}, /*index=...) while((s32[]{:T(128)}, f32[1024,3,64]{0,2,1:T(8,128)}, ...), condition=%wide.region_47.48_spmd.clone, body=%wide.region_45.47_spmd.clone.sunk | while | flops 1032977408 | bytes 112323472 | solution.py:136
  881.1 43.0 %all-reduce.30.cloned.1.call-done = bf16[1024,768]{1,0:T(8,128)(2,1)} async-done(((bf16[1024,768]{1,0:T(8,128)(2,1)}), bf16[1024,768]{1,0:T(8,128)(2,1)}) %all-reduce.30.cloned.1.call-update) | async-done | bytes 1572880 | tf_op jit(solution)/shard_map/psum | solution.py:231
  924.1 4.6 fusion.176
  933.6 36.9 %collective-permute-done.6 = bf16[1024,768]{1,0:T(8,128)(2,1)} collective-permute-done((bf16[1024,768]{1,0:T(8,128)(2,1)}, bf16[1024,768]{1,0:T(8,128)(2,1)}, u32[]{:S(2)}, u32[]{:S(2)}) %collective-permute-start.6) | collective-permute-done | bytes 1572896 | tf_op jit(solution)/shard_map/ppermute | solution.py:19
  970.5 5.7 fusion.194
  980.0 5.3 fusion.226
  989.6 32.8 %all-reduce.32.cloned.1.call-done = bf16[1024,768]{1,0:T(8,128)(2,1)} async-done(((bf16[1024,768]{1,0:T(8,128)(2,1)}), bf16[1024,768]{1,0:T(8,128)(2,1)}) %all-reduce.32.cloned.1.call-update) | async-done | bytes 1572880 | tf_op jit(solution)/shard_map/psum | solution.py:210
  1022.4 4.6 fusion.181
  1033.4 44.5 %while.86 = (s32[]{:T(128)}, f32[1024,3,64]{0,2,1:T(8,128)}, f32[1024,3,64]{0,2,1:T(8,128)}, bf16[2,512,3,64]{1,3,2,0:T(8,128)(2,1)}, s32[2]{0:T(128)}, /*index=...) while((s32[]{:T(128)}, f32[1024,3,64]{0,2,1:T(8,128)}, ...), condition=%wide.region_56.57_spmd.clone, body=%wide.region_54.56_spmd.clone.sunk | while | flops 1032977408 | bytes 112323472 | solution.py:136
  1098.3 5.7 reduce-scatter.15.cloned.1.call-done
  1110.7 4.6 fusion.272
  1115.3 4.6 add_convert_fusion.4
  1122.6 4.2 fusion.308
  1132.3 5.4 convolution_convert_fusion
  1149.7 31.2 %all-reduce.34.cloned.1.call-done = bf16[192,1152]{1,0:T(8,128)(2,1)} async-done(((bf16[192,1152]{1,0:T(8,128)(2,1)}), bf16[192,1152]{1,0:T(8,128)(2,1)}) %all-reduce.34.cloned.1.call-update) | async-done | bytes 442384 | tf_op jit(solution)/shard_map/psum | solution.py:346
  1182.8 22.9 %reduce-scatter.13.cloned.1.call-done = bf16[192,2,192]{2,0,1:T(8,128)(2,1)} async-done(((bf16[768,2,192]{2,0,1:T(8,128)(2,1)}), bf16[192,2,192]{2,0,1:T(8,128)(2,1)}) %reduce-scatter.13.cloned.1.call-update) | async-done | bytes 147472 | tf_op jit(solution)/shard_map/reduce_scatter | solution.py:324
  1207.7 28.9 %reduce-scatter.23.cloned.1.call-done = bf16[192,768]{1,0:T(8,128)(2,1)} async-done(((bf16[768,768]{1,0:T(8,128)(2,1)}), bf16[192,768]{1,0:T(8,128)(2,1)}) %reduce-scatter.23.cloned.1.call-update) | async-done | bytes 294928
  1240.9 25.7 %reduce-scatter.17.cloned.1.call-done = bf16[192,768]{1,0:T(8,128)(2,1)} async-done(((bf16[768,768]{1,0:T(8,128)(2,1)}), bf16[192,768]{1,0:T(8,128)(2,1)}) %reduce-scatter.17.cloned.1.call-update) | async-done | bytes 294928 | tf_op jit(solution)/shard_map/reduce_scatter | solution.py:330
  1268.4 68.1 %all-reduce.36.cloned.1.call-done = (bf16[1024,768]{1,0:T(8,128)(2,1)}, bf16[1024,768]{1,0:T(8,128)(2,1)}) async-done(((bf16[1024,768]{1,0:T(8,128)(2,1)}, bf16[1024,768]{1,0:T(8,128)(2,1)}), (bf16[1024,768]{1,0:T(8,128)(2,1)}, bf16[1024,768]{1,0:T(8,128)(2,1)})) %all-reduce.36.cloned.1.call-update) | async-done | bytes 3145744 | tf_op jit(solution)/shard_map/psum | solution.py:231
  1349.0 11.1 reduce-scatter.19.cloned.1.call-done
  (696 shorter events, 409.1 us)
Async XLA Ops:
  8.0 167.8 %all-reduce.14.cloned.1.call-start = ((), (), s32[]{:S(2)}) async-start(), calls=%async_computation.6 | async-start | bytes 3145728 | tf_op jit(solution)/shard_map/psum | solution.py:162
  27.8 47.2 %copy-start.110 = (f32[1024]{0:T(1024)}, f32[1024]{0:T(1024)S(1)}, u32[]{:S(2)}) copy-start(f32[1024]{0:T(1024)S(1)} %broadcast_multiply_fusion.17) | copy-start | bytes 12292
  29.9 45.1 %copy-start.124 = (f32[1024]{0:T(1024)}, f32[1024]{0:T(1024)S(1)}, u32[]{:S(2)}) copy-start(f32[1024]{0:T(1024)S(1)} %add_rsqrt_fusion.5) | copy-start | bytes 12292
  47.4 426.6 %copy-start.98 = (f32[768]{0:T(1024)}, f32[768]{0:T(1024)S(1)}, u32[]{:S(2)}) copy-start(f32[768]{0:T(1024)S(1)} %get-tuple-element.496) | copy-start | bytes 9220
  105.6 148.9 %copy-start.93 = (s32[1024]{0:T(1024)}, s32[1024]{0:T(1024)S(1)}, u32[]{:S(2)}) copy-start(s32[1024]{0:T(1024)S(1)} %get-tuple-element.1333) | copy-start | bytes 12292
  133.0 45.9 %all-gather.8.cloned.1.call-start = ((), (), s32[]{:S(2)}) async-start(), calls=%async_computation.20 | async-start | bytes 1474560 | tf_op jit(solution)/shard_map/all_gather | solution.py:265
  133.6 62.4 %all-gather.10.cloned.1.call-start = ((), (), s32[]{:S(2)}) async-start(), calls=%async_computation.21 | async-start | bytes 1474560 | tf_op jit(solution)/shard_map/all_gather | solution.py:269
  134.2 109.4 %all-reduce.16.cloned.1.call-start = ((), (), s32[]{:S(2)}) async-start(), calls=%async_computation.7 | async-start | bytes 3145728 | tf_op jit(solution)/shard_map/psum | solution.py:168
  201.4 52.8 %copy-start.146 = (s32[8,1]{0,1:T(1,128)S(1)}, s32[8,1]{0,1:T(1,128)}, u32[]{:S(2)}) copy-start(s32[8,1]{0,1:T(1,128)} %get-tuple-element.642) | copy-start | bytes 100
  201.4 171.8 %all-reduce.18.cloned.1.call-start = ((), (), s32[]{:S(2)}) async-start(), calls=%async_computation.8 | async-start | bytes 3145728 | tf_op jit(solution)/shard_map/psum | solution.py:162
  247.4 38.5 %collective-permute-start = (bf16[1024,768]{1,0:T(8,128)(2,1)}, bf16[1024,768]{1,0:T(8,128)(2,1)}, u32[]{:S(2)}, u32[]{:S(2)}) collective-permute-start(bf16[1024,768]{1,0:T(8,128)(2,1)} %add_convert_fusion.3), channel_id=1, source_target_pairs={{0,16},{1,17},{2,18},{3,19},{4,20},{5,21},{6,22},{7,23},{8,24},{9,... | collective-permute-start | bytes 4718600 | tf_op jit(solution)/shard_map/ppermute | solution.py:19
  251.9 41.9 %collective-permute-start.1 = (bf16[1024,192]{0,1:T(8,128)(2,1)}, bf16[1024,192]{0,1:T(8,128)(2,1)}, u32[]{:S(2)}, u32[]{:S(2)}) collective-permute-start(bf16[1024,192]{0,1:T(8,128)(2,1)} %fusion.238), channel_id=1, source_target_pairs={{0,16},{1,17},{2,18},{3,19},{4,20},{5,21},{6,22},{7,23},{8,24},{9,... | collective-permute-start | bytes 1179656 | tf_op jit(solution)/shard_map/ppermute | solution.py:19
  323.1 52.8 %copy-start.23 = (bf16[1024,3,64]{0,2,1:T(8,128)(2,1)}, bf16[1024,3,64]{0,2,1:T(8,128)(2,1)S(1)}, u32[]{:S(2)}) copy-start(bf16[1024,3,64]{0,2,1:T(8,128)(2,1)S(1)} %get-tuple-element.1266) | copy-start | bytes 1179652
  323.1 52.8 %copy-start.95 = (s32[1024]{0:T(1024)}, s32[1024]{0:T(1024)S(1)}, u32[]{:S(2)}) copy-start(s32[1024]{0:T(1024)S(1)} %get-tuple-element.1337) | copy-start | bytes 12292
  328.2 99.3 %all-reduce.20.cloned.1.call-start = ((), (), s32[]{:S(2)}) async-start(), calls=%async_computation.9 | async-start | bytes 3145728 | tf_op jit(solution)/shard_map/psum | solution.py:168
  384.4 169.8 %all-reduce.22.cloned.1.call-start = ((), (), s32[]{:S(2)}) async-start(), calls=%async_computation.10 | async-start | bytes 3145728 | tf_op jit(solution)/shard_map/psum | solution.py:162
  431.4 38.5 %collective-permute-start.2 = (bf16[1024,768]{1,0:T(8,128)(2,1)}, bf16[1024,768]{1,0:T(8,128)(2,1)}, u32[]{:S(2)}, u32[]{:S(2)}) collective-permute-start(bf16[1024,768]{1,0:T(8,128)(2,1)} %fusion.214), channel_id=1, source_target_pairs={{0,16},{1,17},{2,18},{3,19},{4,20},{5,21},{6,22},{7,23},{8,24},{9,... | collective-permute-start | bytes 4718600 | tf_op jit(solution)/shard_map/ppermute | solution.py:19
  435.9 42.6 %collective-permute-start.3 = (bf16[1024,192]{0,1:T(8,128)(2,1)}, bf16[1024,192]{0,1:T(8,128)(2,1)S(1)}, u32[]{:S(2)}, u32[]{:S(2)}) collective-permute-start(bf16[1024,192]{0,1:T(8,128)(2,1)} %fusion.239), channel_id=1, source_target_pairs={{0,16},{1,17},{2,18},{3,19},{4,20},{5,21},{6,22},{7,23},{8,24},{9,... | collective-permute-start | bytes 1179656 | tf_op jit(solution)/shard_map/ppermute | solution.py:19
  510.2 100.1 %all-reduce.24.cloned.1.call-start = ((), (), s32[]{:S(2)}) async-start(), calls=%async_computation.11 | async-start | bytes 3145728 | tf_op jit(solution)/shard_map/psum | solution.py:210
  556.9 58.0 %copy-start.118 = (f32[1024]{0:T(1024)}, f32[1024]{0:T(1024)S(1)}, u32[]{:S(2)}) copy-start(f32[1024]{0:T(1024)S(1)} %broadcast_multiply_fusion.12) | copy-start | bytes 12292
  559.0 55.9 %copy-start.133 = (f32[1024]{0:T(1024)}, f32[1024]{0:T(1024)S(1)}, u32[]{:S(2)}) copy-start(f32[1024]{0:T(1024)S(1)} %add_rsqrt_fusion) | copy-start | bytes 12292
  567.3 144.8 %all-reduce.26.cloned.1.call-start = ((), (), s32[]{:S(2)}) async-start(), calls=%async_computation.12 | async-start | bytes 3145728 | tf_op jit(solution)/shard_map/psum | solution.py:231
  669.1 149.7 %all-reduce.28.cloned.1.call-start = ((), (), s32[]{:S(2)}) async-start(), calls=%async_computation.13 | async-start | bytes 3145728 | tf_op jit(solution)/shard_map/psum | solution.py:210
  731.4 38.0 %collective-permute-start.4 = (bf16[1024,768]{1,0:T(8,128)(2,1)S(1)}, bf16[1024,768]{1,0:T(8,128)(2,1)S(1)}, u32[]{:S(2)}, u32[]{:S(2)}) collective-permute-start(bf16[1024,768]{1,0:T(8,128)(2,1)S(1)} %fusion.164), channel_id=1, source_target_pairs={{16,0},{17,1},{18,2},{19,3},{20,4},{21,5},{22,6},{23,7},{24,8},{25... | collective-permute-start | bytes 4718600 | tf_op jit(solution)/shard_map/ppermute | solution.py:19
  773.7 45.1 %copy-start.103 = (f32[768]{0:T(1024)S(1)}, f32[768]{0:T(1024)}, u32[]{:S(2)}) copy-start(f32[768]{0:T(1024)} %get-tuple-element.495) | copy-start | bytes 9220
  773.7 45.1 %copy-start.113 = (f32[1024]{0:T(1024)S(1)}, f32[1024]{0:T(1024)}, u32[]{:S(2)}) copy-start(f32[1024]{0:T(1024)} %copy-done.112) | copy-start | bytes 12292
  773.7 45.1 %copy-start.128 = (f32[1024]{0:T(1024)S(1)}, f32[1024]{0:T(1024)}, u32[]{:S(2)}) copy-start(f32[1024]{0:T(1024)} %copy-done.127) | copy-start | bytes 12292
  776.3 147.8 %all-reduce.30.cloned.1.call-start = ((), (), s32[]{:S(2)}) async-start(), calls=%async_computation.14 | async-start | bytes 3145728 | tf_op jit(solution)/shard_map/psum | solution.py:231
  776.4 100.6 %collective-permute-start.5 = (bf16[1024,192]{0,1:T(8,128)(2,1)}, bf16[1024,192]{0,1:T(8,128)(2,1)}, u32[]{:S(2)}, u32[]{:S(2)}) collective-permute-start(bf16[1024,192]{0,1:T(8,128)(2,1)} %bitcast.41), channel_id=1, source_target_pairs={{16,0},{17,1},{18,2},{19,3},{20,4},{21,5},{22,6},{23,7},{24,8},{25... | collective-permute-start | bytes 1179656 | tf_op jit(solution)/shard_map/ppermute | solution.py:19
  879.1 45.0 %copy-start.107 = (f32[1024]{0:T(1024)S(1)}, f32[1024]{0:T(1024)}, u32[]{:S(2)}) copy-start(f32[1024]{0:T(1024)} %copy-done.106) | copy-start | bytes 12292
  879.1 45.0 %copy-start.121 = (f32[1024]{0:T(1024)S(1)}, f32[1024]{0:T(1024)}, u32[]{:S(2)}) copy-start(f32[1024]{0:T(1024)} %copy-done.120) | copy-start | bytes 12292
  881.0 141.3 %all-reduce.32.cloned.1.call-start = ((), (), s32[]{:S(2)}) async-start(), calls=%async_computation.15 | async-start | bytes 3145728 | tf_op jit(solution)/shard_map/psum | solution.py:210
  932.3 38.2 %collective-permute-start.6 = (bf16[1024,768]{1,0:T(8,128)(2,1)}, bf16[1024,768]{1,0:T(8,128)(2,1)}, u32[]{:S(2)}, u32[]{:S(2)}) collective-permute-start(bf16[1024,768]{1,0:T(8,128)(2,1)} %fusion.174), channel_id=1, source_target_pairs={{16,0},{17,1},{18,2},{19,3},{20,4},{21,5},{22,6},{23,7},{24,8},{25... | collective-permute-start | bytes 4718600 | tf_op jit(solution)/shard_map/ppermute | solution.py:19
  979.9 124.1 %reduce-scatter.15.cloned.1.call-start = ((), (), s32[]{:S(2)}) async-start(), calls=%async_computation.17 | async-start | bytes 491520 | tf_op jit(solution)/shard_map/reduce_scatter | solution.py:327
  985.3 92.6 %collective-permute-start.7 = (bf16[1024,192]{0,1:T(8,128)(2,1)}, bf16[1024,192]{0,1:T(8,128)(2,1)}, u32[]{:S(2)}, u32[]{:S(2)}) collective-permute-start(bf16[1024,192]{0,1:T(8,128)(2,1)} %get-tuple-element.613), channel_id=1, source_target_pairs={{16,0},{17,1},{18,2},{19,3},{20,4},{21,5},{22,6},{23,7},{24,8},{25... | collective-permute-start | bytes 1179656 | tf_op jit(solution)/shard_map/ppermute | solution.py:19
  1083.4 64.6 %reduce-scatter.21.cloned.1.call-start = ((), (), s32[]{:S(2)}) async-start(), calls=%async_computation.23 | async-start | bytes 491520
  1089.4 91.4 %all-reduce.34.cloned.1.call-start = ((), (), s32[]{:S(2)}) async-start(), calls=%async_computation.18 | async-start | bytes 884736 | tf_op jit(solution)/shard_map/psum | solution.py:346
  1106.6 99.1 %reduce-scatter.13.cloned.1.call-start = ((), (), s32[]{:S(2)}) async-start(), calls=%async_computation.16 | async-start | bytes 983040 | tf_op jit(solution)/shard_map/reduce_scatter | solution.py:324
  1110.6 126.0 %reduce-scatter.23.cloned.1.call-start = ((), (), s32[]{:S(2)}) async-start(), calls=%async_computation.24 | async-start | bytes 1474560
  1122.3 144.3 %reduce-scatter.17.cloned.1.call-start = ((), (), s32[]{:S(2)}) async-start(), calls=%async_computation.19 | async-start | bytes 1474560 | tf_op jit(solution)/shard_map/reduce_scatter | solution.py:330
  1132.3 204.2 %all-reduce.36.cloned.1.call-start = ((), (), s32[]{:S(2)}) async-start(), calls=%async_computation.25 | async-start | bytes 6291456 | tf_op jit(solution)/shard_map/psum | solution.py:231
  1140.8 219.3 %reduce-scatter.19.cloned.1.call-start = ((), (), s32[]{:S(2)}) async-start(), calls=%async_computation.22 | async-start | bytes 245760
  1149.7 186.8 %copy-start.126 = (f32[1024]{0:T(1024)S(1)}, f32[1024]{0:T(1024)}, u32[]{:S(2)}) copy-start(f32[1024]{0:T(1024)} %copy-done.124) | copy-start | bytes 12292
  1238.7 100.8 %copy-start.139 = (f32[768,1]{0,1:T(1,128)S(1)}, f32[768,1]{0,1:T(1,128)}, u32[]{:S(2)}) copy-start(f32[768,1]{0,1:T(1,128)} %stack.28) | copy-start | bytes 9220
  1238.7 100.8 %copy-start.140 = (f32[768,1]{0,1:T(1,128)S(1)}, f32[768,1]{0,1:T(1,128)}, u32[]{:S(2)}) copy-start(f32[768,1]{0,1:T(1,128)} %stack.27) | copy-start | bytes 9220
  1238.7 100.9 %copy-start.141 = (f32[768,1]{0,1:T(1,128)S(1)}, f32[768,1]{0,1:T(1,128)}, u32[]{:S(2)}) copy-start(f32[768,1]{0,1:T(1,128)} %stack.31) | copy-start | bytes 9220
  1238.7 100.9 %copy-start.142 = (f32[768,1]{0,1:T(1,128)S(1)}, f32[768,1]{0,1:T(1,128)}, u32[]{:S(2)}) copy-start(f32[768,1]{0,1:T(1,128)} %stack.30) | copy-start | bytes 9220
  1238.7 100.9 %copy-start.143 = (f32[768,1]{0,1:T(1,128)S(1)}, f32[768,1]{0,1:T(1,128)}, u32[]{:S(2)}) copy-start(f32[768,1]{0,1:T(1,128)} %stack.34) | copy-start | bytes 9220
  (164 other events, 1223.0 us)
Sparse Core Ops, SparseCore 0:
  133.1 42.6 all-reduce.13
  201.5 42.0 all-reduce.15
  328.3 44.8 all-reduce.17
  384.5 42.8 all-reduce.19
  510.3 43.8 all-reduce.21
  567.4 42.8 all-reduce.23
  669.2 42.8 all-reduce.25
  776.4 42.2 all-reduce.27
  881.2 42.8 all-reduce.29
  980.1 42.2 all-reduce.31
Sparse Core Ops, SparseCore 1:
  135.1 30.0 all-gather.7
  166.6 29.4 all-gather.9
  1083.4 20.6 reduce-scatter.14
  1106.5 18.7 reduce-scatter.20
  1129.0 51.8 all-reduce.33
  1183.2 22.5 reduce-scatter.12
  1207.9 28.7 reduce-scatter.22
  1238.8 27.8 reduce-scatter.16
  1269.4 67.0 all-reduce.35
  1340.5 19.5 reduce-scatter.18
where the time goes:
time: 1380 us; the launch traced here: 1370 us
  waiting for transfers between devices  762 us (55%)
  matrix products  229 us (17%)
  other arithmetic  158 us (11%)
  local copies, waits for them, and re-layouts  88.4 us (6%)
  blocking collectives  69.3 us (5%)
  loops' own time  24.4 us (2%)
  starting transfers between devices  20.5 us (1%)
  between operations  18.2 us (1%)
    psum x3, waiting for transfers between devices, layer_backward(): lax.psum(grad_normed_part.astype(jnp.bfloat16), 'mp').astype(jnp.float32)  154 us
    ppermute x8, waiting for transfers between devices, from_behind(): lax.ppermute(value, axis, [(source, source + steps) for source in range(i...  137 us
    psum x3, waiting for transfers between devices, layer_forward(): lax.psum(attn_part.astype(jnp.bfloat16), 'mp').astype(jnp.float32)  130 us
    psum x3, waiting for transfers between devices, layer_backward(): lax.psum(times_back(grad_hidden, w_up).astype(jnp.bfloat16), 'mp')  117 us
    psum x2, waiting for transfers between devices, layer_forward(): lax.psum(mlp_part.astype(jnp.bfloat16), 'mp').astype(jnp.float32)  85.2 us
    unnamed x23, waiting for transfers between devices  41.3 us
    dot_general x15, matrix products, inner_rows(): lax.dot_general(left, right, (((0,), (0,)), ((), ())), preferred_element_...  38.4 us
    reduce_sum x6, other arithmetic, norm_back(): return (factor * inner_sum, jnp.sum(grad_rows * plain_rows, axis=0))  37.6 us
  transfers between devices with their start and end apart: 28, of which 22 were waited for; matrix products, arithmetic and copies ran while one was open for 15% of the time, Pallas kernels for 0%

commit v1 on v0

v1 whole, which is shorter than its diff:
```python
import functools
import math

import jax
import jax.numpy as jnp
from jax import lax
from jax.experimental import pallas as pl
from jax.experimental.pallas import tpu as pltpu
from jax.sharding import Mesh, PartitionSpec as P

HEAD = 64
MB_TOK = 1024
PIECE = 256
PIECES = MB_TOK // PIECE
WINDOW = 3
LANES = 128
EPSILON = 1e-05
GELU_K = math.sqrt(2.0 / math.pi)
GELU_C = 0.044715
MESH = pl.DeviceIdType.MESH
F32 = jnp.float32
LOW = jnp.bfloat16


def mm(left, right):
    return lax.dot_general(left, right, (((1,), (0,)), ((), ())), preferred_element_type=F32)


def mm_back(left, right):
    return lax.dot_general(left, right, (((1,), (1,)), ((), ())), preferred_element_type=F32)


def normalize(rows):
    centred = rows - jnp.mean(rows, axis=1, keepdims=True)
    factor = lax.rsqrt(jnp.mean(centred * centred, axis=1, keepdims=True) + EPSILON)
    return centred * factor, factor


def norm_back(grad, plain, factor, gain):
    scaled = grad * gain
    return factor * (
        scaled
        - jnp.mean(scaled, axis=1, keepdims=True)
        - plain * jnp.mean(scaled * plain, axis=1, keepdims=True)
    )


def flip(tile):
    return pltpu.roll(tile, HEAD, 1)


def layers_kernel(
    width, x_ref, start_ref, gain_ref, w_ref,
    out_ref, grad_ref, gain_grad_ref,
    wa, q_s, k_s, v_s, kt_s, vt_s, o_s, lse_s, plain1, plain2, fac1, fac2,
    a_t, m_t, g_t, h_t, e_s, gd_s, dz_s, do_s, dqkv, dk_acc, dv_acc, bias_s,
    there, there_v, here, here_v, swap_out, swap_in,
    sem_xs, sem_xr, sem_vs, sem_vr, sem_cs, sem_cr,
):
    section = lax.axis_index("section")
    core = lax.axis_index("core")
    other_layer = {"section": 1 - section}
    other_core = {"core": 1 - core}
    first = section == 0
    tiles = width // 2 // LANES

    barrier = pltpu.get_barrier_semaphore()
    pl.semaphore_signal(barrier, inc=1, device_id=other_layer, device_id_type=MESH)
    pl.semaphore_signal(barrier, inc=1, device_id=other_core, device_id_type=MESH)
    pl.semaphore_wait(barrier, 2)

    lane = lax.broadcasted_iota(jnp.int32, (1, LANES), 1)
    low_half = lane < HEAD

    def halves(tile):
        return [jnp.where(low_half, tile, jnp.zeros_like(tile)),
                jnp.where(low_half, jnp.zeros_like(tile), tile)]

    def group_tile(group, index):
        return w_ref[group, :, index * LANES:(index + 1) * LANES]

    for kind in range(4):
        for group in range(2):
            spot = (kind * tiles + group) * LANES
            wa[:, spot:spot + LANES] = group_tile(group, kind)
    for pair in range(2):
        one, two = (group_tile(group, 4 + pair).astype(F32) for group in range(2))
        spot = (2 * pair * tiles + 2) * LANES
        wa[:, spot:spot + LANES] = jnp.where(low_half, one, flip(two)).astype(LOW)
        spot = ((2 * pair + 1) * tiles + 2) * LANES
        wa[:, spot:spot + LANES] = jnp.where(low_half, flip(one), two).astype(LOW)

    gain1 = gain_ref[0:1, :]
    gain2 = gain_ref[1:2, :]
    qkv_cols = 3 * tiles * LANES
    hidden = width

    def swap(slot, value):
        swap_out[...] = value
        copy = pltpu.make_async_remote_copy(
            src_ref=swap_out, dst_ref=swap_in.at[slot],
            send_sem=sem_cs.at[slot], recv_sem=sem_cr.at[slot],
            device_id=other_core, device_id_type=MESH,
        )
        copy.start()
        copy.wait()
        return swap_out[...].astype(F32) + swap_in[slot].astype(F32)

    def hand_over(piece):
        return (
            pltpu.make_async_remote_copy(
                src_ref=there.at[piece], dst_ref=here.at[piece],
                send_sem=sem_xs.at[piece], recv_sem=sem_xr.at[piece],
                device_id=other_layer, device_id_type=MESH,
            ),
            pltpu.make_async_remote_copy(
                src_ref=there_v.at[piece], dst_ref=here_v.at[piece],
                send_sem=sem_vs.at[piece], recv_sem=sem_vr.at[piece],
                device_id=other_layer, device_id_type=MESH,
            ),
        )

    def reused(tile_index):
        if tile_index == 0:
            return None
        if tile_index == 1:
            return jnp.logical_and(jnp.logical_not(first), lane >= 0)
        return jnp.logical_and(jnp.logical_not(first), lane >= HEAD)

    def make_bias(piece, count):
        base = piece * PIECE
        query = base + lax.broadcasted_iota(jnp.int32, (1, PIECE), 1)
        begin = start_ref[piece]
        for j in range(count):
            key = base - (count - 1 - j) * PIECE + lax.broadcasted_iota(jnp.int32, (PIECE, 1), 0)
            fine = jnp.logical_and(key >= begin, key <= query)
            bias_s[j] = jnp.where(fine, 0.0, -1e30).astype(F32)

    def attend(piece, count):
        make_bias(piece, count)
        for t in range(tiles):
            parts = []
            for h, query in enumerate(halves(q_s[piece, t])):
                scores = [
                    mm_back(k_s[piece - (count - 1 - j), t], query) + bias_s[j] for j in range(count)
                ]
                top = functools.reduce(
                    jnp.maximum, [jnp.max(s, axis=0, keepdims=True) for s in scores])
                expo = [jnp.exp(s - top) for s in scores]
                total = functools.reduce(
                    jnp.add, [jnp.sum(e, axis=0, keepdims=True) for e in expo])
                mixed = functools.reduce(jnp.add, [
                    mm(vt_s[piece - (count - 1 - j), t, h * HEAD:(h + 1) * HEAD, :], e.astype(LOW))
                    for j, e in enumerate(expo)
                ])
                parts.append(mixed * (1.0 / total))
                lse_s[piece, 2 * t + h] = top + jnp.log(total)
            o_s[piece, t] = jnp.concatenate(parts, axis=0).T.astype(LOW)

    def attend_back(piece, count):
        make_bias(piece, count)
        for t in range(tiles):
            inner = (do_s[t].astype(F32) * o_s[piece, t].astype(F32)).T
            queries = halves(q_s[piece, t])
            grads = halves(do_s[t])
            dq = [0.0, 0.0]
            sums = [jnp.sum(inner[h * HEAD:(h + 1) * HEAD], axis=0, keepdims=True) for h in range(2)]
            for j in range(count):
                at = piece - (count - 1 - j)
                dk_new, dv_new = 0.0, 0.0
                for h in range(2):
                    probs = jnp.exp(
                        mm_back(k_s[at, t], queries[h]) + bias_s[j] - lse_s[piece, 2 * t + h])
                    dprobs = mm_back(v_s[at, t], grads[h])
                    dscores = (probs * (dprobs - sums[h])).astype(LOW)
                    dv_new = dv_new + mm(probs.astype(LOW), grads[h])
                    dk_new = dk_new + mm(dscores, queries[h])
                    dq[h] = dq[h] + mm(kt_s[at, t, h * HEAD:(h + 1) * HEAD, :], dscores)
                dk_acc[at, t] += dk_new
                dv_acc[at, t] += dv_new
            dq_t = jnp.concatenate(dq, axis=0) * 0.125
            dqkv[piece, :, t * LANES:(t + 1) * LANES] = dq_t.T.astype(LOW)

    def by_count(piece, run):
        for count in range(1, WINDOW + 1):
            fits = piece >= WINDOW - 1 if count == WINDOW else piece == count - 1

            @pl.when(fits)
            def _(count=count):
                run(piece, count)

    def forward(piece, carry):
        @pl.when(jnp.logical_not(first))
        def _():
            for copy in hand_over(piece):
                copy.wait_recv()

        rows = jnp.where(first, x_ref[piece], here[piece]).astype(F32)
        plain, factor = normalize(rows)
        plain1[piece] = plain
        fac1[piece] = factor
        normed = plain * gain1
        a_t[piece] = normed.T.astype(LOW)
        qkv = mm(normed.astype(LOW), wa[:, :qkv_cols])
        for t in range(tiles):
            q_s[piece, t] = (qkv[:, t * LANES:(t + 1) * LANES].astype(LOW) * 0.125).astype(LOW)
            key = qkv[:, (tiles + t) * LANES:(tiles + t + 1) * LANES].astype(LOW)
            value = qkv[:, (2 * tiles + t) * LANES:(2 * tiles + t + 1) * LANES].astype(LOW)
            mask = reused(t)
            if mask is not None:
                value = jnp.where(mask, here_v[piece, t - 1], value)
                there_v[piece, t - 1] = value
            k_s[piece, t] = key
            v_s[piece, t] = value
            kt_s[piece, t] = key.astype(F32).T.astype(LOW)
            vt_s[piece, t] = value.astype(F32).T.astype(LOW)
        by_count(piece, attend)
        mixed = jnp.concatenate([o_s[piece, t] for t in range(tiles)], axis=1)
        middle = rows + swap(0, mm_back(mixed, wa[:, qkv_cols:]).astype(LOW))
        plain, factor = normalize(middle)
        plain2[piece] = plain
        fac2[piece] = factor
        normed = plain * gain2
        m_t[piece] = normed.T.astype(LOW)
        normed = normed.astype(LOW)
        total = 0.0
        for group in range(2):
            z = mm(normed, w_ref[group, :, hidden:2 * hidden])
            square = z * z
            bent = jnp.tanh(GELU_K * z * (1.0 + GELU_C * square))
            upper = 0.5 * (1.0 + bent)
            acted = (z * upper).astype(LOW)
            slope = upper + 0.5 * z * (1.0 - bent * bent) * (GELU_K * (1.0 + 3.0 * GELU_C * square))
            gd_s[piece, group] = slope.astype(LOW)
            e_s[piece, group] = acted
            total = total + mm_back(acted, w_ref[group, :, 2 * hidden:])
        result = middle + swap(1, total.astype(LOW))
        there[piece] = result.astype(LOW)

        @pl.when(first)
        def _():
            for copy in hand_over(piece):
                copy.start()

        @pl.when(jnp.logical_not(first))
        def _():
            out_ref[piece] = there[piece]

        return carry

    lax.fori_loop(0, PIECES, forward, 0)

    @pl.when(first)
    def _():
        for piece in range(PIECES):
            for copy in hand_over(piece):
                copy.wait_send()

    gain_grad_ref[...] = jnp.zeros_like(gain_grad_ref)
    dk_acc[...] = jnp.zeros_like(dk_acc)
    dv_acc[...] = jnp.zeros_like(dv_acc)

    def backward(step, carry):
        piece = PIECES - 1 - step

        @pl.when(first)
        def _():
            for copy in hand_over(piece):
                copy.wait_recv()

        grad_low = jnp.where(first, here[piece], x_ref[piece])
        grad = grad_low.astype(F32)
        g_t[piece] = grad.T.astype(LOW)
        total = 0.0
        for group in range(2):
            dz = mm(grad_low, w_ref[group, :, 2 * hidden:]) * gd_s[piece, group].astype(F32)
            dz = dz.astype(LOW)
            dz_s[piece, group] = dz
            total = total + mm_back(dz, w_ref[group, :, hidden:2 * hidden])
        dm = swap(0, total.astype(LOW))
        plain = plain2[piece]
        gain_grad_ref[1:2, :] += jnp.sum(dm * plain, axis=0, keepdims=True)
        middle = grad + norm_back(dm, plain, fac2[piece], gain2)
        h_t[piece] = middle.T.astype(LOW)
        dmixed = mm(middle.astype(LOW), wa[:, qkv_cols:]).astype(LOW)
        for t in range(tiles):
            do_s[t] = dmixed[:, t * LANES:(t + 1) * LANES]
        by_count(piece, attend_back)
        for t in range(tiles):
            dvalue = dv_acc[piece, t]
            mask = reused(t)
            if mask is not None:
                there_v[piece, t - 1] = dvalue.astype(LOW)
                came = jnp.logical_and(first, jnp.logical_or(t == 1, lane >= HEAD))
                dvalue = jnp.where(came, dvalue + here_v[piece, t - 1].astype(F32), dvalue)
                dvalue = jnp.where(mask, 0.0, dvalue)
            spot = (tiles + t) * LANES
            dqkv[piece, :, spot:spot + LANES] = dk_acc[piece, t].astype(LOW)
            spot = (2 * tiles + t) * LANES
            dqkv[piece, :, spot:spot + LANES] = dvalue.astype(LOW)
        da = swap(1, mm_back(dqkv[piece], wa[:, :qkv_cols]).astype(LOW))
        plain = plain1[piece]
        gain_grad_ref[0:1, :] += jnp.sum(da * plain, axis=0, keepdims=True)
        grad_in = middle + norm_back(da, plain, fac1[piece], gain1)
        there[piece] = grad_in.astype(LOW)

        @pl.when(jnp.logical_not(first))
        def _():
            for copy in hand_over(piece):
                copy.start()

        @pl.when(first)
        def _():
            out_ref[piece] = there[piece]

        return carry

    lax.fori_loop(0, PIECES, backward, 0)

    block = 256

    def weight_block(index, carry):
        group, column = index // (hidden // block), index % (hidden // block)
        spot = pl.multiple_of(column * block, block)
        total = 0.0
        other = 0.0
        for piece in range(PIECES):
            total = total + mm(m_t[piece], dz_s[piece, group, :, pl.ds(spot, block)])
            other = other + mm(g_t[piece], e_s[piece, group, :, pl.ds(spot, block)])
        grad_ref[group, :, pl.ds(pl.multiple_of(hidden + spot, block), block)] = total.astype(LOW)
        grad_ref[group, :, pl.ds(pl.multiple_of(2 * hidden + spot, block), block)] = other.astype(LOW)
        return carry

    lax.fori_loop(0, 2 * (hidden // block), weight_block, 0)

    pairs = []
    for kind in range(4):
        total = 0.0
        for piece in range(PIECES):
            if kind < 3:
                width_kind = tiles * LANES
                total = total + mm(a_t[piece], dqkv[piece, :, kind * width_kind:(kind + 1) * width_kind])
            else:
                mixed = jnp.concatenate([o_s[piece, t] for t in range(tiles)], axis=1)
                total = total + mm(h_t[piece], mixed)
        for group in range(2):
            part = total[:, group * LANES:(group + 1) * LANES].astype(LOW)
            grad_ref[group, :, kind * LANES:(kind + 1) * LANES] = part
        pairs.append(total[:, 2 * LANES:])
    for pair in range(2):
        one, two = pairs[2 * pair:2 * pair + 2]
        spot = (4 + pair) * LANES
        grad_ref[0, :, spot:spot + LANES] = jnp.where(low_half, one, flip(two)).astype(LOW)
        grad_ref[1, :, spot:spot + LANES] = jnp.where(low_half, flip(one), two).astype(LOW)

    @pl.when(jnp.logical_not(first))
    def _():
        for piece in range(PIECES):
            for copy in hand_over(piece):
                copy.wait_send()


def run_layers(x_rows, starts, gains, weights):
    width = x_rows.shape[2]
    tiles = width // 2 // LANES
    vmem = pl.BlockSpec(memory_space=pltpu.VMEM)
    per_tile = (PIECES, tiles, PIECE, LANES)
    turned = (PIECES, tiles, LANES, PIECE)
    flat = (PIECES, PIECE, width)
    flat_turned = (PIECES, width, PIECE)
    wide = (PIECES, 2, PIECE, width)
    low = lambda shape: pltpu.VMEM(shape, LOW)
    full = lambda shape: pltpu.VMEM(shape, F32)
    dma = lambda count: pltpu.SemaphoreType.DMA((count,))
    return pl.pallas_call(
        functools.partial(layers_kernel, width),
        out_shape=(
            jax.ShapeDtypeStruct(flat, LOW),
            jax.ShapeDtypeStruct(weights.shape, LOW),
            jax.ShapeDtypeStruct((8, width), F32),
        ),
        in_specs=[vmem] * 4,
        out_specs=(vmem,) * 3,
        scratch_shapes=[
            low((width, 4 * tiles * LANES)),
            low(per_tile), low(per_tile), low(per_tile), low(turned), low(turned), low(per_tile),
            full((PIECES, 2 * tiles, 1, PIECE)),
            full(flat), full(flat), full((PIECES, PIECE, 1)), full((PIECES, PIECE, 1)),
            low(flat_turned), low(flat_turned), low(flat_turned), low(flat_turned),
            low(wide), low(wide), low(wide), low((tiles, PIECE, LANES)),
            low((PIECES, PIECE, 3 * tiles * LANES)), full(per_tile), full(per_tile),
            full((WINDOW, PIECE, PIECE)),
            low(flat), low((PIECES, 2, PIECE, LANES)), low(flat), low((PIECES, 2, PIECE, LANES)),
            low((PIECE, width)), low((2, PIECE, width)),
            dma(PIECES), dma(PIECES), dma(PIECES), dma(PIECES), dma(2), dma(2),
        ],
        compiler_params=pltpu.CompilerParams(
            collective_id=0, has_side_effects=True, vmem_limit_bytes=63 << 20),
        name="layers",
    )(x_rows, starts, gains, weights)


def pack(parts):
    w_qk, w_value, w_out, w_up, w_down = parts
    query, key, out_t = w_qk[:, 0], w_qk[:, 1], w_out.T
    edge = 2 * HEAD
    return jnp.concatenate(
        [query[:, :edge], key[:, :edge], w_value[:, :edge], out_t[:, :edge],
         query[:, edge:], key[:, edge:], w_value[:, edge:], out_t[:, edge:], w_up, w_down.T],
        axis=1)


def unpack(packed):
    edge = 2 * HEAD
    cut = lambda spot, size: packed[:, spot:spot + size]
    query = jnp.concatenate([cut(0, edge), cut(4 * edge, HEAD)], axis=1)
    key = jnp.concatenate([cut(edge, edge), cut(4 * edge + HEAD, HEAD)], axis=1)
    value = jnp.concatenate([cut(2 * edge, edge), cut(5 * edge, HEAD)], axis=1)
    out_t = jnp.concatenate([cut(3 * edge, edge), cut(5 * edge + HEAD, HEAD)], axis=1)
    hidden = packed.shape[1] // 3
    return (
        jnp.stack([query, key], axis=1), value, out_t.T,
        cut(hidden, hidden), cut(2 * hidden, hidden).T)


def shards(
    ends_in, seq_lengths, norm_gains, qk_weight, value_weight, out_weight, fc_weight, proj_weight
):
    section = lax.axis_index("section")
    lane_y = lax.axis_index("y")
    group = 2 * lane_y + lax.axis_index("core")
    first = section == 0
    cols = qk_weight.shape[3]
    width = ends_in.shape[2]
    fresh = (value_weight.shape[1] - width) // cols
    offset = jnp.where(first, group, width // cols + jnp.minimum(group, fresh - 1)) * cols
    w_value = lax.dynamic_slice_in_dim(value_weight, offset, cols, 1)
    packed = pack((qk_weight[0], w_value, out_weight[0], fc_weight[0], proj_weight[0]))
    weights = lax.all_gather(packed, "dp", axis=0, tiled=True)
    weights = lax.all_gather(weights, "y", axis=0)
    gains = lax.all_gather(norm_gains[0], "dp", axis=0, tiled=True).astype(F32).T
    gains = jnp.concatenate([gains, jnp.zeros((6, width), F32)], axis=0)
    x_rows = lax.dynamic_slice_in_dim(ends_in[0], lane_y * MB_TOK, MB_TOK, 0)
    x_rows = x_rows.reshape(PIECES, PIECE, width)
    ends = jnp.cumsum(lax.dynamic_index_in_dim(seq_lengths, lane_y, 0, keepdims=False))
    places = jnp.arange(MB_TOK, dtype=jnp.int32)
    starts = jnp.max(
        jnp.where(ends[None, :] <= places[:, None], ends[None, :], 0), axis=1)
    starts = starts.astype(jnp.int32).reshape(PIECES, 1, PIECE)
    out_rows, grads, gain_grads = run_layers(x_rows, starts, gains, weights)
    both = lax.all_gather(out_rows.reshape(MB_TOK, width), "y", axis=0, tiled=True)
    grads = lax.psum_scatter(grads, "y", scatter_dimension=0, tiled=False)
    grads = lax.psum_scatter(grads, "dp", scatter_dimension=0, tiled=True)
    gain_rows = lax.psum(gain_grads[:2], "y").T
    gain_rows = lax.psum_scatter(gain_rows, "dp", scatter_dimension=0, tiled=True)
    d_qk, d_value, d_out, d_up, d_down = unpack(grads.astype(F32))
    values = lax.all_gather(d_value.astype(LOW), ("section", "y", "core"), axis=0)
    kept = width // cols + fresh
    d_value = jnp.concatenate([values[index] for index in range(kept)], axis=1).astype(F32)
    return (
        both[None], gain_rows[:, 0][None], gain_rows[:, 1][None], d_qk[None], d_value,
        d_out[None], d_up[None], d_down[None])


def solution(mesh):
    sections, depth, split = (mesh.shape[name] for name in ("section", "dp", "mp"))
    grid = Mesh(mesh.devices.reshape(sections, depth, split // 2, 2), ("section", "dp", "y", "core"))
    mp = ("y", "core")
    in_specs = (
        P("section", "dp", None),
        P("dp", None),
        P("section", "dp", None),
        P("section", "dp", None, mp),
        P("dp", None),
        P("section", mp, "dp"),
        P("section", "dp", mp),
        P("section", mp, "dp"),
    )
    out_specs = (
        P("section", "dp", None),
        P("section", "dp"),
        P("section", "dp"),
        P("section", "dp", None, mp),
        P("dp", None),
        P("section", mp, "dp"),
        P("section", "dp", mp),
        P("section", mp, "dp"),
    )
    return jax.shard_map(shards, mesh=grid, in_specs=in_specs, out_specs=out_specs, check_vma=False)
```

time: 1380 us -> 572 us (0.41)
  waiting for transfers between devices: 762 us -> 356 us
  matrix products: 229 us -> 0 us
  other arithmetic: 158 us -> 2.66 us
  Pallas kernels: 0 us -> 151 us
  local copies, waits for them, and re-layouts: 88.4 us -> 17.6 us
  blocking collectives: 69.3 us -> 30.4 us
  loops' own time: 24.4 us -> 0 us
  starting transfers between devices: 20.5 us -> 0.24 us
    psum x12 -> x0, waiting for transfers between devices: 517 us -> none  [the longest x3 154 us: layer_backward(): lax.psum(grad_normed_part.astype(jnp.bfloat16), 'mp').astype(jnp.float32)]
    dot_general x87 -> x0, matrix products: 229 us -> none  [the longest x15 38.4 us: inner_rows(): lax.dot_general(left, right, (((0,), (0,)), ((), ())), preferred_element_...]
    all_gather x2 -> x3, waiting for transfers between devices: 11.8 us -> 181 us  [the longest x1 72.8 us: shards(): weights = lax.all_gather(packed, 'dp', axis=0, tiled=True)]
    pallas_call x0 -> x1, Pallas kernels: none -> 151 us  [run_layers(): pl.pallas_call(functools.partial(layers_kernel, width), out_shape=(jax.Sh...]
    ppermute x8 -> x0, waiting for transfers between devices: 137 us -> none  [from_behind(): lax.ppermute(value, axis, [(source, source + steps) for source in range(i...]
    reduce_scatter x3 -> x2, waiting for transfers between devices: 54.3 us -> 151 us  [the longest x1 82.4 us: shards(): grads = lax.psum_scatter(grads, 'y', scatter_dimension=0, tiled=False)]
    reduce_sum x26 -> x0, other arithmetic: 70.4 us -> none  [the longest x6 37.6 us: norm_back(): return (factor * inner_sum, jnp.sum(grad_rows * plain_rows, axis=0))]
    all_gather x4 -> x2, blocking collectives: 69.3 us -> 25.4 us  [the longest x1 15 us: shards(): lax.all_gather(norm_gains[0], 'dp', axis=0, tiled=True).astype(F32)]
  transfers between devices with their start and end apart: 28 -> 6, of which waited for: 22 -> 6; matrix products, arithmetic and copies ran while one was open for 15% -> 1% of each run, Pallas kernels for 0% -> 0%
where the time goes in v1:
time: 572 us
  waiting for transfers between devices  356 us (62%)
  Pallas kernels  151 us (26%)
  blocking collectives  30.4 us (5%)
  local copies, waits for them, and re-layouts  17.6 us (3%)
  between operations  14.3 us (2%)
    pallas_call x1, Pallas kernels, run_layers(): pl.pallas_call(functools.partial(layers_kernel, width), out_shape=(jax.Sh...  151 us
    reduce_scatter x1, waiting for transfers between devices, shards(): grads = lax.psum_scatter(grads, 'y', scatter_dimension=0, tiled=False)  82.4 us
    all_gather x1, waiting for transfers between devices, shards(): weights = lax.all_gather(packed, 'dp', axis=0, tiled=True)  72.8 us
    all_gather x1, waiting for transfers between devices, shards(): weights = lax.all_gather(weights, 'y', axis=0)  69.6 us
    reduce_scatter x1, waiting for transfers between devices, shards(): grads = lax.psum_scatter(grads, 'dp', scatter_dimension=0, tiled=True)  68.6 us
    all_gather x1, waiting for transfers between devices, shards(): lax.all_gather(out_rows.reshape(MB_TOK, width), 'y', axis=0, tiled=True)  38.2 us
    unnamed x7, waiting for transfers between devices  24 us
    all_gather x1, blocking collectives, shards(): lax.all_gather(norm_gains[0], 'dp', axis=0, tiled=True).astype(F32)  15 us
  transfers between devices with their start and end apart: 6, of which 6 were waited for; matrix products, arithmetic and copies ran while one was open for 1% of the time, Pallas kernels for 0%

profile of v1, /device:TPU:0, one launch (start us, length us, event | category | flops | bytes accessed | tf_op | source)
XLA Modules:
  0.0 572.0 jit_solution(10581131447634502039)
XLA Ops:
  7.2 0.0 copy-start
  7.2 0.0 all-gather.6.cloned.1.call-start
  7.2 1.0 copy.29
  8.3 1.0 copy.35
  9.4 0.1 constant_dynamic-slice_fusion
  9.5 0.1 constant_dynamic-slice_fusion.1
  9.6 2.0 concatenate.37
  11.6 0.0 all-gather.6.cloned.1.call-update
  11.6 0.0 all-gather.10.cloned.1.call-start
  11.7 72.8 %all-gather.6.cloned.1.call-done = bf16[768,2304]{1,0:T(8,128)(2,1)} async-done(((bf16[192,2304]{1,0:T(8,128)(2,1)}), bf16[768,2304]{1,0:T(8,128)(2,1)}) %all-gather.6.cloned.1.call-update) | async-done | bytes 3538960 | tf_op jit(solution)/shard_map/all_gather | solution.py:439
  84.5 0.0 all-gather.10.cloned.1.call-update
  84.5 0.0 reduce-scatter.6.cloned.1.call-start
  84.6 0.2 reduce-window.8
  84.7 0.2 copy.26
  84.9 15.0 %all-gather = bf16[1,768,2]{2,0,1:T(2,128)(2,1)S(1)} all-gather(bf16[1,192,2]{2,0,1:T(2,128)(2,1)S(1)} %copy.26), channel_id=2, replica_groups=mesh['section'=2,'dp'=4,'y'=2,'core'=2] {'dp'}, dimensions={1}, use_global_device_ids=true | all-gather | bytes 3840 | tf_op jit(solution)/shard_map/all_gather | solution.py:441
  100.0 0.3 copy.27
  100.2 0.6 pad_convert_fusion.gain_ref
  100.9 0.7 select_reduce_fusion
  101.5 2.7 constant_dynamic-slice_fusion.3
  104.2 69.6 %all-gather.10.cloned.1.call-done = bf16[1536,2304]{1,0:T(8,128)(2,1)} async-done(((bf16[768,2304]{1,0:T(8,128)(2,1)}), bf16[1536,2304]{1,0:T(8,128)(2,1)}) %all-gather.10.cloned.1.call-update) | async-done | bytes 7077904 | tf_op jit(solution)/shard_map/all_gather | solution.py:440
  173.9 151.2 %layers.1 = (bf16[4,256,768]{2,1,0:T(8,128)(2,1)}, bf16[2,768,2304]{2,1,0:T(8,128)(2,1)}, f32[8,768]{1,0:T(8,128)}) custom-call(bf16[4,256,768]{2,1,0:T(8,128)(2,1)} %bitcast.66, s32[4,1,256]{2,1,0:T(1,128)} %bitcast.75, f32[8,768]{1,0:T(8,128)} %pad_convert_fusion.gain_ref, bf16[2,768,2304]{2,1,0:T(8,128)(2,1)} %bitcast.65), custom_call_target="tpu_custom_call" | custom-call | tf_op jit(solution)/shard_map/layers/pallas_call | solution.py:375
  325.1 0.0 reduce-scatter.6.cloned.1.call-update
  325.1 0.0 reduce-scatter.10.cloned.1.call-start
  325.1 0.7 slice_bitcast_fusion.12
  325.9 0.9 copy.32
  326.8 0.0 reduce-scatter.10.cloned.1.call-update
  326.8 0.0 all-gather.8.cloned.1.call-start
  326.9 0.5 all-gather.8.cloned.1.call-update
  327.4 0.0 reduce-scatter.8.cloned.1.call-start
  327.5 82.4 %reduce-scatter.6.cloned.1.call-done = bf16[1,768,2304]{2,1,0:T(8,128)(2,1)} async-done(((bf16[2,768,2304]{2,1,0:T(8,128)(2,1)}), bf16[1,768,2304]{2,1,0:T(8,128)(2,1)}) %reduce-scatter.6.cloned.1.call-update) | async-done | bytes 3538960 | tf_op jit(solution)/shard_map/reduce_scatter | solution.py:452
  409.9 0.0 reduce-scatter.8.cloned.1.call-update
  409.9 23.4 %reduce-scatter.10.cloned.1.call-done = f32[192,2]{1,0:T(8,128)} async-done(((f32[768,2]{1,0:T(8,128)}), f32[192,2]{1,0:T(8,128)}) %reduce-scatter.10.cloned.1.call-update) | async-done | bytes 1552
  433.3 1.0 copy.33
  434.3 4.9 psum.8
  439.2 0.6 slice_bitcast_fusion.13
  439.8 38.2 %all-gather.8.cloned.1.call-done = bf16[2048,768]{1,0:T(8,128)(2,1)} async-done(((bf16[1024,768]{1,0:T(8,128)(2,1)}), bf16[2048,768]{1,0:T(8,128)(2,1)}) %all-gather.8.cloned.1.call-update) | async-done | bytes 3145744 | tf_op jit(solution)/shard_map/all_gather | solution.py:451
  478.0 68.6 %reduce-scatter.8.cloned.1.call-done = bf16[192,2304]{1,0:T(8,128)(2,1)} async-done(((bf16[768,2304]{1,0:T(8,128)(2,1)}), bf16[192,2304]{1,0:T(8,128)(2,1)}) %reduce-scatter.8.cloned.1.call-update) | async-done | bytes 884752 | tf_op jit(solution)/shard_map/reduce_scatter | solution.py:453
  546.5 1.0 fusion.2
  547.6 0.9 fusion.1
  548.5 0.8 copy.31
  549.4 1.1 copy.30
  550.4 10.4 %all_gather.24 = bf16[8,192,192]{2,1,0:T(8,128)(2,1)S(1)} all-gather(bf16[1,192,192]{2,1,0:T(8,128)(2,1)S(1)} %pad_maximum_fusion), channel_id=1, replica_groups=mesh['section'=2,'dp'=4,'y'=2,'core'=2] {'section','y','core'}, dimensions={0}, use_global_device_ids=true | all-gather | bytes 663552 | tf_op jit(solution)/shard_map/all_gather | solution.py:457
  560.9 0.2 concatenate.43
  561.1 1.0 convert_element_type.16
  562.1 0.1 convert_element_type.15
  562.2 1.1 slice_bitcast_fusion
  563.3 0.2 copy-done.1
  563.5 1.7 copy.37
  (23 shorter events, 0.2 us)
Async XLA Ops:
  7.2 2.2 copy-start
  7.2 77.3 %all-gather.6.cloned.1.call-start = ((), (), s32[]{:S(2)}) async-start(), calls=%async_computation.3 | async-start | bytes 4423680 | tf_op jit(solution)/shard_map/all_gather | solution.py:439
  9.5 75.0 %copy-start.4 = (s32[2,8]{1,0:T(2,128)S(1)}, s32[2,8]{1,0:T(2,128)}, u32[]{:S(2)}) copy-start(s32[2,8]{1,0:T(2,128)} %param.9) | copy-start | bytes 196
  9.6 75.2 %copy-start.3 = (bf16[1,192,2]{1,2,0:T(2,128)(2,1)S(1)}, bf16[1,192,2]{1,2,0:T(2,128)(2,1)}, u32[]{:S(2)}) copy-start(bf16[1,192,2]{1,2,0:T(2,128)(2,1)} %param.10) | copy-start | bytes 2308
  11.6 162.2 %all-gather.10.cloned.1.call-start = ((), (), s32[]{:S(2)}) async-start(), calls=%async_computation.7 | async-start | bytes 10616832 | tf_op jit(solution)/shard_map/all_gather | solution.py:440
  84.5 325.4 %reduce-scatter.6.cloned.1.call-start = ((), (), s32[]{:S(2)}) async-start(), calls=%async_computation.5 | async-start | bytes 10616832 | tf_op jit(solution)/shard_map/reduce_scatter | solution.py:452
  325.1 108.3 %reduce-scatter.10.cloned.1.call-start = ((), (), s32[]{:S(2)}) async-start(), calls=%async_computation.8 | async-start | bytes 491520
  326.8 151.2 %all-gather.8.cloned.1.call-start = ((), (), s32[]{:S(2)}) async-start(), calls=%async_computation.4 | async-start | bytes 4718592 | tf_op jit(solution)/shard_map/all_gather | solution.py:451
  327.4 219.1 %reduce-scatter.8.cloned.1.call-start = ((), (), s32[]{:S(2)}) async-start(), calls=%async_computation.6 | async-start | bytes 4423680 | tf_op jit(solution)/shard_map/reduce_scatter | solution.py:453
  546.5 3.9 copy-start.2
  561.1 2.4 copy-start.1
Sparse Core Ops, SparseCore 0:
  11.7 72.6 all-gather.5
  86.0 87.8 all-gather.9
  325.2 84.6 reduce-scatter.5
  412.7 20.5 reduce-scatter.9
  434.7 43.2 all-gather.7
  480.1 66.3 reduce-scatter.7

commit v2 on v1

v2 whole, which is shorter than its diff:
```python
import functools
import math

import jax
import jax.numpy as jnp
from jax import lax
from jax.experimental import pallas as pl
from jax.experimental.pallas import tpu as pltpu
from jax.sharding import Mesh, PartitionSpec as P

HEAD = 64
MB_TOK = 1024
PIECE = 256
PIECES = MB_TOK // PIECE
WINDOW = 3
LANES = 128
EPSILON = 1e-05
GELU_K = math.sqrt(2.0 / math.pi)
GELU_C = 0.044715
MESH = pl.DeviceIdType.MESH
F32 = jnp.float32
LOW = jnp.bfloat16


def mm(left, right):
    return lax.dot_general(left, right, (((1,), (0,)), ((), ())), preferred_element_type=F32)


def mm_back(left, right):
    return lax.dot_general(left, right, (((1,), (1,)), ((), ())), preferred_element_type=F32)


def normalize(rows):
    centred = rows - jnp.mean(rows, axis=1, keepdims=True)
    factor = lax.rsqrt(jnp.mean(centred * centred, axis=1, keepdims=True) + EPSILON)
    return centred * factor, factor


def norm_back(grad, plain, factor, gain):
    scaled = grad * gain
    return factor * (
        scaled
        - jnp.mean(scaled, axis=1, keepdims=True)
        - plain * jnp.mean(scaled * plain, axis=1, keepdims=True)
    )


def flip(tile):
    return pltpu.roll(tile, HEAD, 1)


def layers_kernel(width, depth, inside, *refs):
    refs = list(refs)
    take = lambda count: [refs.pop(0) for _ in range(count)]
    x_ref, start_ref, gain_ref, part_ref = take(4)
    out_ref, grad_ref, gain_grad_ref = take(3)
    if inside:
        (value_ref,) = take(1)
    (wa, q_s, k_s, v_s, kt_s, vt_s, o_s, lse_s, plain1, plain2, fac1, fac2,
     a_t, m_t, g_t, h_t, e_s, gd_s, do_s, dqkv, spare, bias_s,
     there, there_v, here, here_v, swap_out, swap_in,
     sem_x, sem_v, sem_f, sem_c, sem_o, sem_l) = take(34)
    if inside:
        (w_ref, gain_all, sums, y_in, z_in, gain_y, gain_z,
         sem_az, sem_ay, sem_gz, sem_ry, sem_rz, sem_gg, sem_va) = take(14)
    else:
        w_ref, sums = part_ref, grad_ref

    section = lax.axis_index("section")
    core = lax.axis_index("core")
    lane_y = lax.axis_index("y")
    deep = lax.axis_index("dp")
    other_layer = {"section": 1 - section}
    other_core = {"core": 1 - core}
    other_y = {"y": 1 - lane_y}
    first = section == 0
    second = jnp.logical_not(first)
    tiles = width // 2 // LANES
    hidden = width
    rows_own = width // depth
    half_cols = width // 2

    def send(src, dst, sems, index, target):
        return pltpu.make_async_remote_copy(
            src_ref=src, dst_ref=dst, send_sem=sems.at[(0,) + index], recv_sem=sems.at[(1,) + index],
            device_id=target, device_id_type=MESH)

    def peer(step):
        return {"dp": lax.rem(deep + step, depth)}

    barrier = pltpu.get_barrier_semaphore()
    friends = [other_layer, other_core, other_y]
    if inside:
        friends = friends + [peer(step) for step in range(1, depth)]
    for friend in friends:
        pl.semaphore_signal(barrier, inc=1, device_id=friend, device_id_type=MESH)
    pl.semaphore_wait(barrier, len(friends))

    lane = lax.broadcasted_iota(jnp.int32, (1, LANES), 1)
    low_half = lane < HEAD

    def rows_at(place):
        return pl.ds(pl.multiple_of(place * rows_own, rows_own), rows_own)

    def cols_at(part):
        return pl.ds(part * hidden, hidden)

    def own_copy(part):
        return pltpu.make_async_copy(
            part_ref.at[:, cols_at(part)], w_ref.at[lane_y, rows_at(deep), cols_at(part)],
            sem_l.at[part])

    def gather_z(part, step):
        return send(part_ref.at[:, cols_at(part)],
                    w_ref.at[lane_y, rows_at(deep), cols_at(part)], sem_az, (part, step), peer(step))

    def gather_y(part, step):
        if step == 0:
            return send(part_ref.at[:, cols_at(part)],
                        w_ref.at[lane_y, rows_at(deep), cols_at(part)], sem_ay, (part, 0), other_y)
        spot = w_ref.at[lane_y, rows_at(lax.rem(deep - step + depth, depth)), cols_at(part)]
        return send(spot, spot, sem_ay, (part, step), other_y)

    def gather_gain(step):
        return send(gain_ref, gain_all.at[deep], sem_gz, (step,), peer(step))

    def gather_start(part):
        own_copy(part).start()
        for step in range(1, depth):
            gather_z(part, step).start()
        gather_y(part, 0).start()

    def gather_pass(part):
        for step in range(1, depth):
            gather_z(part, step).wait_recv()
            gather_y(part, step).start()

    def gather_end(part):
        own_copy(part).wait()
        for step in range(depth):
            gather_y(part, step).wait()
        for step in range(1, depth):
            gather_z(part, step).wait_send()

    block = 2 * LANES

    def block_at(index):
        return pl.ds(index * block, block)

    def reduce_y(index):
        return send(sums.at[1 - lane_y, :, block_at(index)], y_in.at[:, block_at(index)],
                    sem_ry, (index,), other_y)

    def reduce_z(index, step):
        return send(sums.at[lane_y, rows_at(lax.rem(deep + step, depth)), block_at(index)],
                    z_in.at[step - 1, :, block_at(index)], sem_rz, (index, step), peer(step))

    def reduce_mid(index):
        reduce_y(index).wait_recv()
        at = block_at(index)
        sums[lane_y, :, at] = (
            sums[lane_y, :, at].astype(F32) + y_in[:, at].astype(F32)).astype(LOW)
        for step in range(1, depth):
            reduce_z(index, step).start()

    def reduce_end(index):
        at = block_at(index)
        total = sums[lane_y, rows_at(deep), at].astype(F32)
        for step in range(1, depth):
            reduce_z(index, step).wait_recv()
            total = total + z_in[step - 1, :, at].astype(F32)
        grad_ref[:, at] = total

    def halves(tile):
        return [jnp.where(low_half, tile, jnp.zeros_like(tile)),
                jnp.where(low_half, jnp.zeros_like(tile), tile)]

    def group_tile(group, index):
        return w_ref[group, :, index * LANES:(index + 1) * LANES]

    qkv_cols = 3 * tiles * LANES

    def arrange():
        for kind in range(4):
            for group in range(2):
                spot = (kind * tiles + group) * LANES
                wa[:, spot:spot + LANES] = group_tile(group, kind)
        for pair in range(2):
            one, two = (group_tile(group, 4 + pair).astype(F32) for group in range(2))
            spot = (2 * pair * tiles + 2) * LANES
            wa[:, spot:spot + LANES] = jnp.where(low_half, one, flip(two)).astype(LOW)
            spot = ((2 * pair + 1) * tiles + 2) * LANES
            wa[:, spot:spot + LANES] = jnp.where(low_half, flip(one), two).astype(LOW)

    if inside:
        gain_all[deep] = gain_ref[...]
        for step in range(1, depth):
            gather_gain(step).start()
        gather_start(0)
        gather_start(1)
        gather_pass(0)
        gather_start(2)
        for step in range(1, depth):
            gather_gain(step).wait()
        gather_end(0)
        gains = jnp.concatenate([gain_all[place, :, :rows_own] for place in range(depth)], axis=1)
    else:
        gains = gain_ref[...]
    arrange()
    gain1 = gains[0:1, :]
    gain2 = gains[1:2, :]

    def swap(slot, value):
        swap_out[...] = value
        copy = send(swap_out, swap_in.at[slot], sem_c, (slot,), other_core)
        copy.start()
        copy.wait()
        return swap_out[...].astype(F32) + swap_in[slot].astype(F32)

    half = pl.ds(pl.multiple_of(core * half_cols, half_cols), half_cols)

    def hand_over(piece):
        return (
            send(there.at[piece, :, half], here.at[piece, :, half], sem_x, (piece,), other_layer),
            send(there_v.at[piece], here_v.at[piece], sem_v, (piece,), other_layer),
        )

    def hand_on(piece):
        return send(here.at[piece, :, half], here.at[piece, :, half], sem_f, (piece,), other_core)

    def take_over(piece):
        copy, copy_v = hand_over(piece)
        copy.wait_recv()
        passing = hand_on(piece)
        passing.start()
        copy_v.wait_recv()
        passing.wait()

    def emit(piece):
        return (
            pltpu.make_async_copy(there.at[piece], out_ref.at[lane_y, piece], sem_l.at[3 + piece]),
            send(there.at[piece], out_ref.at[lane_y, piece], sem_o, (piece,), other_y),
        )

    def reused(tile_index):
        if tile_index == 0:
            return None
        if tile_index == 1:
            return jnp.logical_and(second, lane >= 0)
        return jnp.logical_and(second, lane >= HEAD)

    def make_bias(piece, count):
        base = piece * PIECE
        query = base + lax.broadcasted_iota(jnp.int32, (1, PIECE), 1)
        begin = start_ref[piece]
        for j in range(count):
            key = base - (count - 1 - j) * PIECE + lax.broadcasted_iota(jnp.int32, (PIECE, 1), 0)
            fine = jnp.logical_and(key >= begin, key <= query)
            bias_s[j] = jnp.where(fine, 0.0, -1e30).astype(F32)

    def attend(piece, count):
        make_bias(piece, count)
        for t in range(tiles):
            parts = []
            for h, query in enumerate(halves(q_s[piece, t])):
                scores = [
                    mm_back(k_s[piece - (count - 1 - j), t], query) + bias_s[j] for j in range(count)
                ]
                top = functools.reduce(
                    jnp.maximum, [jnp.max(s, axis=0, keepdims=True) for s in scores])
                expo = [jnp.exp(s - top) for s in scores]
                total = functools.reduce(
                    jnp.add, [jnp.sum(e, axis=0, keepdims=True) for e in expo])
                mixed = functools.reduce(jnp.add, [
                    mm(vt_s[piece - (count - 1 - j), t, h * HEAD:(h + 1) * HEAD, :], e.astype(LOW))
                    for j, e in enumerate(expo)
                ])
                parts.append(mixed * (1.0 / total))
                lse_s[piece, 2 * t + h] = top + jnp.log(total)
            o_s[piece, t] = jnp.concatenate(parts, axis=0).T.astype(LOW)

    def attend_back(piece, count):
        make_bias(piece, count)
        for t in range(tiles):
            inner = (do_s[t].astype(F32) * o_s[piece, t].astype(F32)).T
            queries = halves(q_s[piece, t])
            grads = halves(do_s[t])
            dq = [0.0, 0.0]
            inners = [jnp.sum(inner[h * HEAD:(h + 1) * HEAD], axis=0, keepdims=True) for h in range(2)]
            for j in range(count):
                at = piece - (count - 1 - j)
                dk_new, dv_new = 0.0, 0.0
                for h in range(2):
                    probs = jnp.exp(
                        mm_back(k_s[at, t], queries[h]) + bias_s[j] - lse_s[piece, 2 * t + h])
                    dprobs = mm_back(v_s[at, t], grads[h])
                    dscores = (probs * (dprobs - inners[h])).astype(LOW)
                    dv_new = dv_new + mm(probs.astype(LOW), grads[h])
                    dk_new = dk_new + mm(dscores, queries[h])
                    dq[h] = dq[h] + mm(kt_s[at, t, h * HEAD:(h + 1) * HEAD, :], dscores)
                spare[at, t] += dk_new
                spare[at, tiles + t] += dv_new
            dq_t = jnp.concatenate(dq, axis=0) * 0.125
            dqkv[piece, :, t * LANES:(t + 1) * LANES] = dq_t.T.astype(LOW)

    def by_count(piece, run):
        for count in range(1, WINDOW + 1):
            fits = piece >= WINDOW - 1 if count == WINDOW else piece == count - 1

            @pl.when(fits)
            def _(count=count):
                run(piece, count)

    def forward_attention(piece):
        @pl.when(second)
        def _():
            take_over(piece)

        rows = jnp.where(first, x_ref[piece], here[piece]).astype(F32)
        plain, factor = normalize(rows)
        plain1[piece] = plain.astype(LOW)
        fac1[piece] = factor
        normed = plain * gain1
        a_t[piece] = normed.T.astype(LOW)
        qkv = mm(normed.astype(LOW), wa[:, :qkv_cols])
        for t in range(tiles):
            q_s[piece, t] = (qkv[:, t * LANES:(t + 1) * LANES].astype(LOW) * 0.125).astype(LOW)
            key = qkv[:, (tiles + t) * LANES:(tiles + t + 1) * LANES].astype(LOW)
            value = qkv[:, (2 * tiles + t) * LANES:(2 * tiles + t + 1) * LANES].astype(LOW)
            mask = reused(t)
            if mask is not None:
                value = jnp.where(mask, here_v[piece, t - 1], value)
                there_v[piece, t - 1] = value
            k_s[piece, t] = key
            v_s[piece, t] = value
            kt_s[piece, t] = key.astype(F32).T.astype(LOW)
            vt_s[piece, t] = value.astype(F32).T.astype(LOW)
        by_count(piece, attend)
        mixed = jnp.concatenate([o_s[piece, t] for t in range(tiles)], axis=1)
        middle = rows + swap(jnp.where(first, lax.rem(piece, 2), 0), mm_back(mixed, wa[:, qkv_cols:]).astype(LOW))
        for t in range(2 * tiles):
            spare[piece, t] = middle[:, t * LANES:(t + 1) * LANES]

    def forward_hidden(piece):
        middle = jnp.concatenate([spare[piece, t] for t in range(2 * tiles)], axis=1)
        plain, factor = normalize(middle)
        plain2[piece] = plain.astype(LOW)
        fac2[piece] = factor
        normed = plain * gain2
        m_t[piece] = normed.T.astype(LOW)
        normed = normed.astype(LOW)
        total = 0.0
        for group in range(2):
            z = mm(normed, w_ref[group, :, hidden:2 * hidden])
            square = z * z
            bent = jnp.tanh(GELU_K * z * (1.0 + GELU_C * square))
            upper = 0.5 * (1.0 + bent)
            acted = (z * upper).astype(LOW)
            slope = upper + 0.5 * z * (1.0 - bent * bent) * (GELU_K * (1.0 + 3.0 * GELU_C * square))
            gd_s[piece, group] = slope.astype(LOW)
            e_s[piece, group] = acted
            total = total + mm_back(acted, w_ref[group, :, 2 * hidden:])
        result = middle + swap(jnp.where(first, lax.rem(piece, 2), 1), total.astype(LOW))
        there[piece] = result.astype(LOW)

        @pl.when(first)
        def _():
            for copy in hand_over(piece):
                copy.start()

        @pl.when(second)
        def _():
            for copy in emit(piece):
                copy.start()

    def forward(step, carry):
        early = step < PIECES

        @pl.when(jnp.logical_xor(early, second))
        def _():
            forward_attention(lax.rem(step, PIECES))

        if inside:
            @pl.when(step == 1)
            def _():
                gather_pass(1)

            @pl.when(step == PIECES - 1)
            def _():
                gather_pass(2)
                gather_end(1)
                gather_end(2)

        @pl.when(jnp.logical_not(early))
        def _():
            forward_hidden(step - PIECES)

        return carry

    lax.fori_loop(0, 2 * PIECES, forward, 0)

    @pl.when(first)
    def _():
        for piece in range(PIECES):
            for copy in hand_over(piece):
                copy.wait_send()

    @pl.when(second)
    def _():
        for piece in range(PIECES):
            for copy in emit(piece):
                copy.wait()

    gain_grad_ref[...] = jnp.zeros_like(gain_grad_ref)
    spare[...] = jnp.zeros_like(spare)

    def hidden_grads(index, carry):
        group, column = index // (hidden // block), index % (hidden // block)
        spot = pl.multiple_of(column * block, block)
        total = 0.0
        other = 0.0
        for piece in range(PIECES):
            total = total + mm(m_t[piece], gd_s[piece, group, :, pl.ds(spot, block)])
            other = other + mm(g_t[piece], e_s[piece, group, :, pl.ds(spot, block)])
        sums[group, :, pl.ds(pl.multiple_of(hidden + spot, block), block)] = total.astype(LOW)
        sums[group, :, pl.ds(pl.multiple_of(2 * hidden + spot, block), block)] = other.astype(LOW)
        return carry

    def head_grads():
        pairs = []
        for kind in range(4):
            total = 0.0
            for piece in range(PIECES):
                if kind < 3:
                    size = tiles * LANES
                    total = total + mm(a_t[piece], dqkv[piece, :, kind * size:(kind + 1) * size])
                else:
                    mixed = jnp.concatenate([o_s[piece, t] for t in range(tiles)], axis=1)
                    total = total + mm(h_t[piece], mixed)
            for group in range(2):
                part = total[:, group * LANES:(group + 1) * LANES].astype(LOW)
                sums[group, :, kind * LANES:(kind + 1) * LANES] = part
            pairs.append(total[:, 2 * LANES:])
        for pair in range(2):
            one, two = pairs[2 * pair:2 * pair + 2]
            spot = (4 + pair) * LANES
            sums[0, :, spot:spot + LANES] = jnp.where(low_half, one, flip(two)).astype(LOW)
            sums[1, :, spot:spot + LANES] = jnp.where(low_half, flip(one), two).astype(LOW)

    per_part = hidden // block
    early_blocks = [per_part + index for index in range(per_part)]
    head_blocks = [index for index in range(per_part)]
    late_blocks = [2 * per_part + index for index in range(per_part)]
    order = early_blocks + head_blocks + late_blocks

    def backward(step, carry):
        piece = PIECES - 1 - step

        @pl.when(first)
        def _():
            take_over(piece)

        grad_low = jnp.where(first, here[piece], x_ref[piece])
        grad = grad_low.astype(F32)
        g_t[piece] = grad.T.astype(LOW)
        total = 0.0
        for group in range(2):
            dz = mm(grad_low, w_ref[group, :, 2 * hidden:]) * gd_s[piece, group].astype(F32)
            dz = dz.astype(LOW)
            gd_s[piece, group] = dz
            total = total + mm_back(dz, w_ref[group, :, hidden:2 * hidden])
        dm = swap(0, total.astype(LOW))

        @pl.when(step == PIECES - 1)
        def _():
            lax.fori_loop(0, 2 * per_part, hidden_grads, 0)
            if inside:
                for index in early_blocks:
                    reduce_y(index).start()

        plain = plain2[piece].astype(F32)
        gain_grad_ref[1:2, :] += jnp.sum(dm * plain, axis=0, keepdims=True)
        middle = grad + norm_back(dm, plain, fac2[piece], gain2)
        h_t[piece] = middle.T.astype(LOW)
        dmixed = mm(middle.astype(LOW), wa[:, qkv_cols:]).astype(LOW)
        for t in range(tiles):
            do_s[t] = dmixed[:, t * LANES:(t + 1) * LANES]
        by_count(piece, attend_back)
        for t in range(tiles):
            dvalue = spare[piece, tiles + t]
            mask = reused(t)
            if mask is not None:
                there_v[piece, t - 1] = dvalue.astype(LOW)
                came = jnp.logical_and(first, jnp.logical_or(t == 1, lane >= HEAD))
                dvalue = jnp.where(came, dvalue + here_v[piece, t - 1].astype(F32), dvalue)
                dvalue = jnp.where(mask, 0.0, dvalue)
            spot = (tiles + t) * LANES
            dqkv[piece, :, spot:spot + LANES] = spare[piece, t].astype(LOW)
            spot = (2 * tiles + t) * LANES
            dqkv[piece, :, spot:spot + LANES] = dvalue.astype(LOW)
        da = swap(1, mm_back(dqkv[piece], wa[:, :qkv_cols]).astype(LOW))
        plain = plain1[piece].astype(F32)
        gain_grad_ref[0:1, :] += jnp.sum(da * plain, axis=0, keepdims=True)
        grad_in = middle + norm_back(da, plain, fac1[piece], gain1)
        there[piece] = grad_in.astype(LOW)

        @pl.when(second)
        def _():
            for copy in hand_over(piece):
                copy.start()

        @pl.when(first)
        def _():
            for copy in emit(piece):
                copy.start()

        return carry

    lax.fori_loop(0, PIECES, backward, 0)
    head_grads()

    if inside:
        gain_copy = send(gain_grad_ref, gain_y, sem_gg, (0,), other_y)
        gain_copy.start()
        reduce_mid(order[0])
        for index in head_blocks:
            reduce_y(index).start()
        gain_copy.wait()
        gain_y[...] = gain_y[...] + gain_grad_ref[...]
        gain_sends = [
            send(gain_y, gain_z.at[step - 1], sem_gg, (step,), peer(step)) for step in range(1, depth)]
        for copy in gain_sends:
            copy.start()
        for index in early_blocks[1:]:
            reduce_mid(index)
        for index in late_blocks:
            reduce_y(index).start()
        for index in head_blocks:
            reduce_mid(index)
        for index in early_blocks + head_blocks:
            reduce_end(index)
        total = gain_y[...]
        for step, copy in enumerate(gain_sends):
            copy.wait()
            total = total + gain_z[step]
        gain_grad_ref[...] = total

        def place(sec, row, unit):
            return (sec * 2 + row) * 2 + unit

        mine = place(section, lane_y, core)
        for half_tile, tile_index in enumerate((2, 5)):
            value_ref[mine, :, half_tile * LANES:(half_tile + 1) * LANES] = (
                grad_ref[:, tile_index * LANES:(tile_index + 1) * LANES].astype(LOW))
        value_x = send(value_ref.at[mine], value_ref.at[mine], sem_va, (0,), other_layer)
        value_x.start()
        reduce_mid(late_blocks[0])
        value_x.wait()
        value_y = []
        for sec in range(2):
            at = place(sec, lane_y, core)
            value_y.append(send(value_ref.at[at], value_ref.at[at], sem_va, (1 + sec,), other_y))
            value_y[-1].start()
        for index in late_blocks[1:]:
            reduce_mid(index)
        for copy in value_y:
            copy.wait()
        value_c = []
        for sec in range(2):
            for row in range(2):
                at = place(sec, row, core)
                value_c.append(
                    send(value_ref.at[at], value_ref.at[at], sem_va, (3 + 2 * sec + row,), other_core))
                value_c[-1].start()
        for index in late_blocks:
            reduce_end(index)
        for copy in value_c:
            copy.wait()
        for index in order:
            reduce_y(index).wait_send()
            for step in range(1, depth):
                reduce_z(index, step).wait_send()

    @pl.when(second)
    def _():
        for piece in range(PIECES):
            for copy in hand_over(piece):
                copy.wait_send()

    @pl.when(first)
    def _():
        for piece in range(PIECES):
            for copy in emit(piece):
                copy.wait()


def run_layers(x_rows, starts, gains, weights, depth, inside):
    width = x_rows.shape[2]
    tiles = width // 2 // LANES
    rows_own = width // depth
    columns = weights.shape[-1]
    blocks = columns // (2 * LANES)
    vmem = pl.BlockSpec(memory_space=pltpu.VMEM)
    anywhere = pl.BlockSpec(memory_space=pl.ANY)
    per_tile = (PIECES, tiles, PIECE, LANES)
    turned = (PIECES, tiles, LANES, PIECE)
    flat = (PIECES, PIECE, width)
    flat_turned = (PIECES, width, PIECE)
    wide = (PIECES, 2, PIECE, width)
    low = lambda shape: pltpu.VMEM(shape, LOW)
    full = lambda shape: pltpu.VMEM(shape, F32)
    dma = lambda *shape: pltpu.SemaphoreType.DMA(shape)
    out_shape = [
        jax.ShapeDtypeStruct((2,) + flat, LOW),
        jax.ShapeDtypeStruct((rows_own, columns), F32) if inside
        else jax.ShapeDtypeStruct(weights.shape, LOW),
        jax.ShapeDtypeStruct((8, width), F32),
    ]
    out_specs = [anywhere, vmem, vmem]
    scratch = [
        low((width, 4 * tiles * LANES)),
        low(per_tile), low(per_tile), low(per_tile), low(turned), low(turned), low(per_tile),
        full((PIECES, 2 * tiles, 1, PIECE)),
        low(flat), low(flat), full((PIECES, PIECE, 1)), full((PIECES, PIECE, 1)),
        low(flat_turned), low(flat_turned), low(flat_turned), low(flat_turned),
        low(wide), low(wide), low((tiles, PIECE, LANES)),
        low((PIECES, PIECE, 3 * tiles * LANES)), full((PIECES, 2 * tiles, PIECE, LANES)),
        full((WINDOW, PIECE, PIECE)),
        low(flat), low((PIECES, 2, PIECE, LANES)), low(flat), low((PIECES, 2, PIECE, LANES)),
        low((PIECE, width)), low((2, PIECE, width)),
        dma(2, PIECES), dma(2, PIECES), dma(2, PIECES), dma(2, 2), dma(2, PIECES), dma(3 + PIECES),
    ]
    if inside:
        out_shape.append(jax.ShapeDtypeStruct((8, rows_own, 2 * LANES), LOW))
        out_specs.append(vmem)
        scratch += [
            low((2, width, columns)), full((depth,) + gains.shape),
            low((2, width, columns)), low((width, columns)), low((depth - 1, rows_own, columns)),
            full((8, width)), full((depth - 1, 8, width)),
            dma(2, 3, depth), dma(2, 3, depth), dma(2, depth), dma(2, blocks),
            dma(2, blocks, depth), dma(2, depth), dma(2, 7),
        ]
    return pl.pallas_call(
        functools.partial(layers_kernel, width, depth, inside),
        out_shape=out_shape,
        in_specs=[vmem, vmem, vmem, anywhere if inside else vmem],
        out_specs=out_specs,
        scratch_shapes=scratch,
        compiler_params=pltpu.CompilerParams(
            collective_id=0, has_side_effects=True, vmem_limit_bytes=63 << 20),
        name="layers",
    )(x_rows, starts, gains, weights)


def pack(parts):
    w_qk, w_value, w_out, w_up, w_down = parts
    query, key, out_t = w_qk[:, 0], w_qk[:, 1], w_out.T
    edge = 2 * HEAD
    return jnp.concatenate(
        [query[:, :edge], key[:, :edge], w_value[:, :edge], out_t[:, :edge],
         query[:, edge:], key[:, edge:], w_value[:, edge:], out_t[:, edge:], w_up, w_down.T],
        axis=1)


def unpack(packed):
    edge = 2 * HEAD
    cut = lambda spot, size: packed[:, spot:spot + size]
    query = jnp.concatenate([cut(0, edge), cut(4 * edge, HEAD)], axis=1)
    key = jnp.concatenate([cut(edge, edge), cut(4 * edge + HEAD, HEAD)], axis=1)
    value = jnp.concatenate([cut(2 * edge, edge), cut(5 * edge, HEAD)], axis=1)
    out_t = jnp.concatenate([cut(3 * edge, edge), cut(5 * edge + HEAD, HEAD)], axis=1)
    hidden = packed.shape[1] // 3
    return (
        jnp.stack([query, key], axis=1), value, out_t.T,
        cut(hidden, hidden), cut(2 * hidden, hidden).T)


def shards(
    ends_in, seq_lengths, norm_gains, qk_weight, value_weight, out_weight, fc_weight, proj_weight
):
    section = lax.axis_index("section")
    lane_y = lax.axis_index("y")
    group = 2 * lane_y + lax.axis_index("core")
    first = section == 0
    cols = qk_weight.shape[3]
    width = ends_in.shape[2]
    fresh = (value_weight.shape[1] - width) // cols
    offset = jnp.where(first, group, width // cols + jnp.minimum(group, fresh - 1)) * cols
    w_value = lax.dynamic_slice_in_dim(value_weight, offset, cols, 1)
    packed = pack((qk_weight[0], w_value, out_weight[0], fc_weight[0], proj_weight[0]))
    depth = lax.axis_size("dp")
    inside = depth > 1 and depth <= 4 and width % (16 * depth) == 0
    if inside:
        weights = packed
        gains = norm_gains[0].astype(F32).T
        gains = jnp.pad(gains, ((0, 6), (0, -gains.shape[1] % LANES)))
    else:
        weights = lax.all_gather(packed, "dp", axis=0, tiled=True)
        weights = lax.all_gather(weights, "y", axis=0)
        gains = lax.all_gather(norm_gains[0], "dp", axis=0, tiled=True).astype(F32).T
        gains = jnp.pad(gains, ((0, 6), (0, 0)))
    x_rows = lax.dynamic_slice_in_dim(ends_in[0], lane_y * MB_TOK, MB_TOK, 0)
    x_rows = x_rows.reshape(PIECES, PIECE, width)
    ends = jnp.cumsum(lax.dynamic_index_in_dim(seq_lengths, lane_y, 0, keepdims=False))
    places = jnp.arange(MB_TOK, dtype=jnp.int32)
    starts = jnp.max(
        jnp.where(ends[None, :] <= places[:, None], ends[None, :], 0), axis=1)
    starts = starts.astype(jnp.int32).reshape(PIECES, 1, PIECE)
    kept = width // cols + fresh
    edge = 2 * HEAD
    results = run_layers(x_rows, starts, gains, weights, depth, inside)
    both = results[0].reshape(2 * MB_TOK, width)
    if inside:
        _, grads, gain_grads, values = results
        rows_own = width // depth
        gain_rows = lax.dynamic_slice_in_dim(
            gain_grads[:2], lax.axis_index("dp") * rows_own, rows_own, 1).T
        values = values[:, :, :cols]
    else:
        _, grads, gain_grads = results
        grads = lax.psum_scatter(grads, "y", scatter_dimension=0, tiled=False)
        grads = lax.psum_scatter(grads, "dp", scatter_dimension=0, tiled=True)
        gain_rows = lax.psum(gain_grads[:2], "y").T
        gain_rows = lax.psum_scatter(gain_rows, "dp", scatter_dimension=0, tiled=True)
        values = lax.all_gather(
            unpack(grads)[1].astype(LOW), ("section", "y", "core"), axis=0)
    d_qk, _, d_out, d_up, d_down = unpack(grads.astype(F32))
    d_value = jnp.concatenate([values[index] for index in range(kept)], axis=1).astype(F32)
    return (
        both[None], gain_rows[:, 0][None], gain_rows[:, 1][None], d_qk[None], d_value,
        d_out[None], d_up[None], d_down[None])


def solution(mesh):
    sections, depth, split = (mesh.shape[name] for name in ("section", "dp", "mp"))
    grid = Mesh(mesh.devices.reshape(sections, depth, split // 2, 2), ("section", "dp", "y", "core"))
    mp = ("y", "core")
    in_specs = (
        P("section", "dp", None),
        P("dp", None),
        P("section", "dp", None),
        P("section", "dp", None, mp),
        P("dp", None),
        P("section", mp, "dp"),
        P("section", "dp", mp),
        P("section", mp, "dp"),
    )
    out_specs = (
        P("section", "dp", None),
        P("section", "dp"),
        P("section", "dp"),
        P("section", "dp", None, mp),
        P("dp", None),
        P("section", mp, "dp"),
        P("section", "dp", mp),
        P("section", mp, "dp"),
    )
    return jax.shard_map(shards, mesh=grid, in_specs=in_specs, out_specs=out_specs, check_vma=False)
```

time: 572 us -> 375 us (0.66)
  waiting for transfers between devices: 356 us -> 0 us
  Pallas kernels: 151 us -> 352 us
  blocking collectives: 30.4 us -> 0 us
  between operations: 14.3 us -> 0.82 us
    pallas_call x1, Pallas kernels: 151 us -> 352 us  [run_layers(): pl.pallas_call(functools.partial(layers_kernel, width, depth, inside), ou...]
    all_gather x3 -> x0, waiting for transfers between devices: 181 us -> none  [the longest x1 72.8 us: shards(): weights = lax.all_gather(packed, 'dp', axis=0, tiled=True)]
    reduce_scatter x2 -> x0, waiting for transfers between devices: 151 us -> none  [the longest x1 82.4 us: shards(): grads = lax.psum_scatter(grads, 'y', scatter_dimension=0, tiled=False)]
    all_gather x2 -> x0, blocking collectives: 25.4 us -> none  [the longest x1 15 us: shards(): lax.all_gather(norm_gains[0], 'dp', axis=0, tiled=True).astype(F32)]
    unnamed x7 -> x0, waiting for transfers between devices: 24 us -> none
  transfers between devices with their start and end apart: 6 -> 0, of which waited for: 6 -> 0; matrix products, arithmetic and copies ran while one was open for 1% -> 0% of each run, Pallas kernels for 0% -> 0%
where the time goes in v2:
time: 375 us
  Pallas kernels  352 us (94%)
  local copies, waits for them, and re-layouts  18.4 us (5%)
    pallas_call x1, Pallas kernels, run_layers(): pl.pallas_call(functools.partial(layers_kernel, width, depth, inside), ou...  352 us
    unnamed x13, local copies, waits for them, and re-layouts  7.56 us

profile of v2, /device:TPU:0, one launch (start us, length us, event | category | flops | bytes accessed | tf_op | source)
XLA Modules:
  0.0 374.9 jit_solution(13081110244728408243)
XLA Ops:
  0.6 0.0 copy-start
  0.6 0.0 copy-start.3
  0.7 0.0 copy-start.2
  0.7 0.8 fusion
  1.5 0.2 reduce-window.8
  1.6 0.7 select_reduce_fusion
  2.3 1.3 pad_convert_fusion.refs_2_
  3.6 0.0 copy-done
  3.6 0.1 constant_dynamic-slice_fusion
  3.7 0.1 constant_dynamic-slice_fusion.1
  3.8 1.0 copy.21
  4.8 1.0 copy.25
  5.8 0.0 copy-done.3
  5.9 0.0 copy-done.2
  5.9 1.1 concatenate.15.refs_3_
  7.0 2.7 constant_dynamic-slice_fusion.3
  9.6 352.5 %layers.1 = (bf16[2,4,256,768]{3,2,1,0:T(8,128)(2,1)}, f32[192,2304]{1,0:T(8,128)}, f32[8,768]{1,0:T(8,128)}, bf16[8,192,256]{2,1,0:T(8,128)(2,1)}) custom-call(bf16[4,256,768]{2,1,0:T(8,128)(2,1)} %bitcast.57, s32[4,1,256]{2,1,0:T(1,128)} %bitcast.64, f32[8,256]{1,0:T(8,128)} %pad_convert_fusion.refs_2_, bf16[192,2304]{1,0:T(8,128)(2,1)} %concatenate.15.refs_3_), custom_call_target="tpu_custom_call" | custom-call | tf_op jit(solution)/shard_map/layers/pallas_call | solution.py:643
  362.1 0.7 slice.98
  362.8 0.1 dynamic-slice_bitcast_fusion
  362.9 0.6 slice_bitcast_fusion.10
  363.5 1.1 fusion.2
  364.6 1.0 fusion.1
  365.6 2.3 slice_bitcast_fusion
  367.9 0.0 copy-start.1
  367.9 0.8 copy.23
  368.8 1.1 copy.22
  369.9 0.0 copy-done.1
  369.9 0.2 concatenate.18
  370.1 1.0 convert_element_type.10
  371.1 3.8 %copy.27 = bf16[1,2048,768]{2,1,0:T(8,128)(2,1)} copy(bf16[1,2048,768]{2,1,0:T(8,128)(2,1)} %bitcast.58) | data formatting | bytes 6291456
  (11 shorter events, 0.2 us)
Async XLA Ops:
  0.6 3.0 copy-start
  0.6 5.2 %copy-start.3 = (bf16[1,768,192]{1,2,0:T(8,128)(2,1)S(1)}, bf16[1,768,192]{1,2,0:T(8,128)(2,1)}, u32[]{:S(2)}) copy-start(bf16[1,768,192]{1,2,0:T(8,128)(2,1)} %param.15) | copy-start | bytes 884740
  0.7 5.2 %copy-start.2 = (bf16[1,192,768]{2,1,0:T(8,128)(2,1)S(1)}, bf16[1,192,768]{2,1,0:T(8,128)(2,1)}, u32[]{:S(2)}) copy-start(bf16[1,192,768]{2,1,0:T(8,128)(2,1)} %param.14) | copy-start | bytes 884740
  367.9 1.9 copy-start.1

commit v3 on v2

--- a/solution.py
+++ b/solution.py
@@ -13,6 +13,7 @@
 PIECE = 256
 PIECES = MB_TOK // PIECE
 WINDOW = 3
+PARTS = 6
 LANES = 128
 EPSILON = 1e-05
 GELU_K = math.sqrt(2.0 / math.pi)
@@ -52,14 +53,14 @@
 def layers_kernel(width, depth, inside, *refs):
     refs = list(refs)
     take = lambda count: [refs.pop(0) for _ in range(count)]
-    x_ref, start_ref, gain_ref, part_ref = take(4)
+    length_ref, x_all, gain_ref, part_ref = take(4)
     out_ref, grad_ref, gain_grad_ref = take(3)
     if inside:
         (value_ref,) = take(1)
     (wa, q_s, k_s, v_s, kt_s, vt_s, o_s, lse_s, plain1, plain2, fac1, fac2,
-     a_t, m_t, g_t, h_t, e_s, gd_s, do_s, dqkv, spare, bias_s,
+     a_t, m_t, g_t, h_t, e_s, gd_s, do_s, dqkv, spare, bias_s, x_ref, start_s,
      there, there_v, here, here_v, swap_out, swap_in,
-     sem_x, sem_v, sem_f, sem_c, sem_o, sem_l) = take(34)
+     sem_x, sem_v, sem_f, sem_c, sem_o, sem_oc, sem_l) = take(37)
     if inside:
         (w_ref, gain_all, sums, y_in, z_in, gain_y, gain_z,
          sem_az, sem_ay, sem_gz, sem_ry, sem_rz, sem_gg, sem_va) = take(14)
@@ -102,50 +103,86 @@
     def rows_at(place):
         return pl.ds(pl.multiple_of(place * rows_own, rows_own), rows_own)
 
+    unit = part_ref.shape[-1] // PARTS
+    ways = (1, -1)
+    mixed_part = PARTS - 1
+
     def cols_at(part):
-        return pl.ds(part * hidden, hidden)
-
-    def own_copy(part):
-        return pltpu.make_async_copy(
-            part_ref.at[:, cols_at(part)], w_ref.at[lane_y, rows_at(deep), cols_at(part)],
-            sem_l.at[part])
-
-    def gather_z(part, step):
-        return send(part_ref.at[:, cols_at(part)],
-                    w_ref.at[lane_y, rows_at(deep), cols_at(part)], sem_az, (part, step), peer(step))
-
-    def gather_y(part, step):
-        if step == 0:
-            return send(part_ref.at[:, cols_at(part)],
-                        w_ref.at[lane_y, rows_at(deep), cols_at(part)], sem_ay, (part, 0), other_y)
-        spot = w_ref.at[lane_y, rows_at(lax.rem(deep - step + depth, depth)), cols_at(part)]
-        return send(spot, spot, sem_ay, (part, step), other_y)
+        return pl.ds(part * unit, unit)
+
+    def on_line(place):
+        return jnp.logical_and(place >= 0, place < depth)
+
+    def own_copy():
+        return pltpu.make_async_copy(part_ref, w_ref.at[lane_y, rows_at(deep)], sem_l.at[PIECES])
+
+    def gather_line(part, row, hop, way):
+        place = deep - hop * ways[way]
+        home = lane_y if row == 0 else 1 - lane_y
+        spot = w_ref.at[home, rows_at(place), cols_at(part)]
+        src = part_ref.at[:, cols_at(part)] if row == 0 and hop == 0 else spot
+        return send(src, spot, sem_az, (part + row, hop, way), {"dp": deep + ways[way]})
+
+    def line_start(part, row, hop, way):
+        @pl.when(jnp.logical_and(on_line(deep - hop * ways[way]), on_line(deep + ways[way])))
+        def _():
+            gather_line(part, row, hop, way).start()
+
+    def line_sent(part, row, hop, way):
+        @pl.when(jnp.logical_and(on_line(deep - hop * ways[way]), on_line(deep + ways[way])))
+        def _():
+            gather_line(part, row, hop, way).wait_send()
+
+    def gather_y(part, place, own):
+        spot = w_ref.at[lane_y, rows_at(place), cols_at(part)]
+        src = part_ref.at[:, cols_at(part)] if own else spot
+        return send(src, spot, sem_ay, (part, place), other_y)
 
     def gather_gain(step):
         return send(gain_ref, gain_all.at[deep], sem_gz, (step,), peer(step))
 
     def gather_start(part):
-        own_copy(part).start()
-        for step in range(1, depth):
-            gather_z(part, step).start()
-        gather_y(part, 0).start()
-
-    def gather_pass(part):
-        for step in range(1, depth):
-            gather_z(part, step).wait_recv()
-            gather_y(part, step).start()
+        for way in range(2):
+            line_start(part, 0, 0, way)
+        if part != mixed_part:
+            gather_y(part, deep, True).start()
+
+    def gather_pass(part, row=0):
+        for hop in range(depth - 1):
+            for way in range(2):
+                place = deep - (hop + 1) * ways[way]
+
+                @pl.when(on_line(place))
+                def _(hop=hop, way=way, place=place):
+                    gather_line(part, row, hop, way).wait_recv()
+                    if hop < depth - 2:
+                        line_start(part, row, hop + 1, way)
+                    if part != mixed_part:
+                        gather_y(part, place, False).start()
+
+    def gather_cross():
+        gather_y(mixed_part, deep, True).wait()
+        for way in range(2):
+            line_start(mixed_part, 1, 0, way)
 
     def gather_end(part):
-        own_copy(part).wait()
-        for step in range(depth):
-            gather_y(part, step).wait()
-        for step in range(1, depth):
-            gather_z(part, step).wait_send()
+        if part != mixed_part:
+            for place in range(depth):
+                gather_y(part, place, False).wait()
+        for row in range(2 if part == mixed_part else 1):
+            for hop in range(depth - 1):
+                for way in range(2):
+                    line_sent(part, row, hop, way)
 
     block = 2 * LANES
+    spans = [(spot, block) for spot in (
+        [hidden + index * block for index in range(hidden // block)]
+        + [index * block for index in range(hidden // block)]
+        + [2 * hidden + index * block for index in range(hidden // block - 1)])]
+    spans += [(3 * hidden - block, LANES), (3 * hidden - LANES, LANES)]
 
     def block_at(index):
-        return pl.ds(index * block, block)
+        return pl.ds(spans[index][0], spans[index][1])
 
     def reduce_y(index):
         return send(sums.at[1 - lane_y, :, block_at(index)], y_in.at[:, block_at(index)],
@@ -155,8 +192,12 @@
         return send(sums.at[lane_y, rows_at(lax.rem(deep + step, depth)), block_at(index)],
                     z_in.at[step - 1, :, block_at(index)], sem_rz, (index, step), peer(step))
 
+    ahead = 2
+
     def reduce_mid(index):
         reduce_y(index).wait_recv()
+        if index + ahead < len(spans) and index + ahead >= early_blocks:
+            reduce_y(index + ahead).start()
         at = block_at(index)
         sums[lane_y, :, at] = (
             sums[lane_y, :, at].astype(F32) + y_in[:, at].astype(F32)).astype(LOW)
@@ -192,21 +233,43 @@
             spot = ((2 * pair + 1) * tiles + 2) * LANES
             wa[:, spot:spot + LANES] = jnp.where(low_half, flip(one), two).astype(LOW)
 
+    x_copy = pltpu.make_async_copy(x_all.at[lane_y], x_ref, sem_l.at[PIECES + 1])
     if inside:
+        gather_start(0)
+        gather_start(1)
+        gather_y(mixed_part, deep, True).start()
         gain_all[deep] = gain_ref[...]
         for step in range(1, depth):
             gather_gain(step).start()
-        gather_start(0)
-        gather_start(1)
+        own_copy().start()
+    x_copy.start()
+
+    for piece in range(PIECES):
+        place = piece * PIECE + lax.broadcasted_iota(jnp.int32, (1, PIECE), 1)
+        begin = jnp.zeros((1, PIECE), jnp.int32)
+        end = 0
+        for index in range(length_ref.shape[1]):
+            end = end + length_ref[lane_y, index]
+            begin = jnp.where(place >= end, end, begin)
+        start_s[piece] = begin
+
+    if inside:
         gather_pass(0)
         gather_start(2)
+        gather_pass(1)
+        gather_start(3)
+        gather_pass(2)
+        gather_start(4)
         for step in range(1, depth):
             gather_gain(step).wait()
         gather_end(0)
+        gather_end(1)
+        own_copy().wait()
         gains = jnp.concatenate([gain_all[place, :, :rows_own] for place in range(depth)], axis=1)
     else:
         gains = gain_ref[...]
     arrange()
+    x_copy.wait()
     gain1 = gains[0:1, :]
     gain2 = gains[1:2, :]
 
@@ -219,28 +282,38 @@
 
     half = pl.ds(pl.multiple_of(core * half_cols, half_cols), half_cols)
 
+    def hand_rows(piece):
+        return send(there.at[piece, :, half], here.at[piece, :, half], sem_x, (piece,), other_layer)
+
+    def hand_values(piece):
+        return send(there_v.at[piece], here_v.at[piece], sem_v, (piece,), other_layer)
+
     def hand_over(piece):
-        return (
-            send(there.at[piece, :, half], here.at[piece, :, half], sem_x, (piece,), other_layer),
-            send(there_v.at[piece], here_v.at[piece], sem_v, (piece,), other_layer),
-        )
+        return [hand_rows(piece), hand_values(piece)]
 
     def hand_on(piece):
         return send(here.at[piece, :, half], here.at[piece, :, half], sem_f, (piece,), other_core)
 
-    def take_over(piece):
-        copy, copy_v = hand_over(piece)
-        copy.wait_recv()
-        passing = hand_on(piece)
-        passing.start()
-        copy_v.wait_recv()
-        passing.wait()
-
-    def emit(piece):
-        return (
-            pltpu.make_async_copy(there.at[piece], out_ref.at[lane_y, piece], sem_l.at[3 + piece]),
-            send(there.at[piece], out_ref.at[lane_y, piece], sem_o, (piece,), other_y),
-        )
+    def take_start(piece):
+        hand_rows(piece).wait_recv()
+        hand_on(piece).start()
+
+    def take_values(piece):
+        hand_values(piece).wait_recv()
+
+    def emit_here(piece, stage):
+        return pltpu.make_async_copy(stage.at[piece], out_ref.at[lane_y, piece], sem_l.at[piece])
+
+    def emit_there(piece, stage):
+        return send(stage.at[piece, :, half], out_ref.at[lane_y, piece, :, half],
+                    sem_o, (piece,), other_y)
+
+    def emit(piece, stage):
+        return [emit_here(piece, stage), emit_there(piece, stage)]
+
+    def emit_on(piece):
+        spot = out_ref.at[1 - lane_y, piece, :, half]
+        return send(spot, spot, sem_oc, (piece,), other_core)
 
     def reused(tile_index):
         if tile_index == 0:
@@ -252,7 +325,7 @@
     def make_bias(piece, count):
         base = piece * PIECE
         query = base + lax.broadcasted_iota(jnp.int32, (1, PIECE), 1)
-        begin = start_ref[piece]
+        begin = start_s[piece]
         for j in range(count):
             key = base - (count - 1 - j) * PIECE + lax.broadcasted_iota(jnp.int32, (PIECE, 1), 0)
             fine = jnp.logical_and(key >= begin, key <= query)
@@ -314,7 +387,11 @@
     def forward_attention(piece):
         @pl.when(second)
         def _():
-            take_over(piece)
+            @pl.when(piece == 0)
+            def _():
+                take_start(piece)
+
+            hand_on(piece).wait()
 
         rows = jnp.where(first, x_ref[piece], here[piece]).astype(F32)
         plain, factor = normalize(rows)
@@ -323,6 +400,11 @@
         normed = plain * gain1
         a_t[piece] = normed.T.astype(LOW)
         qkv = mm(normed.astype(LOW), wa[:, :qkv_cols])
+
+        @pl.when(second)
+        def _():
+            take_values(piece)
+
         for t in range(tiles):
             q_s[piece, t] = (qkv[:, t * LANES:(t + 1) * LANES].astype(LOW) * 0.125).astype(LOW)
             key = qkv[:, (tiles + t) * LANES:(tiles + t + 1) * LANES].astype(LOW)
@@ -360,17 +442,24 @@
             gd_s[piece, group] = slope.astype(LOW)
             e_s[piece, group] = acted
             total = total + mm_back(acted, w_ref[group, :, 2 * hidden:])
+
+        @pl.when(jnp.logical_and(second, piece < PIECES - 1))
+        def _():
+            take_start(piece + 1)
+
         result = middle + swap(jnp.where(first, lax.rem(piece, 2), 1), total.astype(LOW))
-        there[piece] = result.astype(LOW)
+        result = result.astype(LOW)
 
         @pl.when(first)
         def _():
+            there[piece] = result
             for copy in hand_over(piece):
                 copy.start()
 
         @pl.when(second)
         def _():
-            for copy in emit(piece):
+            here[piece] = result
+            for copy in emit(piece, here):
                 copy.start()
 
     def forward(step, carry):
@@ -381,15 +470,25 @@
             forward_attention(lax.rem(step, PIECES))
 
         if inside:
+            @pl.when(step == 0)
+            def _():
+                gather_pass(3)
+                gather_start(5)
+                gather_cross()
+
             @pl.when(step == 1)
             def _():
-                gather_pass(1)
+                gather_pass(4)
+
+            @pl.when(step == 2)
+            def _():
+                gather_pass(5)
+                gather_pass(5, 1)
 
             @pl.when(step == PIECES - 1)
             def _():
-                gather_pass(2)
-                gather_end(1)
-                gather_end(2)
+                for part in range(2, PARTS):
+                    gather_end(part)
 
         @pl.when(jnp.logical_not(early))
         def _():
@@ -404,12 +503,6 @@
         for piece in range(PIECES):
             for copy in hand_over(piece):
                 copy.wait_send()
-
-    @pl.when(second)
-    def _():
-        for piece in range(PIECES):
-            for copy in emit(piece):
-                copy.wait()
 
     gain_grad_ref[...] = jnp.zeros_like(gain_grad_ref)
     spare[...] = jnp.zeros_like(spare)
@@ -448,17 +541,15 @@
             sums[1, :, spot:spot + LANES] = jnp.where(low_half, flip(one), two).astype(LOW)
 
     per_part = hidden // block
-    early_blocks = [per_part + index for index in range(per_part)]
-    head_blocks = [index for index in range(per_part)]
-    late_blocks = [2 * per_part + index for index in range(per_part)]
-    order = early_blocks + head_blocks + late_blocks
+    early_blocks = per_part
 
     def backward(step, carry):
         piece = PIECES - 1 - step
 
         @pl.when(first)
         def _():
-            take_over(piece)
+            take_start(piece)
+            hand_on(piece).wait()
 
         grad_low = jnp.where(first, here[piece], x_ref[piece])
         grad = grad_low.astype(F32)
@@ -475,7 +566,7 @@
         def _():
             lax.fori_loop(0, 2 * per_part, hidden_grads, 0)
             if inside:
-                for index in early_blocks:
+                for index in range(early_blocks):
                     reduce_y(index).start()
 
         plain = plain2[piece].astype(F32)
@@ -486,6 +577,11 @@
         for t in range(tiles):
             do_s[t] = dmixed[:, t * LANES:(t + 1) * LANES]
         by_count(piece, attend_back)
+
+        @pl.when(first)
+        def _():
+            take_values(piece)
+
         for t in range(tiles):
             dvalue = spare[piece, tiles + t]
             mask = reused(t)
@@ -511,39 +607,59 @@
 
         @pl.when(first)
         def _():
-            for copy in emit(piece):
+            for copy in emit(piece, there):
                 copy.start()
 
         return carry
 
     lax.fori_loop(0, PIECES, backward, 0)
     head_grads()
+
+    def emit_stage(run):
+        @pl.when(first)
+        def _():
+            run(there)
+
+        @pl.when(second)
+        def _():
+            run(here)
+
+    def pass_outputs(stage):
+        for piece in range(PIECES):
+            emit_there(piece, stage).wait_recv()
+            emit_on(piece).start()
+
+    def finish_outputs(stage):
+        for piece in range(PIECES):
+            emit_here(piece, stage).wait()
+            emit_there(piece, stage).wait_send()
+            emit_on(piece).wait()
 
     if inside:
         gain_copy = send(gain_grad_ref, gain_y, sem_gg, (0,), other_y)
         gain_copy.start()
-        reduce_mid(order[0])
-        for index in head_blocks:
-            reduce_y(index).start()
+        reduce_mid(0)
         gain_copy.wait()
         gain_y[...] = gain_y[...] + gain_grad_ref[...]
         gain_sends = [
             send(gain_y, gain_z.at[step - 1], sem_gg, (step,), peer(step)) for step in range(1, depth)]
         for copy in gain_sends:
             copy.start()
-        for index in early_blocks[1:]:
+        reduce_mid(1)
+        reduce_mid(2)
+        reduce_end(0)
+        emit_stage(pass_outputs)
+        for index in range(3, 6):
             reduce_mid(index)
-        for index in late_blocks:
-            reduce_y(index).start()
-        for index in head_blocks:
-            reduce_mid(index)
-        for index in early_blocks + head_blocks:
-            reduce_end(index)
+            reduce_end(index - 2)
         total = gain_y[...]
         for step, copy in enumerate(gain_sends):
             copy.wait()
             total = total + gain_z[step]
         gain_grad_ref[...] = total
+        reduce_end(4)
+        reduce_mid(6)
+        reduce_end(5)
 
         def place(sec, row, unit):
             return (sec * 2 + row) * 2 + unit
@@ -554,15 +670,15 @@
                 grad_ref[:, tile_index * LANES:(tile_index + 1) * LANES].astype(LOW))
         value_x = send(value_ref.at[mine], value_ref.at[mine], sem_va, (0,), other_layer)
         value_x.start()
-        reduce_mid(late_blocks[0])
+        reduce_mid(7)
         value_x.wait()
         value_y = []
         for sec in range(2):
             at = place(sec, lane_y, core)
             value_y.append(send(value_ref.at[at], value_ref.at[at], sem_va, (1 + sec,), other_y))
             value_y[-1].start()
-        for index in late_blocks[1:]:
-            reduce_mid(index)
+        reduce_end(6)
+        reduce_mid(8)
         for copy in value_y:
             copy.wait()
         value_c = []
@@ -572,14 +688,20 @@
                 value_c.append(
                     send(value_ref.at[at], value_ref.at[at], sem_va, (3 + 2 * sec + row,), other_core))
                 value_c[-1].start()
-        for index in late_blocks:
-            reduce_end(index)
+        reduce_end(7)
+        reduce_mid(9)
+        reduce_end(8)
+        reduce_end(9)
         for copy in value_c:
             copy.wait()
-        for index in order:
+        for index in range(len(spans)):
             reduce_y(index).wait_send()
             for step in range(1, depth):
                 reduce_z(index, step).wait_send()
+    else:
+        emit_stage(pass_outputs)
+
+    emit_stage(finish_outputs)
 
     @pl.when(second)
     def _():
@@ -587,21 +709,16 @@
             for copy in hand_over(piece):
                 copy.wait_send()
 
-    @pl.when(first)
-    def _():
-        for piece in range(PIECES):
-            for copy in emit(piece):
-                copy.wait()
-
-
-def run_layers(x_rows, starts, gains, weights, depth, inside):
-    width = x_rows.shape[2]
+
+def run_layers(lengths, x_rows, gains, weights, depth, inside):
+    width = x_rows.shape[3]
     tiles = width // 2 // LANES
     rows_own = width // depth
     columns = weights.shape[-1]
-    blocks = columns // (2 * LANES)
+    blocks = columns // (2 * LANES) + 1
     vmem = pl.BlockSpec(memory_space=pltpu.VMEM)
     anywhere = pl.BlockSpec(memory_space=pl.ANY)
+    smem = pl.BlockSpec(memory_space=pltpu.SMEM)
     per_tile = (PIECES, tiles, PIECE, LANES)
     turned = (PIECES, tiles, LANES, PIECE)
     flat = (PIECES, PIECE, width)
@@ -625,10 +742,11 @@
         low(flat_turned), low(flat_turned), low(flat_turned), low(flat_turned),
         low(wide), low(wide), low((tiles, PIECE, LANES)),
         low((PIECES, PIECE, 3 * tiles * LANES)), full((PIECES, 2 * tiles, PIECE, LANES)),
-        full((WINDOW, PIECE, PIECE)),
+        full((WINDOW, PIECE, PIECE)), low(flat), pltpu.VMEM((PIECES, 1, PIECE), jnp.int32),
         low(flat), low((PIECES, 2, PIECE, LANES)), low(flat), low((PIECES, 2, PIECE, LANES)),
         low((PIECE, width)), low((2, PIECE, width)),
-        dma(2, PIECES), dma(2, PIECES), dma(2, PIECES), dma(2, 2), dma(2, PIECES), dma(3 + PIECES),
+        dma(2, PIECES), dma(2, PIECES), dma(2, PIECES), dma(2, 2), dma(2, PIECES), dma(2, PIECES),
+        dma(2 + PIECES),
     ]
     if inside:
         out_shape.append(jax.ShapeDtypeStruct((8, rows_own, 2 * LANES), LOW))
@@ -637,19 +755,19 @@
             low((2, width, columns)), full((depth,) + gains.shape),
             low((2, width, columns)), low((width, columns)), low((depth - 1, rows_own, columns)),
             full((8, width)), full((depth - 1, 8, width)),
-            dma(2, 3, depth), dma(2, 3, depth), dma(2, depth), dma(2, blocks),
+            dma(2, PARTS + 1, depth - 1, 2), dma(2, PARTS, depth), dma(2, depth), dma(2, blocks),
             dma(2, blocks, depth), dma(2, depth), dma(2, 7),
         ]
     return pl.pallas_call(
         functools.partial(layers_kernel, width, depth, inside),
         out_shape=out_shape,
-        in_specs=[vmem, vmem, vmem, anywhere if inside else vmem],
+        in_specs=[smem, anywhere, vmem, anywhere if inside else vmem],
         out_specs=out_specs,
         scratch_shapes=scratch,
         compiler_params=pltpu.CompilerParams(
             collective_id=0, has_side_effects=True, vmem_limit_bytes=63 << 20),
         name="layers",
-    )(x_rows, starts, gains, weights)
+    )(lengths, x_rows, gains, weights)
 
 
 def pack(parts):
@@ -699,16 +817,10 @@
         weights = lax.all_gather(weights, "y", axis=0)
         gains = lax.all_gather(norm_gains[0], "dp", axis=0, tiled=True).astype(F32).T
         gains = jnp.pad(gains, ((0, 6), (0, 0)))
-    x_rows = lax.dynamic_slice_in_dim(ends_in[0], lane_y * MB_TOK, MB_TOK, 0)
-    x_rows = x_rows.reshape(PIECES, PIECE, width)
-    ends = jnp.cumsum(lax.dynamic_index_in_dim(seq_lengths, lane_y, 0, keepdims=False))
-    places = jnp.arange(MB_TOK, dtype=jnp.int32)
-    starts = jnp.max(
-        jnp.where(ends[None, :] <= places[:, None], ends[None, :], 0), axis=1)
-    starts = starts.astype(jnp.int32).reshape(PIECES, 1, PIECE)
+    x_rows = ends_in[0].reshape(2, PIECES, PIECE, width)
     kept = width // cols + fresh
     edge = 2 * HEAD
-    results = run_layers(x_rows, starts, gains, weights, depth, inside)
+    results = run_layers(seq_lengths, x_rows, gains, weights, depth, inside)
     both = results[0].reshape(2 * MB_TOK, width)
     if inside:
         _, grads, gain_grads, values = results

time: 375 us -> 328 us (0.87)
  Pallas kernels: 352 us -> 309 us
    pallas_call x1, Pallas kernels: 352 us -> 309 us  [run_layers(): pl.pallas_call(functools.partial(layers_kernel, width, depth, inside), ou...]
where the time goes in v3:
time: 328 us
  Pallas kernels  309 us (94%)
  local copies, waits for them, and re-layouts  15 us (5%)
    pallas_call x1, Pallas kernels, run_layers(): pl.pallas_call(functools.partial(layers_kernel, width, depth, inside), ou...  309 us
    unnamed x13, local copies, waits for them, and re-layouts  7.56 us

profile of v3, /device:TPU:0, one launch (start us, length us, event | category | flops | bytes accessed | tf_op | source)
XLA Modules:
  0.0 327.6 jit_solution(9264751693793768910)
XLA Ops:
  0.6 0.0 copy-start
  0.6 0.0 copy-start.3
  0.7 0.0 copy-start.2
  0.7 1.4 pad_convert_fusion.refs_2_
  2.0 0.0 copy-done
  2.1 0.1 constant_dynamic-slice_fusion
  2.1 0.1 constant_dynamic-slice_fusion.1
  2.2 1.0 copy.17
  3.3 1.0 copy.21
  4.3 0.0 copy-done.3
  4.3 0.0 copy-done.2
  4.3 1.1 concatenate.15.refs_3_
  5.4 309.4 %layers.1 = (bf16[2,4,256,768]{3,2,1,0:T(8,128)(2,1)}, f32[192,2304]{1,0:T(8,128)}, f32[8,768]{1,0:T(8,128)}, bf16[8,192,256]{2,1,0:T(8,128)(2,1)}) custom-call(s32[2,8]{1,0:T(2,128)} %refs_0_.1, bf16[2,4,256,768]{3,2,1,0:T(8,128)(2,1)} %bitcast.53, f32[8,256]{1,0:T(8,128)} %pad_convert_fusion.refs_2_, bf16[192,2304]{1,0:T(8,128)(2,1)} %concatenate.15.refs_3_), custom_call_target="tpu_custom_call" | custom-call | tf_op jit(solution)/shard_map/layers/pallas_call | solution.py:761
  314.8 0.7 slice.98
  315.6 0.1 dynamic-slice_bitcast_fusion
  315.7 0.6 slice_bitcast_fusion.10
  316.2 1.1 fusion.1
  317.3 1.0 fusion
  318.3 2.3 slice_bitcast_fusion
  320.7 0.0 copy-start.1
  320.7 0.8 copy.19
  321.6 1.1 copy.18
  322.6 0.0 copy-done.1
  322.7 0.2 concatenate.18
  322.9 1.0 convert_element_type.10
  323.9 3.8 %copy.23 = bf16[1,2048,768]{2,1,0:T(8,128)(2,1)} copy(bf16[1,2048,768]{2,1,0:T(8,128)(2,1)} %bitcast.54) | data formatting | bytes 6291456
  (11 shorter events, 0.2 us)
Async XLA Ops:
  0.6 1.4 copy-start
  0.6 3.6 %copy-start.3 = (bf16[1,768,192]{1,2,0:T(8,128)(2,1)S(1)}, bf16[1,768,192]{1,2,0:T(8,128)(2,1)}, u32[]{:S(2)}) copy-start(bf16[1,768,192]{1,2,0:T(8,128)(2,1)} %param.15) | copy-start | bytes 884740
  0.7 3.6 %copy-start.2 = (bf16[1,192,768]{2,1,0:T(8,128)(2,1)S(1)}, bf16[1,192,768]{2,1,0:T(8,128)(2,1)}, u32[]{:S(2)}) copy-start(bf16[1,192,768]{2,1,0:T(8,128)(2,1)} %param.14) | copy-start | bytes 884740
  320.7 1.9 copy-start.1

commit v4 on v3

--- a/solution.py
+++ b/solution.py
@@ -53,19 +53,20 @@
 def layers_kernel(width, depth, inside, *refs):
     refs = list(refs)
     take = lambda count: [refs.pop(0) for _ in range(count)]
-    length_ref, x_all, gain_ref, part_ref = take(4)
+    length_ref, x_all, gain_ref = take(3)
+    part_refs = take(3 if inside else 1)
     out_ref, grad_ref, gain_grad_ref = take(3)
     if inside:
         (value_ref,) = take(1)
-    (wa, q_s, k_s, v_s, kt_s, vt_s, o_s, lse_s, plain1, plain2, fac1, fac2,
-     a_t, m_t, g_t, h_t, e_s, gd_s, do_s, dqkv, spare, bias_s, x_ref, start_s,
+    (wa, q_s, k_s, v_s, turn_s, o_s, lse_s, plain1, plain2, fac1, fac2,
+     a_t, m_t, g_t, h_t, e_s, gd_s, do_s, spare, bias_s, x_ref, start_s,
      there, there_v, here, here_v, swap_out, swap_in,
-     sem_x, sem_v, sem_f, sem_c, sem_o, sem_oc, sem_l) = take(37)
+     sem_x, sem_v, sem_f, sem_c, sem_o, sem_oc, sem_l) = take(35)
     if inside:
         (w_ref, gain_all, sums, y_in, z_in, gain_y, gain_z,
-         sem_az, sem_ay, sem_gz, sem_ry, sem_rz, sem_gg, sem_va) = take(14)
+         sem_az, sem_ay, sem_gz, sem_ry, sem_rz, sem_rm, sem_gg, sem_va) = take(15)
     else:
-        w_ref, sums = part_ref, grad_ref
+        w_ref, sums = part_refs[0], grad_ref
 
     section = lax.axis_index("section")
     core = lax.axis_index("core")
@@ -93,6 +94,7 @@
     friends = [other_layer, other_core, other_y]
     if inside:
         friends = friends + [peer(step) for step in range(1, depth)]
+        twin = {"dp": deep + 1 - 2 * lax.rem(deep, 2)}
     for friend in friends:
         pl.semaphore_signal(barrier, inc=1, device_id=friend, device_id_type=MESH)
     pl.semaphore_wait(barrier, len(friends))
@@ -103,7 +105,8 @@
     def rows_at(place):
         return pl.ds(pl.multiple_of(place * rows_own, rows_own), rows_own)
 
-    unit = part_ref.shape[-1] // PARTS
+    unit = 3 * hidden // PARTS
+    per_ref = PARTS // 3
     ways = (1, -1)
     mixed_part = PARTS - 1
 
@@ -113,14 +116,19 @@
     def on_line(place):
         return jnp.logical_and(place >= 0, place < depth)
 
-    def own_copy():
-        return pltpu.make_async_copy(part_ref, w_ref.at[lane_y, rows_at(deep)], sem_l.at[PIECES])
+    def own_part(part):
+        return part_refs[part // per_ref].at[:, pl.ds(part % per_ref * unit, unit)]
+
+    def own_copy(index):
+        return pltpu.make_async_copy(
+            part_refs[index], w_ref.at[lane_y, rows_at(deep), pl.ds(index * hidden, hidden)],
+            sem_l.at[PIECES + index])
 
     def gather_line(part, row, hop, way):
         place = deep - hop * ways[way]
         home = lane_y if row == 0 else 1 - lane_y
         spot = w_ref.at[home, rows_at(place), cols_at(part)]
-        src = part_ref.at[:, cols_at(part)] if row == 0 and hop == 0 else spot
+        src = own_part(part) if row == 0 and hop == 0 else spot
         return send(src, spot, sem_az, (part + row, hop, way), {"dp": deep + ways[way]})
 
     def line_start(part, row, hop, way):
@@ -135,11 +143,11 @@
 
     def gather_y(part, place, own):
         spot = w_ref.at[lane_y, rows_at(place), cols_at(part)]
-        src = part_ref.at[:, cols_at(part)] if own else spot
+        src = own_part(part) if own else spot
         return send(src, spot, sem_ay, (part, place), other_y)
 
     def gather_gain(step):
-        return send(gain_ref, gain_all.at[deep], sem_gz, (step,), peer(step))
+        return send(gain_all.at[deep], gain_all.at[deep], sem_gz, (step,), peer(step))
 
     def gather_start(part):
         for way in range(2):
@@ -175,11 +183,12 @@
                     line_sent(part, row, hop, way)
 
     block = 2 * LANES
-    spans = [(spot, block) for spot in (
-        [hidden + index * block for index in range(hidden // block)]
-        + [index * block for index in range(hidden // block)]
-        + [2 * hidden + index * block for index in range(hidden // block - 1)])]
-    spans += [(3 * hidden - block, LANES), (3 * hidden - LANES, LANES)]
+    last = block // 2
+    spans = [
+        (2 * hidden, block), (2 * hidden + block, last), (hidden, block), (hidden + block, block),
+        (block, block), (2 * block, block), (0, block),
+        (hidden + 2 * block, last), (hidden + 2 * block + last, last)]
+    mixed_at = pl.ds(2 * hidden + block + last, block + last)
 
     def block_at(index):
         return pl.ds(spans[index][0], spans[index][1])
@@ -188,29 +197,107 @@
         return send(sums.at[1 - lane_y, :, block_at(index)], y_in.at[:, block_at(index)],
                     sem_ry, (index,), other_y)
 
-    def reduce_z(index, step):
-        return send(sums.at[lane_y, rows_at(lax.rem(deep + step, depth)), block_at(index)],
-                    z_in.at[step - 1, :, block_at(index)], sem_rz, (index, step), peer(step))
-
-    ahead = 2
-
-    def reduce_mid(index):
+    def share_of(near, index):
+        own = lax.rem(deep, 2)
+        return rows_at((own if near else 1 - own) + 2 * index)
+
+    def reduce_near(index, share):
+        at = block_at(index)
+        return send(sums.at[lane_y, share_of(False, share), at], z_in.at[share, :, at],
+                    sem_rz, (index, share), twin)
+
+    def reduce_far(index):
+        at = block_at(index)
+        return send(sums.at[lane_y, rows_at(lax.rem(deep + 2, depth)), at], z_in.at[2, :, at],
+                    sem_rz, (index, 2), peer(2))
+
+    def reduce_mid(index, following=None):
         reduce_y(index).wait_recv()
-        if index + ahead < len(spans) and index + ahead >= early_blocks:
-            reduce_y(index + ahead).start()
+        if following is not None:
+            reduce_y(following).start()
         at = block_at(index)
         sums[lane_y, :, at] = (
             sums[lane_y, :, at].astype(F32) + y_in[:, at].astype(F32)).astype(LOW)
-        for step in range(1, depth):
-            reduce_z(index, step).start()
+        for share in range(2):
+            reduce_near(index, share).start()
+
+    def reduce_late(index):
+        at = block_at(index)
+        for share in range(2):
+            reduce_near(index, share).wait_recv()
+            rows = share_of(True, share)
+            sums[lane_y, rows, at] = (
+                sums[lane_y, rows, at].astype(F32) + z_in[share, :, at].astype(F32)).astype(LOW)
+        reduce_far(index).start()
 
     def reduce_end(index):
         at = block_at(index)
-        total = sums[lane_y, rows_at(deep), at].astype(F32)
-        for step in range(1, depth):
-            reduce_z(index, step).wait_recv()
-            total = total + z_in[step - 1, :, at].astype(F32)
-        grad_ref[:, at] = total
+        reduce_far(index).wait_recv()
+        grad_ref[:, at] = (
+            sums[lane_y, rows_at(deep), at].astype(F32) + z_in[2, :, at].astype(F32))
+
+    def mixed_home(row, share):
+        if row == 0:
+            return z_in.at[share, :, mixed_at]
+        return y_in.at[rows_at(share), mixed_at]
+
+    def mixed_group(row):
+        return lane_y if row == 0 else 1 - lane_y
+
+    def mixed_near(row, share):
+        return send(sums.at[mixed_group(row), share_of(False, share), mixed_at],
+                    mixed_home(row, share), sem_rm, (row, share), twin)
+
+    def mixed_far(row):
+        return send(sums.at[mixed_group(row), rows_at(lax.rem(deep + 2, depth)), mixed_at],
+                    mixed_home(row, 2), sem_rm, (row, 2), peer(2))
+
+    def mixed_cross():
+        return send(sums.at[1 - lane_y, rows_at(deep), mixed_at], mixed_home(1, 3),
+                    sem_rm, (1, 3), other_y)
+
+    def mixed_start():
+        for row in range(2):
+            for share in range(2):
+                mixed_near(row, share).start()
+
+    def mixed_mid():
+        for row in range(2):
+            for share in range(2):
+                mixed_near(row, share).wait_recv()
+                rows = share_of(True, share)
+                group = mixed_group(row)
+                sums[group, rows, mixed_at] = (
+                    sums[group, rows, mixed_at].astype(F32)
+                    + mixed_home(row, share)[...].astype(F32)).astype(LOW)
+            mixed_far(row).start()
+
+    def mixed_late():
+        for row in range(2):
+            mixed_far(row).wait_recv()
+            total = (sums[mixed_group(row), rows_at(deep), mixed_at].astype(F32)
+                     + mixed_home(row, 2)[...].astype(F32))
+            if row == 0:
+                grad_ref[:, mixed_at] = total
+            else:
+                sums[mixed_group(row), rows_at(deep), mixed_at] = total.astype(LOW)
+        mixed_cross().start()
+
+    def mixed_end():
+        mixed_cross().wait_recv()
+        grad_ref[:, mixed_at] += mixed_home(1, 3)[...].astype(F32)
+
+    def reduce_sent():
+        for index in range(len(spans)):
+            reduce_y(index).wait_send()
+            for share in range(2):
+                reduce_near(index, share).wait_send()
+            reduce_far(index).wait_send()
+        for row in range(2):
+            for share in range(2):
+                mixed_near(row, share).wait_send()
+            mixed_far(row).wait_send()
+        mixed_cross().wait_send()
 
     def halves(tile):
         return [jnp.where(low_half, tile, jnp.zeros_like(tile)),
@@ -233,15 +320,16 @@
             spot = ((2 * pair + 1) * tiles + 2) * LANES
             wa[:, spot:spot + LANES] = jnp.where(low_half, flip(one), two).astype(LOW)
 
-    x_copy = pltpu.make_async_copy(x_all.at[lane_y], x_ref, sem_l.at[PIECES + 1])
+    x_copy = pltpu.make_async_copy(x_all.at[lane_y], x_ref, sem_l.at[PIECES + 3])
     if inside:
         gather_start(0)
         gather_start(1)
         gather_y(mixed_part, deep, True).start()
-        gain_all[deep] = gain_ref[...]
+        gain_all[deep, 0:2, 0:rows_own] = gain_ref[...].astype(F32)
         for step in range(1, depth):
             gather_gain(step).start()
-        own_copy().start()
+        for index in range(3):
+            own_copy(index).start()
     x_copy.start()
 
     for piece in range(PIECES):
@@ -264,7 +352,8 @@
             gather_gain(step).wait()
         gather_end(0)
         gather_end(1)
-        own_copy().wait()
+        for index in range(3):
+            own_copy(index).wait()
         gains = jnp.concatenate([gain_all[place, :, :rows_own] for place in range(depth)], axis=1)
     else:
         gains = gain_ref[...]
@@ -273,12 +362,38 @@
     gain1 = gains[0:1, :]
     gain2 = gains[1:2, :]
 
-    def swap(slot, value):
-        swap_out[...] = value
-        copy = send(swap_out, swap_in.at[slot], sem_c, (slot,), other_core)
-        copy.start()
-        copy.wait()
-        return swap_out[...].astype(F32) + swap_in[slot].astype(F32)
+    def swap_copy(leave, enter):
+        return send(swap_out.at[leave], swap_in.at[enter], sem_c, (enter,), other_core)
+
+    def swap_start(slots, value):
+        swap_out[slots[0]] = value
+        swap_copy(*slots).start()
+
+    def swap_end(slots):
+        swap_copy(*slots).wait()
+        return swap_out[slots[0]].astype(F32) + swap_in[slots[1]].astype(F32)
+
+    def first_slots(piece):
+        return lax.rem(piece, 2), piece
+
+    def turned_slots(piece):
+        return lax.rem(piece, 2), lax.rem(piece + 2, PIECES)
+
+    def second_slots(piece):
+        return 2, PIECES + lax.rem(piece, 2)
+
+    def last_slots(piece):
+        return 2, PIECES + lax.rem(piece + 1, 2)
+
+    def put_rows(piece, rows):
+        for t in range(2 * tiles):
+            spare[piece, t] = rows[:, t * LANES:(t + 1) * LANES]
+
+    def get_rows(piece):
+        return jnp.concatenate([spare[piece, t] for t in range(2 * tiles)], axis=1)
+
+    def joined(*stores):
+        return jnp.concatenate([store[t] for store in stores for t in range(tiles)], axis=1)
 
     half = pl.ds(pl.multiple_of(core * half_cols, half_cols), half_cols)
 
@@ -287,9 +402,6 @@
 
     def hand_values(piece):
         return send(there_v.at[piece], here_v.at[piece], sem_v, (piece,), other_layer)
-
-    def hand_over(piece):
-        return [hand_rows(piece), hand_values(piece)]
 
     def hand_on(piece):
         return send(here.at[piece, :, half], here.at[piece, :, half], sem_f, (piece,), other_core)
@@ -345,7 +457,7 @@
                 total = functools.reduce(
                     jnp.add, [jnp.sum(e, axis=0, keepdims=True) for e in expo])
                 mixed = functools.reduce(jnp.add, [
-                    mm(vt_s[piece - (count - 1 - j), t, h * HEAD:(h + 1) * HEAD, :], e.astype(LOW))
+                    mm(turn_s[piece - (count - 1 - j), t, h * HEAD:(h + 1) * HEAD, :], e.astype(LOW))
                     for j, e in enumerate(expo)
                 ])
                 parts.append(mixed * (1.0 / total))
@@ -370,11 +482,11 @@
                     dscores = (probs * (dprobs - inners[h])).astype(LOW)
                     dv_new = dv_new + mm(probs.astype(LOW), grads[h])
                     dk_new = dk_new + mm(dscores, queries[h])
-                    dq[h] = dq[h] + mm(kt_s[at, t, h * HEAD:(h + 1) * HEAD, :], dscores)
+                    dq[h] = dq[h] + mm(turn_s[at, t, h * HEAD:(h + 1) * HEAD, :], dscores)
                 spare[at, t] += dk_new
                 spare[at, tiles + t] += dv_new
             dq_t = jnp.concatenate(dq, axis=0) * 0.125
-            dqkv[piece, :, t * LANES:(t + 1) * LANES] = dq_t.T.astype(LOW)
+            q_s[piece, t] = dq_t.T.astype(LOW)
 
     def by_count(piece, run):
         for count in range(1, WINDOW + 1):
@@ -387,7 +499,7 @@
     def forward_attention(piece):
         @pl.when(second)
         def _():
-            @pl.when(piece == 0)
+            @pl.when(piece < 2)
             def _():
                 take_start(piece)
 
@@ -415,17 +527,21 @@
                 there_v[piece, t - 1] = value
             k_s[piece, t] = key
             v_s[piece, t] = value
-            kt_s[piece, t] = key.astype(F32).T.astype(LOW)
-            vt_s[piece, t] = value.astype(F32).T.astype(LOW)
+            turn_s[piece, t] = value.astype(F32).T.astype(LOW)
+
+        @pl.when(first)
+        def _():
+            hand_values(piece).start()
+
         by_count(piece, attend)
-        mixed = jnp.concatenate([o_s[piece, t] for t in range(tiles)], axis=1)
-        middle = rows + swap(jnp.where(first, lax.rem(piece, 2), 0), mm_back(mixed, wa[:, qkv_cols:]).astype(LOW))
-        for t in range(2 * tiles):
-            spare[piece, t] = middle[:, t * LANES:(t + 1) * LANES]
+        put_rows(piece, rows)
+        swap_start(first_slots(piece), mm_back(joined(o_s.at[piece]), wa[:, qkv_cols:]).astype(LOW))
+
+    def forward_middle(piece):
+        put_rows(piece, get_rows(piece) + swap_end(first_slots(piece)))
 
     def forward_hidden(piece):
-        middle = jnp.concatenate([spare[piece, t] for t in range(2 * tiles)], axis=1)
-        plain, factor = normalize(middle)
+        plain, factor = normalize(get_rows(piece))
         plain2[piece] = plain.astype(LOW)
         fac2[piece] = factor
         normed = plain * gain2
@@ -442,19 +558,15 @@
             gd_s[piece, group] = slope.astype(LOW)
             e_s[piece, group] = acted
             total = total + mm_back(acted, w_ref[group, :, 2 * hidden:])
-
-        @pl.when(jnp.logical_and(second, piece < PIECES - 1))
-        def _():
-            take_start(piece + 1)
-
-        result = middle + swap(jnp.where(first, lax.rem(piece, 2), 1), total.astype(LOW))
-        result = result.astype(LOW)
+        swap_start(second_slots(piece), total.astype(LOW))
+
+    def forward_result(piece):
+        result = (get_rows(piece) + swap_end(second_slots(piece))).astype(LOW)
 
         @pl.when(first)
         def _():
             there[piece] = result
-            for copy in hand_over(piece):
-                copy.start()
+            hand_rows(piece).start()
 
         @pl.when(second)
         def _():
@@ -462,12 +574,16 @@
             for copy in emit(piece, here):
                 copy.start()
 
+    def within(step, low_end, high_end):
+        return jnp.logical_and(step >= low_end, step < high_end)
+
     def forward(step, carry):
-        early = step < PIECES
-
-        @pl.when(jnp.logical_xor(early, second))
-        def _():
-            forward_attention(lax.rem(step, PIECES))
+        lag = jnp.where(first, 0, PIECES)
+        place = step - lag
+
+        @pl.when(within(place, 0, PIECES))
+        def _():
+            forward_attention(place)
 
         if inside:
             @pl.when(step == 0)
@@ -490,34 +606,51 @@
                 for part in range(2, PARTS):
                     gather_end(part)
 
-        @pl.when(jnp.logical_not(early))
-        def _():
-            forward_hidden(step - PIECES)
+        @pl.when(jnp.logical_and(second, within(place, 2, PIECES + 1)))
+        def _():
+            forward_result(place - 2)
+
+        @pl.when(within(place, 1, PIECES + 1))
+        def _():
+            forward_middle(place - 1)
+
+        hidden_place = jnp.where(first, place - PIECES, place - 1)
+
+        @pl.when(within(hidden_place, 0, PIECES))
+        def _():
+            @pl.when(jnp.logical_and(second, hidden_place < PIECES - 2))
+            def _():
+                take_start(hidden_place + 2)
+
+            forward_hidden(hidden_place)
+
+            @pl.when(first)
+            def _():
+                forward_result(hidden_place)
 
         return carry
 
-    lax.fori_loop(0, 2 * PIECES, forward, 0)
+    lax.fori_loop(0, 2 * PIECES + 1, forward, 0)
 
     @pl.when(first)
     def _():
         for piece in range(PIECES):
-            for copy in hand_over(piece):
-                copy.wait_send()
+            hand_rows(piece).wait_send()
+            hand_values(piece).wait_send()
 
     gain_grad_ref[...] = jnp.zeros_like(gain_grad_ref)
-    spare[...] = jnp.zeros_like(spare)
-
-    def hidden_grads(index, carry):
-        group, column = index // (hidden // block), index % (hidden // block)
-        spot = pl.multiple_of(column * block, block)
-        total = 0.0
-        other = 0.0
-        for piece in range(PIECES):
-            total = total + mm(m_t[piece], gd_s[piece, group, :, pl.ds(spot, block)])
-            other = other + mm(g_t[piece], e_s[piece, group, :, pl.ds(spot, block)])
-        sums[group, :, pl.ds(pl.multiple_of(hidden + spot, block), block)] = total.astype(LOW)
-        sums[group, :, pl.ds(pl.multiple_of(2 * hidden + spot, block), block)] = other.astype(LOW)
-        return carry
+
+    def hidden_grads(left, right, base):
+        def one(index, carry):
+            group, column = index // (hidden // block), index % (hidden // block)
+            spot = pl.multiple_of(column * block, block)
+            total = 0.0
+            for piece in range(PIECES):
+                total = total + mm(left[piece], right[piece, group, :, pl.ds(spot, block)])
+            sums[group, :, pl.ds(pl.multiple_of(base + spot, block), block)] = total.astype(LOW)
+            return carry
+
+        lax.fori_loop(0, 2 * (hidden // block), one, 0)
 
     def head_grads():
         pairs = []
@@ -525,11 +658,9 @@
             total = 0.0
             for piece in range(PIECES):
                 if kind < 3:
-                    size = tiles * LANES
-                    total = total + mm(a_t[piece], dqkv[piece, :, kind * size:(kind + 1) * size])
+                    total = total + mm(a_t[piece], joined((q_s, k_s, v_s)[kind].at[piece]))
                 else:
-                    mixed = jnp.concatenate([o_s[piece, t] for t in range(tiles)], axis=1)
-                    total = total + mm(h_t[piece], mixed)
+                    total = total + mm(h_t[piece], joined(o_s.at[piece]))
             for group in range(2):
                 part = total[:, group * LANES:(group + 1) * LANES].astype(LOW)
                 sums[group, :, kind * LANES:(kind + 1) * LANES] = part
@@ -540,80 +671,127 @@
             sums[0, :, spot:spot + LANES] = jnp.where(low_half, one, flip(two)).astype(LOW)
             sums[1, :, spot:spot + LANES] = jnp.where(low_half, flip(one), two).astype(LOW)
 
-    per_part = hidden // block
-    early_blocks = per_part
-
-    def backward(step, carry):
-        piece = PIECES - 1 - step
-
+    def grad_rows(piece):
+        return jnp.where(first, here[piece], x_ref[piece])
+
+    def backward_hidden(piece):
         @pl.when(first)
         def _():
             take_start(piece)
             hand_on(piece).wait()
 
-        grad_low = jnp.where(first, here[piece], x_ref[piece])
-        grad = grad_low.astype(F32)
-        g_t[piece] = grad.T.astype(LOW)
+        grad_low = grad_rows(piece)
+        g_t[piece] = grad_low.astype(F32).T.astype(LOW)
+
+        @pl.when(piece == 0)
+        def _():
+            hidden_grads(g_t, e_s, 2 * hidden)
+            if inside:
+                reduce_y(0).start()
+                reduce_y(1).start()
+                mixed_start()
+
         total = 0.0
         for group in range(2):
             dz = mm(grad_low, w_ref[group, :, 2 * hidden:]) * gd_s[piece, group].astype(F32)
             dz = dz.astype(LOW)
             gd_s[piece, group] = dz
             total = total + mm_back(dz, w_ref[group, :, hidden:2 * hidden])
-        dm = swap(0, total.astype(LOW))
-
-        @pl.when(step == PIECES - 1)
-        def _():
-            lax.fori_loop(0, 2 * per_part, hidden_grads, 0)
+        swap_start(turned_slots(piece), total.astype(LOW))
+
+        @pl.when(piece == 0)
+        def _():
+            hidden_grads(m_t, gd_s, hidden)
             if inside:
-                for index in range(early_blocks):
-                    reduce_y(index).start()
-
+                reduce_y(2).start()
+
+    def backward_attention(piece):
+        dm = swap_end(turned_slots(piece))
         plain = plain2[piece].astype(F32)
         gain_grad_ref[1:2, :] += jnp.sum(dm * plain, axis=0, keepdims=True)
-        middle = grad + norm_back(dm, plain, fac2[piece], gain2)
+        middle = grad_rows(piece).astype(F32) + norm_back(dm, plain, fac2[piece], gain2)
         h_t[piece] = middle.T.astype(LOW)
         dmixed = mm(middle.astype(LOW), wa[:, qkv_cols:]).astype(LOW)
         for t in range(tiles):
             do_s[t] = dmixed[:, t * LANES:(t + 1) * LANES]
         by_count(piece, attend_back)
+        for t in range(1, tiles):
+            there_v[piece, t - 1] = spare[piece, tiles + t].astype(LOW)
 
         @pl.when(first)
         def _():
-            take_values(piece)
+            hand_values(piece).wait_recv()
+
+        @pl.when(second)
+        def _():
+            hand_values(piece).start()
 
         for t in range(tiles):
             dvalue = spare[piece, tiles + t]
             mask = reused(t)
             if mask is not None:
-                there_v[piece, t - 1] = dvalue.astype(LOW)
                 came = jnp.logical_and(first, jnp.logical_or(t == 1, lane >= HEAD))
                 dvalue = jnp.where(came, dvalue + here_v[piece, t - 1].astype(F32), dvalue)
                 dvalue = jnp.where(mask, 0.0, dvalue)
-            spot = (tiles + t) * LANES
-            dqkv[piece, :, spot:spot + LANES] = spare[piece, t].astype(LOW)
-            spot = (2 * tiles + t) * LANES
-            dqkv[piece, :, spot:spot + LANES] = dvalue.astype(LOW)
-        da = swap(1, mm_back(dqkv[piece], wa[:, :qkv_cols]).astype(LOW))
+            k_s[piece, t] = spare[piece, t].astype(LOW)
+            v_s[piece, t] = dvalue.astype(LOW)
+        put_rows(piece, middle)
+        terms = joined(q_s.at[piece], k_s.at[piece], v_s.at[piece])
+        swap_start(last_slots(piece), mm_back(terms, wa[:, :qkv_cols]).astype(LOW))
+
+    def backward_result(piece):
+        da = swap_end(last_slots(piece))
         plain = plain1[piece].astype(F32)
         gain_grad_ref[0:1, :] += jnp.sum(da * plain, axis=0, keepdims=True)
-        grad_in = middle + norm_back(da, plain, fac1[piece], gain1)
-        there[piece] = grad_in.astype(LOW)
+        there[piece] = (get_rows(piece) + norm_back(da, plain, fac1[piece], gain1)).astype(LOW)
 
         @pl.when(second)
         def _():
-            for copy in hand_over(piece):
-                copy.start()
+            hand_rows(piece).start()
 
         @pl.when(first)
         def _():
             for copy in emit(piece, there):
                 copy.start()
 
+    def backward(step, carry):
+        @pl.when(step < PIECES)
+        def _():
+            backward_hidden(PIECES - 1 - step)
+
+        @pl.when(step == 0)
+        def _():
+            @pl.when(second)
+            def _():
+                forward_result(PIECES - 1)
+
+            spare[...] = jnp.zeros_like(spare)
+            for piece in range(PIECES):
+                for t in range(tiles):
+                    turn_s[piece, t] = k_s[piece, t].astype(F32).T.astype(LOW)
+
+        if inside:
+            @pl.when(step == PIECES)
+            def _():
+                mixed_mid()
+                reduce_mid(0, 3)
+                reduce_mid(1)
+
+        @pl.when(step >= 2)
+        def _():
+            backward_result(PIECES + 1 - step)
+
+        @pl.when(step >= 1)
+        def _():
+            backward_attention(PIECES - step)
+
         return carry
 
-    lax.fori_loop(0, PIECES, backward, 0)
+    lax.fori_loop(0, PIECES + 1, backward, 0)
     head_grads()
+    if inside:
+        reduce_y(4).start()
+    backward_result(0)
 
     def emit_stage(run):
         @pl.when(first)
@@ -638,27 +816,37 @@
     if inside:
         gain_copy = send(gain_grad_ref, gain_y, sem_gg, (0,), other_y)
         gain_copy.start()
-        reduce_mid(0)
+        reduce_late(0)
+        mixed_late()
+        reduce_mid(2, 5)
+        reduce_late(1)
         gain_copy.wait()
         gain_y[...] = gain_y[...] + gain_grad_ref[...]
         gain_sends = [
             send(gain_y, gain_z.at[step - 1], sem_gg, (step,), peer(step)) for step in range(1, depth)]
         for copy in gain_sends:
             copy.start()
-        reduce_mid(1)
-        reduce_mid(2)
+        reduce_mid(3, 6)
+        reduce_late(2)
         reduce_end(0)
-        emit_stage(pass_outputs)
-        for index in range(3, 6):
-            reduce_mid(index)
-            reduce_end(index - 2)
+        reduce_mid(4, 7)
+        reduce_late(3)
+        reduce_end(1)
+        reduce_end(2)
         total = gain_y[...]
         for step, copy in enumerate(gain_sends):
             copy.wait()
             total = total + gain_z[step]
         gain_grad_ref[...] = total
+        reduce_mid(5, 8)
+        reduce_late(4)
+        reduce_end(3)
+        emit_stage(pass_outputs)
+        reduce_mid(6)
+        reduce_late(5)
         reduce_end(4)
-        reduce_mid(6)
+        reduce_mid(7)
+        reduce_late(6)
         reduce_end(5)
 
         def place(sec, row, unit):
@@ -670,15 +858,18 @@
                 grad_ref[:, tile_index * LANES:(tile_index + 1) * LANES].astype(LOW))
         value_x = send(value_ref.at[mine], value_ref.at[mine], sem_va, (0,), other_layer)
         value_x.start()
-        reduce_mid(7)
+        mixed_end()
+        reduce_mid(8)
+        reduce_late(7)
+        reduce_end(6)
         value_x.wait()
         value_y = []
         for sec in range(2):
             at = place(sec, lane_y, core)
             value_y.append(send(value_ref.at[at], value_ref.at[at], sem_va, (1 + sec,), other_y))
             value_y[-1].start()
-        reduce_end(6)
-        reduce_mid(8)
+        reduce_late(8)
+        reduce_end(7)
         for copy in value_y:
             copy.wait()
         value_c = []
@@ -688,16 +879,10 @@
                 value_c.append(
                     send(value_ref.at[at], value_ref.at[at], sem_va, (3 + 2 * sec + row,), other_core))
                 value_c[-1].start()
-        reduce_end(7)
-        reduce_mid(9)
         reduce_end(8)
-        reduce_end(9)
         for copy in value_c:
             copy.wait()
-        for index in range(len(spans)):
-            reduce_y(index).wait_send()
-            for step in range(1, depth):
-                reduce_z(index, step).wait_send()
+        reduce_sent()
     else:
         emit_stage(pass_outputs)
 
@@ -706,16 +891,15 @@
     @pl.when(second)
     def _():
         for piece in range(PIECES):
-            for copy in hand_over(piece):
-                copy.wait_send()
+            hand_rows(piece).wait_send()
+            hand_values(piece).wait_send()
 
 
 def run_layers(lengths, x_rows, gains, weights, depth, inside):
     width = x_rows.shape[3]
     tiles = width // 2 // LANES
     rows_own = width // depth
-    columns = weights.shape[-1]
-    blocks = columns // (2 * LANES) + 1
+    columns = 3 * width
     vmem = pl.BlockSpec(memory_space=pltpu.VMEM)
     anywhere = pl.BlockSpec(memory_space=pl.ANY)
     smem = pl.BlockSpec(memory_space=pltpu.SMEM)
@@ -730,53 +914,52 @@
     out_shape = [
         jax.ShapeDtypeStruct((2,) + flat, LOW),
         jax.ShapeDtypeStruct((rows_own, columns), F32) if inside
-        else jax.ShapeDtypeStruct(weights.shape, LOW),
+        else jax.ShapeDtypeStruct(weights[0].shape, LOW),
         jax.ShapeDtypeStruct((8, width), F32),
     ]
     out_specs = [anywhere, vmem, vmem]
     scratch = [
         low((width, 4 * tiles * LANES)),
-        low(per_tile), low(per_tile), low(per_tile), low(turned), low(turned), low(per_tile),
+        low(per_tile), low(per_tile), low(per_tile), low(turned), low(per_tile),
         full((PIECES, 2 * tiles, 1, PIECE)),
         low(flat), low(flat), full((PIECES, PIECE, 1)), full((PIECES, PIECE, 1)),
         low(flat_turned), low(flat_turned), low(flat_turned), low(flat_turned),
         low(wide), low(wide), low((tiles, PIECE, LANES)),
-        low((PIECES, PIECE, 3 * tiles * LANES)), full((PIECES, 2 * tiles, PIECE, LANES)),
+        full((PIECES, 2 * tiles, PIECE, LANES)),
         full((WINDOW, PIECE, PIECE)), low(flat), pltpu.VMEM((PIECES, 1, PIECE), jnp.int32),
         low(flat), low((PIECES, 2, PIECE, LANES)), low(flat), low((PIECES, 2, PIECE, LANES)),
-        low((PIECE, width)), low((2, PIECE, width)),
-        dma(2, PIECES), dma(2, PIECES), dma(2, PIECES), dma(2, 2), dma(2, PIECES), dma(2, PIECES),
-        dma(2 + PIECES),
+        low((3, PIECE, width)), low((PIECES + 2, PIECE, width)),
+        dma(2, PIECES), dma(2, PIECES), dma(2, PIECES), dma(2, PIECES + 2), dma(2, PIECES),
+        dma(2, PIECES), dma(4 + PIECES),
     ]
     if inside:
         out_shape.append(jax.ShapeDtypeStruct((8, rows_own, 2 * LANES), LOW))
         out_specs.append(vmem)
         scratch += [
-            low((2, width, columns)), full((depth,) + gains.shape),
+            low((2, width, columns)), full((depth, 8, -(-rows_own // LANES) * LANES)),
             low((2, width, columns)), low((width, columns)), low((depth - 1, rows_own, columns)),
             full((8, width)), full((depth - 1, 8, width)),
-            dma(2, PARTS + 1, depth - 1, 2), dma(2, PARTS, depth), dma(2, depth), dma(2, blocks),
-            dma(2, blocks, depth), dma(2, depth), dma(2, 7),
+            dma(2, PARTS + 1, depth - 1, 2), dma(2, PARTS, depth), dma(2, depth), dma(2, 9),
+            dma(2, 9, 3), dma(2, 2, 4), dma(2, depth), dma(2, 7),
         ]
     return pl.pallas_call(
         functools.partial(layers_kernel, width, depth, inside),
         out_shape=out_shape,
-        in_specs=[smem, anywhere, vmem, anywhere if inside else vmem],
+        in_specs=[smem, anywhere, vmem] + [anywhere if inside else vmem] * len(weights),
         out_specs=out_specs,
         scratch_shapes=scratch,
         compiler_params=pltpu.CompilerParams(
             collective_id=0, has_side_effects=True, vmem_limit_bytes=63 << 20),
         name="layers",
-    )(lengths, x_rows, gains, weights)
-
-
-def pack(parts):
-    w_qk, w_value, w_out, w_up, w_down = parts
+    )(lengths, x_rows, gains, *weights)
+
+
+def pack(w_qk, w_value, w_out):
     query, key, out_t = w_qk[:, 0], w_qk[:, 1], w_out.T
     edge = 2 * HEAD
     return jnp.concatenate(
         [query[:, :edge], key[:, :edge], w_value[:, :edge], out_t[:, :edge],
-         query[:, edge:], key[:, edge:], w_value[:, edge:], out_t[:, edge:], w_up, w_down.T],
+         query[:, edge:], key[:, edge:], w_value[:, edge:], out_t[:, edge:]],
         axis=1)
 
 
@@ -805,18 +988,16 @@
     fresh = (value_weight.shape[1] - width) // cols
     offset = jnp.where(first, group, width // cols + jnp.minimum(group, fresh - 1)) * cols
     w_value = lax.dynamic_slice_in_dim(value_weight, offset, cols, 1)
-    packed = pack((qk_weight[0], w_value, out_weight[0], fc_weight[0], proj_weight[0]))
+    parts = [pack(qk_weight[0], w_value, out_weight[0]), fc_weight[0], proj_weight[0].T]
     depth = lax.axis_size("dp")
-    inside = depth > 1 and depth <= 4 and width % (16 * depth) == 0
+    inside = depth == 4 and width % (16 * depth) == 0
     if inside:
-        weights = packed
-        gains = norm_gains[0].astype(F32).T
-        gains = jnp.pad(gains, ((0, 6), (0, -gains.shape[1] % LANES)))
+        weights = parts
+        gains = norm_gains[0].T
     else:
-        weights = lax.all_gather(packed, "dp", axis=0, tiled=True)
-        weights = lax.all_gather(weights, "y", axis=0)
+        weights = lax.all_gather(jnp.concatenate(parts, axis=1), "dp", axis=0, tiled=True)
+        weights = [lax.all_gather(weights, "y", axis=0)]
         gains = lax.all_gather(norm_gains[0], "dp", axis=0, tiled=True).astype(F32).T
-        gains = jnp.pad(gains, ((0, 6), (0, 0)))
     x_rows = ends_in[0].reshape(2, PIECES, PIECE, width)
     kept = width // cols + fresh
     edge = 2 * HEAD

time: 328 us -> 301 us (0.918)
  Pallas kernels: 309 us -> 284 us
    pallas_call x1, Pallas kernels: 309 us -> 284 us  [run_layers(): pl.pallas_call(functools.partial(layers_kernel, width, depth, inside), ou...]
    unnamed x13 -> x9, local copies, waits for them, and re-layouts: 7.56 us -> 8.54 us
where the time goes in v4:
time: 301 us
  Pallas kernels  284 us (94%)
  local copies, waits for them, and re-layouts  15.7 us (5%)
    pallas_call x1, Pallas kernels, run_layers(): pl.pallas_call(functools.partial(layers_kernel, width, depth, inside), ou...  284 us
    unnamed x9, local copies, waits for them, and re-layouts  8.54 us

profile of v4, /device:TPU:0, one launch (start us, length us, event | category | flops | bytes accessed | tf_op | source)
XLA Modules:
  0.0 301.1 jit_solution(7774044769542693560)
XLA Ops:
  0.6 0.0 copy-start
  0.7 1.0 copy-done
  1.7 0.1 constant_dynamic-slice_fusion
  1.7 0.1 constant_dynamic-slice_fusion.1
  1.8 1.0 copy.17
  2.9 1.0 copy.21
  3.9 0.8 concatenate.15.refs_3_
  4.7 283.5 %layers.1 = (bf16[2,4,256,768]{3,2,1,0:T(8,128)(2,1)}, f32[192,2304]{1,0:T(8,128)}, f32[8,768]{1,0:T(8,128)}, bf16[8,192,256]{2,1,0:T(8,128)(2,1)}) custom-call(s32[2,8]{1,0:T(2,128)} %refs_0_.1, bf16[2,4,256,768]{3,2,1,0:T(8,128)(2,1)} %bitcast.53, bf16[2,192]{1,0:T(2,128)(2,1)} %bitcast.60, bf16[192,768]{1,0:T(8,128)(2,1)} %concatenate.15.refs_3_, ...), custom_call_target="tpu_custom_call" | custom-call | tf_op jit(solution)/shard_map/layers/pallas_call | solution.py:945
  288.3 0.7 slice.98
  289.0 0.1 dynamic-slice_bitcast_fusion
  289.1 0.6 slice_bitcast_fusion.10
  289.7 1.1 fusion.1
  290.8 1.0 fusion
  291.8 2.3 slice_bitcast_fusion
  294.1 0.0 copy-start.1
  294.1 0.8 copy.19
  295.0 1.1 copy.18
  296.1 0.0 copy-done.1
  296.1 0.2 concatenate.18
  296.3 1.0 convert_element_type.3
  297.3 3.8 %copy.23 = bf16[1,2048,768]{2,1,0:T(8,128)(2,1)} copy(bf16[1,2048,768]{2,1,0:T(8,128)(2,1)} %bitcast.54) | data formatting | bytes 6291456
  (11 shorter events, 0.2 us)
Async XLA Ops:
  0.6 1.0 copy-start
  294.1 1.9 copy-start.1

commit v5 on v4

--- a/solution.py
+++ b/solution.py
@@ -155,8 +155,8 @@
         if part != mixed_part:
             gather_y(part, deep, True).start()
 
-    def gather_pass(part, row=0):
-        for hop in range(depth - 1):
+    def gather_pass(part, row=0, hops=None):
+        for hop in range(depth - 1) if hops is None else hops:
             for way in range(2):
                 place = deep - (hop + 1) * ways[way]
 
@@ -540,24 +540,26 @@
     def forward_middle(piece):
         put_rows(piece, get_rows(piece) + swap_end(first_slots(piece)))
 
-    def forward_hidden(piece):
+    def forward_spread(piece):
         plain, factor = normalize(get_rows(piece))
         plain2[piece] = plain.astype(LOW)
         fac2[piece] = factor
         normed = plain * gain2
         m_t[piece] = normed.T.astype(LOW)
         normed = normed.astype(LOW)
-        total = 0.0
         for group in range(2):
             z = mm(normed, w_ref[group, :, hidden:2 * hidden])
             square = z * z
             bent = jnp.tanh(GELU_K * z * (1.0 + GELU_C * square))
             upper = 0.5 * (1.0 + bent)
-            acted = (z * upper).astype(LOW)
             slope = upper + 0.5 * z * (1.0 - bent * bent) * (GELU_K * (1.0 + 3.0 * GELU_C * square))
             gd_s[piece, group] = slope.astype(LOW)
-            e_s[piece, group] = acted
-            total = total + mm_back(acted, w_ref[group, :, 2 * hidden:])
+            e_s[piece, group] = (z * upper).astype(LOW)
+
+    def forward_fold(piece):
+        total = 0.0
+        for group in range(2):
+            total = total + mm_back(e_s[piece, group], w_ref[group, :, 2 * hidden:])
         swap_start(second_slots(piece), total.astype(LOW))
 
     def forward_result(piece):
@@ -577,8 +579,9 @@
     def within(step, low_end, high_end):
         return jnp.logical_and(step >= low_end, step < high_end)
 
+    lag = jnp.where(first, 0, 2 * PIECES)
+
     def forward(step, carry):
-        lag = jnp.where(first, 0, PIECES)
         place = step - lag
 
         @pl.when(within(place, 0, PIECES))
@@ -586,51 +589,60 @@
             forward_attention(place)
 
         if inside:
-            @pl.when(step == 0)
+            @pl.when(step == 1)
             def _():
                 gather_pass(3)
                 gather_start(5)
                 gather_cross()
 
-            @pl.when(step == 1)
+            @pl.when(step == PIECES - 1)
             def _():
                 gather_pass(4)
-
-            @pl.when(step == 2)
+                gather_end(2)
+                gather_end(3)
+
+            for hop in range(depth - 1):
+                @pl.when(step == PIECES + hop)
+                def _(hop=hop):
+                    gather_pass(5, 0, [hop])
+                    gather_pass(5, 1, [hop])
+
+            @pl.when(step == 2 * PIECES - 1)
             def _():
-                gather_pass(5)
-                gather_pass(5, 1)
-
-            @pl.when(step == PIECES - 1)
+                gather_end(4)
+                gather_end(5)
+
+        @pl.when(jnp.logical_and(second, within(place, 2, PIECES + 1)))
+        def _():
+            forward_result(place - 2)
+
+        @pl.when(within(place, 1, PIECES + 1))
+        def _():
+            forward_middle(place - 1)
+
+        spread_place = place - jnp.where(first, PIECES, 1)
+
+        @pl.when(within(spread_place, 0, PIECES))
+        def _():
+            forward_spread(spread_place)
+
+        fold_place = place - jnp.where(first, 2 * PIECES, 1)
+
+        @pl.when(within(fold_place, 0, PIECES))
+        def _():
+            @pl.when(jnp.logical_and(second, fold_place < PIECES - 2))
             def _():
-                for part in range(2, PARTS):
-                    gather_end(part)
-
-        @pl.when(jnp.logical_and(second, within(place, 2, PIECES + 1)))
-        def _():
-            forward_result(place - 2)
-
-        @pl.when(within(place, 1, PIECES + 1))
-        def _():
-            forward_middle(place - 1)
-
-        hidden_place = jnp.where(first, place - PIECES, place - 1)
-
-        @pl.when(within(hidden_place, 0, PIECES))
-        def _():
-            @pl.when(jnp.logical_and(second, hidden_place < PIECES - 2))
-            def _():
-                take_start(hidden_place + 2)
-
-            forward_hidden(hidden_place)
+                take_start(fold_place + 2)
+
+            forward_fold(fold_place)
 
             @pl.when(first)
             def _():
-                forward_result(hidden_place)
+                forward_result(fold_place)
 
         return carry
 
-    lax.fori_loop(0, 2 * PIECES + 1, forward, 0)
+    lax.fori_loop(0, 3 * PIECES + 1, forward, 0)
 
     @pl.when(first)
     def _():
@@ -671,6 +683,23 @@
             sums[0, :, spot:spot + LANES] = jnp.where(low_half, one, flip(two)).astype(LOW)
             sums[1, :, spot:spot + LANES] = jnp.where(low_half, flip(one), two).astype(LOW)
 
+    def down_grads():
+        hidden_grads(g_t, e_s, 2 * hidden)
+        if inside:
+            reduce_y(0).start()
+            reduce_y(1).start()
+            mixed_start()
+
+    def up_grads():
+        hidden_grads(m_t, gd_s, hidden)
+        if inside:
+            reduce_y(2).start()
+
+    def reduce_open():
+        if inside:
+            mixed_mid()
+            reduce_mid(0, 3)
+
     def grad_rows(piece):
         return jnp.where(first, here[piece], x_ref[piece])
 
@@ -683,13 +712,9 @@
         grad_low = grad_rows(piece)
         g_t[piece] = grad_low.astype(F32).T.astype(LOW)
 
-        @pl.when(piece == 0)
-        def _():
-            hidden_grads(g_t, e_s, 2 * hidden)
-            if inside:
-                reduce_y(0).start()
-                reduce_y(1).start()
-                mixed_start()
+        @pl.when(jnp.logical_and(first, piece == 0))
+        def _():
+            down_grads()
 
         total = 0.0
         for group in range(2):
@@ -699,11 +724,9 @@
             total = total + mm_back(dz, w_ref[group, :, hidden:2 * hidden])
         swap_start(turned_slots(piece), total.astype(LOW))
 
-        @pl.when(piece == 0)
-        def _():
-            hidden_grads(m_t, gd_s, hidden)
-            if inside:
-                reduce_y(2).start()
+        @pl.when(jnp.logical_and(first, piece == 0))
+        def _():
+            up_grads()
 
     def backward_attention(piece):
         dm = swap_end(turned_slots(piece))
@@ -755,9 +778,12 @@
                 copy.start()
 
     def backward(step, carry):
-        @pl.when(step < PIECES)
-        def _():
-            backward_hidden(PIECES - 1 - step)
+        turn = step // 2
+        even = lax.rem(step, 2) == 0
+
+        @pl.when(jnp.logical_and(jnp.logical_xor(even, first), turn < PIECES))
+        def _():
+            backward_hidden(PIECES - 1 - turn)
 
         @pl.when(step == 0)
         def _():
@@ -770,28 +796,33 @@
                 for t in range(tiles):
                     turn_s[piece, t] = k_s[piece, t].astype(F32).T.astype(LOW)
 
-        if inside:
-            @pl.when(step == PIECES)
+        @pl.when(jnp.logical_and(first, step == 2 * PIECES))
+        def _():
+            reduce_open()
+
+        @pl.when(jnp.logical_and(jnp.logical_xor(even, second), turn >= 1))
+        def _():
+            @pl.when(turn >= 2)
             def _():
-                mixed_mid()
-                reduce_mid(0, 3)
-                reduce_mid(1)
-
-        @pl.when(step >= 2)
-        def _():
-            backward_result(PIECES + 1 - step)
-
-        @pl.when(step >= 1)
-        def _():
-            backward_attention(PIECES - step)
+                backward_result(PIECES + 1 - turn)
+
+            backward_attention(PIECES - turn)
 
         return carry
 
-    lax.fori_loop(0, PIECES + 1, backward, 0)
+    lax.fori_loop(0, 2 * PIECES + 2, backward, 0)
+    backward_result(0)
+
+    @pl.when(second)
+    def _():
+        down_grads()
+        up_grads()
+        reduce_open()
+
     head_grads()
     if inside:
         reduce_y(4).start()
-    backward_result(0)
+        reduce_mid(1)
 
     def emit_stage(run):
         @pl.when(first)

time: 301 us -> 293 us (0.973)
  Pallas kernels: 284 us -> 276 us
    pallas_call x1, Pallas kernels: 284 us -> 276 us  [run_layers(): pl.pallas_call(functools.partial(layers_kernel, width, depth, inside), ou...]
where the time goes in v5:
time: 293 us
  Pallas kernels  276 us (94%)
  local copies, waits for them, and re-layouts  15.7 us (5%)
    pallas_call x1, Pallas kernels, run_layers(): pl.pallas_call(functools.partial(layers_kernel, width, depth, inside), ou...  276 us
    unnamed x9, local copies, waits for them, and re-layouts  8.54 us

profile of v5, /device:TPU:0, one launch (start us, length us, event | category | flops | bytes accessed | tf_op | source)
XLA Modules:
  0.0 293.1 jit_solution(14018429293201095847)
XLA Ops:
  0.6 0.0 copy-start
  0.7 1.0 copy-done
  1.7 0.1 constant_dynamic-slice_fusion
  1.7 0.1 constant_dynamic-slice_fusion.1
  1.8 1.0 copy.17
  2.9 1.0 copy.21
  3.9 0.8 concatenate.15.refs_3_
  4.7 275.5 %layers.1 = (bf16[2,4,256,768]{3,2,1,0:T(8,128)(2,1)}, f32[192,2304]{1,0:T(8,128)}, f32[8,768]{1,0:T(8,128)}, bf16[8,192,256]{2,1,0:T(8,128)(2,1)}) custom-call(s32[2,8]{1,0:T(2,128)} %refs_0_.1, bf16[2,4,256,768]{3,2,1,0:T(8,128)(2,1)} %bitcast.53, bf16[2,192]{1,0:T(2,128)(2,1)} %bitcast.60, bf16[192,768]{1,0:T(8,128)(2,1)} %concatenate.15.refs_3_, ...), custom_call_target="tpu_custom_call" | custom-call | tf_op jit(solution)/shard_map/layers/pallas_call | solution.py:976
  280.3 0.7 slice.98
  281.0 0.1 dynamic-slice_bitcast_fusion
  281.1 0.6 slice_bitcast_fusion.10
  281.7 1.1 fusion.1
  282.8 1.0 fusion
  283.8 2.3 slice_bitcast_fusion
  286.1 0.0 copy-start.1
  286.1 0.8 copy.19
  287.0 1.1 copy.18
  288.0 0.0 copy-done.1
  288.1 0.2 concatenate.18
  288.3 1.0 convert_element_type.3
  289.3 3.8 %copy.23 = bf16[1,2048,768]{2,1,0:T(8,128)(2,1)} copy(bf16[1,2048,768]{2,1,0:T(8,128)(2,1)} %bitcast.54) | data formatting | bytes 6291456
  (11 shorter events, 0.2 us)
Async XLA Ops:
  0.6 1.0 copy-start
  286.1 1.9 copy-start.1

commit v6 on v5

--- a/solution.py
+++ b/solution.py
@@ -185,10 +185,10 @@
     block = 2 * LANES
     last = block // 2
     spans = [
-        (2 * hidden, block), (2 * hidden + block, last), (hidden, block), (hidden + block, block),
+        (2 * hidden, block), (hidden, block), (hidden + block, block),
         (block, block), (2 * block, block), (0, block),
         (hidden + 2 * block, last), (hidden + 2 * block + last, last)]
-    mixed_at = pl.ds(2 * hidden + block + last, block + last)
+    mixed_at = pl.ds(2 * hidden + block, 2 * block)
 
     def block_at(index):
         return pl.ds(spans[index][0], spans[index][1])
@@ -346,12 +346,14 @@
         gather_start(2)
         gather_pass(1)
         gather_start(3)
-        gather_pass(2)
+        gather_pass(2, 0, [0, 1])
         gather_start(4)
         for step in range(1, depth):
             gather_gain(step).wait()
         gather_end(0)
         gather_end(1)
+        gather_pass(2, 0, [2])
+        gather_pass(3, 0, [0])
         for index in range(3):
             own_copy(index).wait()
         gains = jnp.concatenate([gain_all[place, :, :rows_own] for place in range(depth)], axis=1)
@@ -589,23 +591,35 @@
             forward_attention(place)
 
         if inside:
+            @pl.when(step == 0)
+            def _():
+                gather_pass(3, 0, [1])
+                gather_start(5)
+                gather_cross()
+
             @pl.when(step == 1)
             def _():
-                gather_pass(3)
-                gather_start(5)
-                gather_cross()
-
-            @pl.when(step == PIECES - 1)
+                gather_pass(3, 0, [2])
+                gather_pass(4, 0, [0])
+
+            @pl.when(step == 2)
             def _():
-                gather_pass(4)
+                gather_pass(4, 0, [1])
+                gather_pass(5, 0, [0])
+                gather_pass(5, 1, [0])
+
+            @pl.when(step == 3)
+            def _():
+                gather_pass(4, 0, [2])
+                gather_pass(5, 0, [1])
+                gather_pass(5, 1, [1])
                 gather_end(2)
                 gather_end(3)
 
-            for hop in range(depth - 1):
-                @pl.when(step == PIECES + hop)
-                def _(hop=hop):
-                    gather_pass(5, 0, [hop])
-                    gather_pass(5, 1, [hop])
+            @pl.when(step == 2 * PIECES - 2)
+            def _():
+                gather_pass(5, 0, [2])
+                gather_pass(5, 1, [2])
 
             @pl.when(step == 2 * PIECES - 1)
             def _():
@@ -687,18 +701,13 @@
         hidden_grads(g_t, e_s, 2 * hidden)
         if inside:
             reduce_y(0).start()
-            reduce_y(1).start()
             mixed_start()
 
     def up_grads():
         hidden_grads(m_t, gd_s, hidden)
         if inside:
+            reduce_y(1).start()
             reduce_y(2).start()
-
-    def reduce_open():
-        if inside:
-            mixed_mid()
-            reduce_mid(0, 3)
 
     def grad_rows(piece):
         return jnp.where(first, here[piece], x_ref[piece])
@@ -796,10 +805,6 @@
                 for t in range(tiles):
                     turn_s[piece, t] = k_s[piece, t].astype(F32).T.astype(LOW)
 
-        @pl.when(jnp.logical_and(first, step == 2 * PIECES))
-        def _():
-            reduce_open()
-
         @pl.when(jnp.logical_and(jnp.logical_xor(even, second), turn >= 1))
         def _():
             @pl.when(turn >= 2)
@@ -817,12 +822,8 @@
     def _():
         down_grads()
         up_grads()
-        reduce_open()
 
     head_grads()
-    if inside:
-        reduce_y(4).start()
-        reduce_mid(1)
 
     def emit_stage(run):
         @pl.when(first)
@@ -847,38 +848,39 @@
     if inside:
         gain_copy = send(gain_grad_ref, gain_y, sem_gg, (0,), other_y)
         gain_copy.start()
-        reduce_late(0)
-        mixed_late()
-        reduce_mid(2, 5)
-        reduce_late(1)
+        reduce_y(3).start()
+        mixed_mid()
+        reduce_mid(0, 4)
         gain_copy.wait()
         gain_y[...] = gain_y[...] + gain_grad_ref[...]
         gain_sends = [
             send(gain_y, gain_z.at[step - 1], sem_gg, (step,), peer(step)) for step in range(1, depth)]
         for copy in gain_sends:
             copy.start()
+        reduce_mid(1)
+        reduce_late(0)
+        reduce_mid(2, 5)
+        mixed_late()
+        reduce_late(1)
         reduce_mid(3, 6)
+        reduce_end(0)
         reduce_late(2)
-        reduce_end(0)
         reduce_mid(4, 7)
+        reduce_end(1)
         reduce_late(3)
-        reduce_end(1)
         reduce_end(2)
         total = gain_y[...]
         for step, copy in enumerate(gain_sends):
             copy.wait()
             total = total + gain_z[step]
         gain_grad_ref[...] = total
-        reduce_mid(5, 8)
+        reduce_mid(5)
         reduce_late(4)
         reduce_end(3)
         emit_stage(pass_outputs)
         reduce_mid(6)
         reduce_late(5)
         reduce_end(4)
-        reduce_mid(7)
-        reduce_late(6)
-        reduce_end(5)
 
         def place(sec, row, unit):
             return (sec * 2 + row) * 2 + unit
@@ -890,17 +892,17 @@
         value_x = send(value_ref.at[mine], value_ref.at[mine], sem_va, (0,), other_layer)
         value_x.start()
         mixed_end()
-        reduce_mid(8)
-        reduce_late(7)
-        reduce_end(6)
+        reduce_mid(7)
+        reduce_late(6)
+        reduce_end(5)
         value_x.wait()
         value_y = []
         for sec in range(2):
             at = place(sec, lane_y, core)
             value_y.append(send(value_ref.at[at], value_ref.at[at], sem_va, (1 + sec,), other_y))
             value_y[-1].start()
-        reduce_late(8)
-        reduce_end(7)
+        reduce_late(7)
+        reduce_end(6)
         for copy in value_y:
             copy.wait()
         value_c = []
@@ -910,7 +912,7 @@
                 value_c.append(
                     send(value_ref.at[at], value_ref.at[at], sem_va, (3 + 2 * sec + row,), other_core))
                 value_c[-1].start()
-        reduce_end(8)
+        reduce_end(7)
         for copy in value_c:
             copy.wait()
         reduce_sent()
@@ -970,8 +972,8 @@
             low((2, width, columns)), full((depth, 8, -(-rows_own // LANES) * LANES)),
             low((2, width, columns)), low((width, columns)), low((depth - 1, rows_own, columns)),
             full((8, width)), full((depth - 1, 8, width)),
-            dma(2, PARTS + 1, depth - 1, 2), dma(2, PARTS, depth), dma(2, depth), dma(2, 9),
-            dma(2, 9, 3), dma(2, 2, 4), dma(2, depth), dma(2, 7),
+            dma(2, PARTS + 1, depth - 1, 2), dma(2, PARTS, depth), dma(2, depth), dma(2, 8),
+            dma(2, 8, 3), dma(2, 2, 4), dma(2, depth), dma(2, 7),
         ]
     return pl.pallas_call(
         functools.partial(layers_kernel, width, depth, inside),

time: 293 us -> 282 us (0.962)
  Pallas kernels: 276 us -> 264 us
    pallas_call x1, Pallas kernels: 276 us -> 264 us  [run_layers(): pl.pallas_call(functools.partial(layers_kernel, width, depth, inside), ou...]
where the time goes in v6:
time: 282 us
  Pallas kernels  264 us (94%)
  local copies, waits for them, and re-layouts  15.7 us (6%)
    pallas_call x1, Pallas kernels, run_layers(): pl.pallas_call(functools.partial(layers_kernel, width, depth, inside), ou...  264 us
    unnamed x9, local copies, waits for them, and re-layouts  8.54 us

profile of v6, /device:TPU:0, one launch (start us, length us, event | category | flops | bytes accessed | tf_op | source)
XLA Modules:
  0.0 282.0 jit_solution(8562839181535923662)
XLA Ops:
  0.6 0.0 copy-start
  0.7 1.0 copy-done
  1.7 0.1 constant_dynamic-slice_fusion
  1.7 0.1 constant_dynamic-slice_fusion.1
  1.8 1.0 copy.17
  2.9 1.0 copy.21
  3.9 0.8 concatenate.15.refs_3_
  4.7 264.4 %layers.1 = (bf16[2,4,256,768]{3,2,1,0:T(8,128)(2,1)}, f32[192,2304]{1,0:T(8,128)}, f32[8,768]{1,0:T(8,128)}, bf16[8,192,256]{2,1,0:T(8,128)(2,1)}) custom-call(s32[2,8]{1,0:T(2,128)} %refs_0_.1, bf16[2,4,256,768]{3,2,1,0:T(8,128)(2,1)} %bitcast.53, bf16[2,192]{1,0:T(2,128)(2,1)} %bitcast.60, bf16[192,768]{1,0:T(8,128)(2,1)} %concatenate.15.refs_3_, ...), custom_call_target="tpu_custom_call" | custom-call | tf_op jit(solution)/shard_map/layers/pallas_call | solution.py:978
  269.2 0.7 slice.98
  269.9 0.1 dynamic-slice_bitcast_fusion
  270.0 0.6 slice_bitcast_fusion.10
  270.6 1.1 fusion.1
  271.7 1.0 fusion
  272.7 2.3 slice_bitcast_fusion
  275.0 0.0 copy-start.1
  275.0 0.8 copy.19
  275.9 1.1 copy.18
  276.9 0.0 copy-done.1
  277.0 0.2 concatenate.18
  277.2 1.0 convert_element_type.3
  278.2 3.8 %copy.23 = bf16[1,2048,768]{2,1,0:T(8,128)(2,1)} copy(bf16[1,2048,768]{2,1,0:T(8,128)(2,1)} %bitcast.54) | data formatting | bytes 6291456
  (11 shorter events, 0.2 us)
Async XLA Ops:
  0.6 1.0 copy-start
  275.0 1.9 copy-start.1

commit v7 on v6

--- a/solution.py
+++ b/solution.py
@@ -57,14 +57,14 @@
     part_refs = take(3 if inside else 1)
     out_ref, grad_ref, gain_grad_ref = take(3)
     if inside:
-        (value_ref,) = take(1)
-    (wa, q_s, k_s, v_s, turn_s, o_s, lse_s, plain1, plain2, fac1, fac2,
+        head_out, gain_out, value_out = take(3)
+    (wa, q_s, k_s, v_s, turn_s, o_s, lse_s, plain1, plain2, fac_s,
      a_t, m_t, g_t, h_t, e_s, gd_s, do_s, spare, bias_s, x_ref, start_s,
      there, there_v, here, here_v, swap_out, swap_in,
-     sem_x, sem_v, sem_f, sem_c, sem_o, sem_oc, sem_l) = take(35)
+     sem_x, sem_v, sem_f, sem_c, sem_o, sem_oc, sem_l) = take(34)
     if inside:
-        (w_ref, gain_all, sums, y_in, z_in, gain_y, gain_z,
-         sem_az, sem_ay, sem_gz, sem_ry, sem_rz, sem_rm, sem_gg, sem_va) = take(15)
+        (w_ref, gain_all, sums, y_in, z_in, gain_y, gain_z, value_ref,
+         sem_az, sem_ay, sem_gz, sem_ry, sem_rz, sem_rm, sem_gg, sem_va) = take(16)
     else:
         w_ref, sums = part_refs[0], grad_ref
 
@@ -189,6 +189,7 @@
         (block, block), (2 * block, block), (0, block),
         (hidden + 2 * block, last), (hidden + 2 * block + last, last)]
     mixed_at = pl.ds(2 * hidden + block, 2 * block)
+    mixed_out = pl.ds(hidden + block, 2 * block)
 
     def block_at(index):
         return pl.ds(spans[index][0], spans[index][1])
@@ -230,11 +231,18 @@
                 sums[lane_y, rows, at].astype(F32) + z_in[share, :, at].astype(F32)).astype(LOW)
         reduce_far(index).start()
 
+    def summed(at):
+        return sums[lane_y, rows_at(deep), at].astype(F32) + z_in[2, :, at].astype(F32)
+
+    def head_tile(index):
+        return summed(pl.ds(index * LANES, LANES))
+
     def reduce_end(index):
         at = block_at(index)
         reduce_far(index).wait_recv()
-        grad_ref[:, at] = (
-            sums[lane_y, rows_at(deep), at].astype(F32) + z_in[2, :, at].astype(F32))
+        spot, size = spans[index]
+        if spot >= hidden:
+            grad_ref[:, spot - hidden:spot - hidden + size] = summed(at)
 
     def mixed_home(row, share):
         if row == 0:
@@ -278,14 +286,13 @@
             total = (sums[mixed_group(row), rows_at(deep), mixed_at].astype(F32)
                      + mixed_home(row, 2)[...].astype(F32))
             if row == 0:
-                grad_ref[:, mixed_at] = total
+                grad_ref[:, mixed_out] = total
             else:
                 sums[mixed_group(row), rows_at(deep), mixed_at] = total.astype(LOW)
-        mixed_cross().start()
 
     def mixed_end():
         mixed_cross().wait_recv()
-        grad_ref[:, mixed_at] += mixed_home(1, 3)[...].astype(F32)
+        grad_ref[:, mixed_out] += mixed_home(1, 3)[...].astype(F32)
 
     def reduce_sent():
         for index in range(len(spans)):
@@ -510,7 +517,7 @@
         rows = jnp.where(first, x_ref[piece], here[piece]).astype(F32)
         plain, factor = normalize(rows)
         plain1[piece] = plain.astype(LOW)
-        fac1[piece] = factor
+        fac_s[piece, :, 0:1] = factor
         normed = plain * gain1
         a_t[piece] = normed.T.astype(LOW)
         qkv = mm(normed.astype(LOW), wa[:, :qkv_cols])
@@ -545,7 +552,7 @@
     def forward_spread(piece):
         plain, factor = normalize(get_rows(piece))
         plain2[piece] = plain.astype(LOW)
-        fac2[piece] = factor
+        fac_s[piece, :, 1:2] = factor
         normed = plain * gain2
         m_t[piece] = normed.T.astype(LOW)
         normed = normed.astype(LOW)
@@ -715,7 +722,10 @@
     def backward_hidden(piece):
         @pl.when(first)
         def _():
-            take_start(piece)
+            @pl.when(piece == PIECES - 1)
+            def _():
+                take_start(piece)
+
             hand_on(piece).wait()
 
         grad_low = grad_rows(piece)
@@ -741,7 +751,7 @@
         dm = swap_end(turned_slots(piece))
         plain = plain2[piece].astype(F32)
         gain_grad_ref[1:2, :] += jnp.sum(dm * plain, axis=0, keepdims=True)
-        middle = grad_rows(piece).astype(F32) + norm_back(dm, plain, fac2[piece], gain2)
+        middle = grad_rows(piece).astype(F32) + norm_back(dm, plain, fac_s[piece, :, 1:2], gain2)
         h_t[piece] = middle.T.astype(LOW)
         dmixed = mm(middle.astype(LOW), wa[:, qkv_cols:]).astype(LOW)
         for t in range(tiles):
@@ -775,7 +785,7 @@
         da = swap_end(last_slots(piece))
         plain = plain1[piece].astype(F32)
         gain_grad_ref[0:1, :] += jnp.sum(da * plain, axis=0, keepdims=True)
-        there[piece] = (get_rows(piece) + norm_back(da, plain, fac1[piece], gain1)).astype(LOW)
+        there[piece] = (get_rows(piece) + norm_back(da, plain, fac_s[piece, :, 0:1], gain1)).astype(LOW)
 
         @pl.when(second)
         def _():
@@ -810,6 +820,10 @@
             @pl.when(turn >= 2)
             def _():
                 backward_result(PIECES + 1 - turn)
+
+            @pl.when(jnp.logical_and(first, turn < PIECES))
+            def _():
+                take_start(PIECES - 1 - turn)
 
             backward_attention(PIECES - turn)
 
@@ -873,12 +887,15 @@
         for step, copy in enumerate(gain_sends):
             copy.wait()
             total = total + gain_z[step]
-        gain_grad_ref[...] = total
+        gain_out[...] = functools.reduce(jnp.add, [
+            jnp.where(deep == index, total[0:2, index * rows_own:(index + 1) * rows_own], 0.0)
+            for index in range(depth)])
         reduce_mid(5)
         reduce_late(4)
         reduce_end(3)
         emit_stage(pass_outputs)
         reduce_mid(6)
+        mixed_cross().start()
         reduce_late(5)
         reduce_end(4)
 
@@ -888,22 +905,21 @@
         mine = place(section, lane_y, core)
         for half_tile, tile_index in enumerate((2, 5)):
             value_ref[mine, :, half_tile * LANES:(half_tile + 1) * LANES] = (
-                grad_ref[:, tile_index * LANES:(tile_index + 1) * LANES].astype(LOW))
-        value_x = send(value_ref.at[mine], value_ref.at[mine], sem_va, (0,), other_layer)
-        value_x.start()
-        mixed_end()
+                head_tile(tile_index).astype(LOW))
+        value_y = send(value_ref.at[mine], value_ref.at[mine], sem_va, (0,), other_y)
+        value_y.start()
         reduce_mid(7)
         reduce_late(6)
         reduce_end(5)
-        value_x.wait()
-        value_y = []
-        for sec in range(2):
-            at = place(sec, lane_y, core)
-            value_y.append(send(value_ref.at[at], value_ref.at[at], sem_va, (1 + sec,), other_y))
-            value_y[-1].start()
+        value_y.wait()
+        value_x = []
+        for row in range(2):
+            at = place(section, row, core)
+            value_x.append(send(value_ref.at[at], value_ref.at[at], sem_va, (1 + row,), other_layer))
+            value_x[-1].start()
         reduce_late(7)
         reduce_end(6)
-        for copy in value_y:
+        for copy in value_x:
             copy.wait()
         value_c = []
         for sec in range(2):
@@ -912,9 +928,23 @@
                 value_c.append(
                     send(value_ref.at[at], value_ref.at[at], sem_va, (3 + 2 * sec + row,), other_core))
                 value_c[-1].start()
+        mixed_end()
         reduce_end(7)
+        edge = 2 * HEAD
+
+        def columns(kind, pair, upper):
+            rest = head_tile(pair)
+            return jnp.concatenate(
+                [head_tile(kind), rest[:, HEAD:] if upper else rest[:, :HEAD]], axis=1)
+
+        head_out[0] = columns(0, 4, False)
+        head_out[1] = columns(1, 4, True)
+        head_out[2] = columns(3, 5, True)
         for copy in value_c:
             copy.wait()
+        value_out[...] = jnp.concatenate(
+            [value_ref[index, :, :edge + HEAD] for index in range(value_out.shape[1] // (edge + HEAD))],
+            axis=1).astype(F32)
         reduce_sent()
     else:
         emit_stage(pass_outputs)
@@ -928,7 +958,7 @@
             hand_values(piece).wait_send()
 
 
-def run_layers(lengths, x_rows, gains, weights, depth, inside):
+def run_layers(lengths, x_rows, gains, weights, cols, value_cols, depth, inside):
     width = x_rows.shape[3]
     tiles = width // 2 // LANES
     rows_own = width // depth
@@ -946,7 +976,7 @@
     dma = lambda *shape: pltpu.SemaphoreType.DMA(shape)
     out_shape = [
         jax.ShapeDtypeStruct((2,) + flat, LOW),
-        jax.ShapeDtypeStruct((rows_own, columns), F32) if inside
+        jax.ShapeDtypeStruct((rows_own, 2 * width), F32) if inside
         else jax.ShapeDtypeStruct(weights[0].shape, LOW),
         jax.ShapeDtypeStruct((8, width), F32),
     ]
@@ -955,7 +985,7 @@
         low((width, 4 * tiles * LANES)),
         low(per_tile), low(per_tile), low(per_tile), low(turned), low(per_tile),
         full((PIECES, 2 * tiles, 1, PIECE)),
-        low(flat), low(flat), full((PIECES, PIECE, 1)), full((PIECES, PIECE, 1)),
+        low(flat), low(flat), full((PIECES, PIECE, 2)),
         low(flat_turned), low(flat_turned), low(flat_turned), low(flat_turned),
         low(wide), low(wide), low((tiles, PIECE, LANES)),
         full((PIECES, 2 * tiles, PIECE, LANES)),
@@ -966,12 +996,16 @@
         dma(2, PIECES), dma(4 + PIECES),
     ]
     if inside:
-        out_shape.append(jax.ShapeDtypeStruct((8, rows_own, 2 * LANES), LOW))
-        out_specs.append(vmem)
+        out_shape += [
+            jax.ShapeDtypeStruct((3, rows_own, cols), F32),
+            jax.ShapeDtypeStruct((2, rows_own), F32),
+            jax.ShapeDtypeStruct((rows_own, value_cols), F32)]
+        out_specs += [vmem] * 3
         scratch += [
             low((2, width, columns)), full((depth, 8, -(-rows_own // LANES) * LANES)),
             low((2, width, columns)), low((width, columns)), low((depth - 1, rows_own, columns)),
             full((8, width)), full((depth - 1, 8, width)),
+            low((8, rows_own, 2 * LANES)),
             dma(2, PARTS + 1, depth - 1, 2), dma(2, PARTS, depth), dma(2, depth), dma(2, 8),
             dma(2, 8, 3), dma(2, 2, 4), dma(2, depth), dma(2, 7),
         ]
@@ -1033,27 +1067,27 @@
         gains = lax.all_gather(norm_gains[0], "dp", axis=0, tiled=True).astype(F32).T
     x_rows = ends_in[0].reshape(2, PIECES, PIECE, width)
     kept = width // cols + fresh
-    edge = 2 * HEAD
-    results = run_layers(seq_lengths, x_rows, gains, weights, depth, inside)
+    results = run_layers(
+        seq_lengths, x_rows, gains, weights, cols, value_weight.shape[1], depth, inside)
     both = results[0].reshape(2 * MB_TOK, width)
     if inside:
-        _, grads, gain_grads, values = results
-        rows_own = width // depth
-        gain_rows = lax.dynamic_slice_in_dim(
-            gain_grads[:2], lax.axis_index("dp") * rows_own, rows_own, 1).T
-        values = values[:, :, :cols]
+        _, grads, _, heads, gain_rows, d_value = results
+        attn_gain, mlp_gain = gain_rows[0], gain_rows[1]
+        d_qk = jnp.stack([heads[0], heads[1]], axis=1)
+        d_out = heads[2].T
+        d_up, d_down = grads[:, :width], grads[:, width:].T
     else:
         _, grads, gain_grads = results
         grads = lax.psum_scatter(grads, "y", scatter_dimension=0, tiled=False)
         grads = lax.psum_scatter(grads, "dp", scatter_dimension=0, tiled=True)
         gain_rows = lax.psum(gain_grads[:2], "y").T
         gain_rows = lax.psum_scatter(gain_rows, "dp", scatter_dimension=0, tiled=True)
-        values = lax.all_gather(
-            unpack(grads)[1].astype(LOW), ("section", "y", "core"), axis=0)
-    d_qk, _, d_out, d_up, d_down = unpack(grads.astype(F32))
-    d_value = jnp.concatenate([values[index] for index in range(kept)], axis=1).astype(F32)
+        attn_gain, mlp_gain = gain_rows[:, 0], gain_rows[:, 1]
+        d_qk, d_value, d_out, d_up, d_down = unpack(grads.astype(F32))
+        values = lax.all_gather(d_value.astype(LOW), ("section", "y", "core"), axis=0)
+        d_value = jnp.concatenate([values[index] for index in range(kept)], axis=1).astype(F32)
     return (
-        both[None], gain_rows[:, 0][None], gain_rows[:, 1][None], d_qk[None], d_value,
+        both[None], attn_gain[None], mlp_gain[None], d_qk[None], d_value,
         d_out[None], d_up[None], d_down[None])
 
 

time: 282 us -> 276 us (0.979)
  local copies, waits for them, and re-layouts: 15.7 us -> 12.1 us
    unnamed x9 -> x14, local copies, waits for them, and re-layouts: 8.54 us -> 7.49 us
where the time goes in v7:
time: 276 us
  Pallas kernels  263 us (95%)
  local copies, waits for them, and re-layouts  12.1 us (4%)
    pallas_call x1, Pallas kernels, run_layers(): pl.pallas_call(functools.partial(layers_kernel, width, depth, inside), ou...  263 us
    unnamed x14, local copies, waits for them, and re-layouts  7.49 us

profile of v7, /device:TPU:0, one launch (start us, length us, event | category | flops | bytes accessed | tf_op | source)
XLA Modules:
  0.0 275.8 jit_solution(17677515464761403719)
XLA Ops:
  0.6 0.0 copy-start
  0.7 1.0 copy-done
  1.7 0.1 constant_dynamic-slice_fusion
  1.7 0.1 constant_dynamic-slice_fusion.1
  1.8 1.0 copy.17
  2.9 1.0 copy.21
  3.9 0.8 concatenate.3.refs_3_
  4.7 262.9 %layers.1 = (bf16[2,4,256,768]{3,2,1,0:T(8,128)(2,1)}, f32[192,1536]{1,0:T(8,128)}, f32[8,768]{1,0:T(8,128)}, f32[3,192,192]{2,1,0:T(8,128)}, f32[2,192]{1,0:T(2,128)}, /*index=5*/f32[192,1152]{1,0:T(8,128)}) custom-call(s32[2,8]{1,0:T(2,128)} %refs_0_.1, bf16[2,4,256,768]{3,2,1,0:T(8,128)(2,1)} %bitcast.37, bf16[2,192]{1,0:T(2,128)(2,1)} %bitcast.44, ...), custom_call_target="tpu_custom_call" | custom-call | tf_op jit(solution)/shard_map/layers/pallas_call | solution.py:1012
  267.6 0.0 copy-start.2
  267.6 1.3 fusion
  268.9 1.2 slice_bitcast_fusion.2
  270.1 0.8 copy.19
  270.9 0.0 copy-start.1
  270.9 1.1 copy.18
  272.0 0.0 copy-done.2
  272.0 1.1 slice_bitcast_fusion
  273.1 0.0 copy-done.1
  273.1 0.0 copy-start.3
  273.1 1.7 copy.24
  274.7 0.1 copy-done.3
  274.9 0.9 copy.25
  (8 shorter events, 0.1 us)
Async XLA Ops:
  0.6 1.0 copy-start
  267.6 4.4 %copy-start.2 = (f32[192,1536]{1,0:T(8,128)S(1)}, f32[192,1536]{1,0:T(8,128)}, u32[]{:S(2)}) copy-start(f32[192,1536]{1,0:T(8,128)} %get-tuple-element.17) | copy-start | bytes 3538948
  270.9 2.2 copy-start.1
  273.1 1.8 copy-start.3

commit v8 on v7

--- a/solution.py
+++ b/solution.py
@@ -562,8 +562,16 @@
             bent = jnp.tanh(GELU_K * z * (1.0 + GELU_C * square))
             upper = 0.5 * (1.0 + bent)
             slope = upper + 0.5 * z * (1.0 - bent * bent) * (GELU_K * (1.0 + 3.0 * GELU_C * square))
+            slope = jnp.where(first, slope, slope * gd_s[piece, group].astype(F32))
             gd_s[piece, group] = slope.astype(LOW)
             e_s[piece, group] = (z * upper).astype(LOW)
+
+    def forward_ahead(piece, carry):
+        grad_low = x_ref[piece]
+        g_t[piece] = grad_low.astype(F32).T.astype(LOW)
+        for group in range(2):
+            gd_s[piece, group] = mm(grad_low, w_ref[group, :, 2 * hidden:]).astype(LOW)
+        return carry
 
     def forward_fold(piece):
         total = 0.0
@@ -633,6 +641,10 @@
                 gather_end(4)
                 gather_end(5)
 
+        @pl.when(jnp.logical_and(second, step == 2 * PIECES - 1))
+        def _():
+            lax.fori_loop(0, PIECES, forward_ahead, 0)
+
         @pl.when(jnp.logical_and(second, within(place, 2, PIECES + 1)))
         def _():
             forward_result(place - 2)
@@ -673,9 +685,9 @@
 
     gain_grad_ref[...] = jnp.zeros_like(gain_grad_ref)
 
-    def hidden_grads(left, right, base):
+    def hidden_grads(left, right, base, low_end, high_end):
         def one(index, carry):
-            group, column = index // (hidden // block), index % (hidden // block)
+            group, column = lax.rem(index, 2), index // 2
             spot = pl.multiple_of(column * block, block)
             total = 0.0
             for piece in range(PIECES):
@@ -683,7 +695,7 @@
             sums[group, :, pl.ds(pl.multiple_of(base + spot, block), block)] = total.astype(LOW)
             return carry
 
-        lax.fori_loop(0, 2 * (hidden // block), one, 0)
+        lax.fori_loop(2 * low_end, 2 * high_end, one, 0)
 
     def head_grads():
         pairs = []
@@ -704,14 +716,18 @@
             sums[0, :, spot:spot + LANES] = jnp.where(low_half, one, flip(two)).astype(LOW)
             sums[1, :, spot:spot + LANES] = jnp.where(low_half, flip(one), two).astype(LOW)
 
+    columns_in = hidden // block
+
     def down_grads():
-        hidden_grads(g_t, e_s, 2 * hidden)
+        hidden_grads(g_t, e_s, 2 * hidden, 0, 1)
         if inside:
             reduce_y(0).start()
+        hidden_grads(g_t, e_s, 2 * hidden, 1, columns_in)
+        if inside:
             mixed_start()
 
     def up_grads():
-        hidden_grads(m_t, gd_s, hidden)
+        hidden_grads(m_t, gd_s, hidden, 0, columns_in)
         if inside:
             reduce_y(1).start()
             reduce_y(2).start()
@@ -722,25 +738,26 @@
     def backward_hidden(piece):
         @pl.when(first)
         def _():
-            @pl.when(piece == PIECES - 1)
+            @pl.when(jnp.logical_or(piece == PIECES - 1, piece == 0))
             def _():
                 take_start(piece)
 
             hand_on(piece).wait()
 
-        grad_low = grad_rows(piece)
-        g_t[piece] = grad_low.astype(F32).T.astype(LOW)
-
-        @pl.when(jnp.logical_and(first, piece == 0))
-        def _():
-            down_grads()
+            grad_low = here[piece]
+            g_t[piece] = grad_low.astype(F32).T.astype(LOW)
+
+            @pl.when(piece == 0)
+            def _():
+                down_grads()
+
+            for group in range(2):
+                dz = mm(grad_low, w_ref[group, :, 2 * hidden:]) * gd_s[piece, group].astype(F32)
+                gd_s[piece, group] = dz.astype(LOW)
 
         total = 0.0
         for group in range(2):
-            dz = mm(grad_low, w_ref[group, :, 2 * hidden:]) * gd_s[piece, group].astype(F32)
-            dz = dz.astype(LOW)
-            gd_s[piece, group] = dz
-            total = total + mm_back(dz, w_ref[group, :, hidden:2 * hidden])
+            total = total + mm_back(gd_s[piece, group], w_ref[group, :, hidden:2 * hidden])
         swap_start(turned_slots(piece), total.astype(LOW))
 
         @pl.when(jnp.logical_and(first, piece == 0))
@@ -796,13 +813,19 @@
             for copy in emit(piece, there):
                 copy.start()
 
+    last_ahead = 2 * PIECES - 2
+
     def backward(step, carry):
         turn = step // 2
         even = lax.rem(step, 2) == 0
-
-        @pl.when(jnp.logical_and(jnp.logical_xor(even, first), turn < PIECES))
-        def _():
-            backward_hidden(PIECES - 1 - turn)
+        hidden_first = jnp.logical_or(
+            step == last_ahead, jnp.logical_and(jnp.logical_not(even), step < last_ahead))
+        hidden_second = jnp.logical_and(even, turn < PIECES)
+        hidden_piece = PIECES - 1 - jnp.where(step == last_ahead, PIECES - 1, turn)
+
+        @pl.when(jnp.where(first, hidden_first, hidden_second))
+        def _():
+            backward_hidden(hidden_piece)
 
         @pl.when(step == 0)
         def _():
@@ -815,17 +838,24 @@
                 for t in range(tiles):
                     turn_s[piece, t] = k_s[piece, t].astype(F32).T.astype(LOW)
 
-        @pl.when(jnp.logical_and(jnp.logical_xor(even, second), turn >= 1))
-        def _():
-            @pl.when(turn >= 2)
-            def _():
-                backward_result(PIECES + 1 - turn)
-
-            @pl.when(jnp.logical_and(first, turn < PIECES))
-            def _():
-                take_start(PIECES - 1 - turn)
-
-            backward_attention(PIECES - turn)
+        mixed_first = jnp.logical_or(
+            jnp.logical_and(step > last_ahead, step <= 2 * PIECES),
+            jnp.logical_and(even, jnp.logical_and(step >= 2, step < last_ahead)))
+        mixed_second = jnp.logical_and(jnp.logical_not(even), turn >= 1)
+        place = PIECES - jnp.where(
+            first, jnp.where(step > last_ahead, step - last_ahead + PIECES - 2, turn), turn)
+
+        @pl.when(jnp.where(first, mixed_first, mixed_second))
+        def _():
+            @pl.when(place < PIECES - 1)
+            def _():
+                backward_result(place + 1)
+
+            @pl.when(jnp.logical_and(first, place >= 2))
+            def _():
+                take_start(place - 1)
+
+            backward_attention(place)
 
         return carry
 

time: 276 us -> 272 us (0.986)
  Pallas kernels: 263 us -> 259 us
    pallas_call x1, Pallas kernels: 263 us -> 259 us  [run_layers(): pl.pallas_call(functools.partial(layers_kernel, width, depth, inside), ou...]
where the time goes in v8:
time: 272 us
  Pallas kernels  259 us (95%)
  local copies, waits for them, and re-layouts  12.1 us (4%)
    pallas_call x1, Pallas kernels, run_layers(): pl.pallas_call(functools.partial(layers_kernel, width, depth, inside), ou...  259 us
    unnamed x14, local copies, waits for them, and re-layouts  7.49 us

profile of v8, /device:TPU:0, one launch (start us, length us, event | category | flops | bytes accessed | tf_op | source)
XLA Modules:
  0.0 271.6 jit_solution(2872183656764326769)
XLA Ops:
  0.6 0.0 copy-start
  0.7 1.0 copy-done
  1.7 0.1 constant_dynamic-slice_fusion
  1.7 0.1 constant_dynamic-slice_fusion.1
  1.8 1.0 copy.17
  2.9 1.0 copy.21
  3.9 0.8 concatenate.3.refs_3_
  4.7 258.7 %layers.1 = (bf16[2,4,256,768]{3,2,1,0:T(8,128)(2,1)}, f32[192,1536]{1,0:T(8,128)}, f32[8,768]{1,0:T(8,128)}, f32[3,192,192]{2,1,0:T(8,128)}, f32[2,192]{1,0:T(2,128)}, /*index=5*/f32[192,1152]{1,0:T(8,128)}) custom-call(s32[2,8]{1,0:T(2,128)} %refs_0_.1, bf16[2,4,256,768]{3,2,1,0:T(8,128)(2,1)} %bitcast.37, bf16[2,192]{1,0:T(2,128)(2,1)} %bitcast.44, ...), custom_call_target="tpu_custom_call" | custom-call | tf_op jit(solution)/shard_map/layers/pallas_call | solution.py:1042
  263.5 0.0 copy-start.2
  263.5 1.3 fusion
  264.8 1.2 slice_bitcast_fusion.2
  266.0 0.8 copy.19
  266.7 0.0 copy-start.1
  266.8 1.1 copy.18
  267.8 0.0 copy-done.2
  267.8 1.1 slice_bitcast_fusion
  268.9 0.0 copy-done.1
  268.9 0.0 copy-start.3
  268.9 1.7 copy.24
  270.6 0.1 copy-done.3
  270.7 0.9 copy.25
  (8 shorter events, 0.1 us)
Async XLA Ops:
  0.6 1.0 copy-start
  263.5 4.4 %copy-start.2 = (f32[192,1536]{1,0:T(8,128)S(1)}, f32[192,1536]{1,0:T(8,128)}, u32[]{:S(2)}) copy-start(f32[192,1536]{1,0:T(8,128)} %get-tuple-element.17) | copy-start | bytes 3538948
  266.7 2.2 copy-start.1
  268.9 1.8 copy-start.3

commit v9 on v8

--- a/solution.py
+++ b/solution.py
@@ -810,8 +810,11 @@
 
         @pl.when(first)
         def _():
-            for copy in emit(piece, there):
-                copy.start()
+            emit_here(piece, there).start()
+
+            @pl.when(piece >= 2)
+            def _():
+                emit_there(piece, there).start()
 
     last_ahead = 2 * PIECES - 2
 
@@ -878,10 +881,19 @@
         def _():
             run(here)
 
-    def pass_outputs(stage):
-        for piece in range(PIECES):
-            emit_there(piece, stage).wait_recv()
-            emit_on(piece).start()
+    def late_outputs():
+        @pl.when(first)
+        def _():
+            for piece in range(2):
+                emit_there(piece, there).start()
+
+    def pass_outputs(pieces):
+        def one(stage):
+            for piece in pieces:
+                emit_there(piece, stage).wait_recv()
+                emit_on(piece).start()
+
+        emit_stage(one)
 
     def finish_outputs(stage):
         for piece in range(PIECES):
@@ -923,7 +935,7 @@
         reduce_mid(5)
         reduce_late(4)
         reduce_end(3)
-        emit_stage(pass_outputs)
+        pass_outputs((3, 2))
         reduce_mid(6)
         mixed_cross().start()
         reduce_late(5)
@@ -939,16 +951,16 @@
         value_y = send(value_ref.at[mine], value_ref.at[mine], sem_va, (0,), other_y)
         value_y.start()
         reduce_mid(7)
-        reduce_late(6)
-        reduce_end(5)
+        late_outputs()
         value_y.wait()
         value_x = []
         for row in range(2):
             at = place(section, row, core)
             value_x.append(send(value_ref.at[at], value_ref.at[at], sem_va, (1 + row,), other_layer))
             value_x[-1].start()
+        reduce_late(6)
+        reduce_end(5)
         reduce_late(7)
-        reduce_end(6)
         for copy in value_x:
             copy.wait()
         value_c = []
@@ -958,8 +970,10 @@
                 value_c.append(
                     send(value_ref.at[at], value_ref.at[at], sem_va, (3 + 2 * sec + row,), other_core))
                 value_c[-1].start()
+        reduce_end(6)
         mixed_end()
         reduce_end(7)
+        pass_outputs((1, 0))
         edge = 2 * HEAD
 
         def columns(kind, pair, upper):
@@ -977,7 +991,8 @@
             axis=1).astype(F32)
         reduce_sent()
     else:
-        emit_stage(pass_outputs)
+        late_outputs()
+        pass_outputs(range(PIECES))
 
     emit_stage(finish_outputs)
 

time: 272 us -> 270 us (level)
  Pallas kernels: 259 us -> 256 us
where the time goes in v9:
time: 270 us; the launch traced here: 269 us
  Pallas kernels  256 us (95%)
  local copies, waits for them, and re-layouts  12.1 us (4%)
    pallas_call x1, Pallas kernels, run_layers(): pl.pallas_call(functools.partial(layers_kernel, width, depth, inside), ou...  256 us
    unnamed x14, local copies, waits for them, and re-layouts  7.49 us

profile of v9, /device:TPU:0, one launch (start us, length us, event | category | flops | bytes accessed | tf_op | source)
XLA Modules:
  0.0 269.1 jit_solution(8227746986982733781)
XLA Ops:
  0.6 0.0 copy-start
  0.7 1.0 copy-done
  1.7 0.1 constant_dynamic-slice_fusion
  1.7 0.1 constant_dynamic-slice_fusion.1
  1.8 1.0 copy.17
  2.9 1.0 copy.21
  3.9 0.8 concatenate.3.refs_3_
  4.7 256.2 %layers.1 = (bf16[2,4,256,768]{3,2,1,0:T(8,128)(2,1)}, f32[192,1536]{1,0:T(8,128)}, f32[8,768]{1,0:T(8,128)}, f32[3,192,192]{2,1,0:T(8,128)}, f32[2,192]{1,0:T(2,128)}, /*index=5*/f32[192,1152]{1,0:T(8,128)}) custom-call(s32[2,8]{1,0:T(2,128)} %refs_0_.1, bf16[2,4,256,768]{3,2,1,0:T(8,128)(2,1)} %bitcast.37, bf16[2,192]{1,0:T(2,128)(2,1)} %bitcast.44, ...), custom_call_target="tpu_custom_call" | custom-call | tf_op jit(solution)/shard_map/layers/pallas_call | solution.py:1057
  260.9 0.0 copy-start.2
  261.0 1.3 fusion
  262.3 1.2 slice_bitcast_fusion.2
  263.4 0.8 copy.19
  264.2 0.0 copy-start.1
  264.3 1.1 copy.18
  265.3 0.0 copy-done.2
  265.3 1.1 slice_bitcast_fusion
  266.4 0.0 copy-done.1
  266.4 0.0 copy-start.3
  266.4 1.7 copy.24
  268.1 0.1 copy-done.3
  268.2 0.9 copy.25
  (8 shorter events, 0.1 us)
Async XLA Ops:
  0.6 1.0 copy-start
  260.9 4.4 %copy-start.2 = (f32[192,1536]{1,0:T(8,128)S(1)}, f32[192,1536]{1,0:T(8,128)}, u32[]{:S(2)}) copy-start(f32[192,1536]{1,0:T(8,128)} %get-tuple-element.17) | copy-start | bytes 3538948
  264.2 2.2 copy-start.1
  266.4 1.8 copy-start.3

commit v10 on v9

--- a/solution.py
+++ b/solution.py
@@ -826,6 +826,10 @@
         hidden_second = jnp.logical_and(even, turn < PIECES)
         hidden_piece = PIECES - 1 - jnp.where(step == last_ahead, PIECES - 1, turn)
 
+        @pl.when(jnp.logical_and(first, step == last_ahead))
+        def _():
+            backward_result(2)
+
         @pl.when(jnp.where(first, hidden_first, hidden_second))
         def _():
             backward_hidden(hidden_piece)
@@ -850,7 +854,8 @@
 
         @pl.when(jnp.where(first, mixed_first, mixed_second))
         def _():
-            @pl.when(place < PIECES - 1)
+            @pl.when(jnp.logical_and(
+                place < PIECES - 1, jnp.logical_or(second, step != last_ahead + 1)))
             def _():
                 backward_result(place + 1)
 

time: 270 us -> 270 us (level)
  no operation moved by 1% of the time
where the time goes in v10:
time: 270 us; the launch traced here: 269 us
  Pallas kernels  256 us (95%)
  local copies, waits for them, and re-layouts  12.1 us (4%)
    pallas_call x1, Pallas kernels, run_layers(): pl.pallas_call(functools.partial(layers_kernel, width, depth, inside), ou...  256 us
    unnamed x14, local copies, waits for them, and re-layouts  7.49 us

profile of v10, /device:TPU:0, one launch (start us, length us, event | category | flops | bytes accessed | tf_op | source)
XLA Modules:
  0.0 268.6 jit_solution(17120225793512351715)
XLA Ops:
  0.6 0.0 copy-start
  0.7 1.0 copy-done
  1.7 0.1 constant_dynamic-slice_fusion
  1.7 0.1 constant_dynamic-slice_fusion.1
  1.8 1.0 copy.17
  2.9 1.0 copy.21
  3.9 0.8 concatenate.3.refs_3_
  4.7 255.7 %layers.1 = (bf16[2,4,256,768]{3,2,1,0:T(8,128)(2,1)}, f32[192,1536]{1,0:T(8,128)}, f32[8,768]{1,0:T(8,128)}, f32[3,192,192]{2,1,0:T(8,128)}, f32[2,192]{1,0:T(2,128)}, /*index=5*/f32[192,1152]{1,0:T(8,128)}) custom-call(s32[2,8]{1,0:T(2,128)} %refs_0_.1, bf16[2,4,256,768]{3,2,1,0:T(8,128)(2,1)} %bitcast.37, bf16[2,192]{1,0:T(2,128)(2,1)} %bitcast.44, ...), custom_call_target="tpu_custom_call" | custom-call | tf_op jit(solution)/shard_map/layers/pallas_call | solution.py:1062
  260.5 0.0 copy-start.2
  260.5 1.3 fusion
  261.8 1.2 slice_bitcast_fusion.2
  263.0 0.8 copy.19
  263.8 0.0 copy-start.1
  263.8 1.1 copy.18
  264.8 0.0 copy-done.2
  264.8 1.1 slice_bitcast_fusion
  265.9 0.0 copy-done.1
  265.9 0.0 copy-start.3
  265.9 1.7 copy.24
  267.6 0.1 copy-done.3
  267.7 0.9 copy.25
  (8 shorter events, 0.1 us)
Async XLA Ops:
  0.6 1.0 copy-start
  260.5 4.4 %copy-start.2 = (f32[192,1536]{1,0:T(8,128)S(1)}, f32[192,1536]{1,0:T(8,128)}, u32[]{:S(2)}) copy-start(f32[192,1536]{1,0:T(8,128)} %get-tuple-element.17) | copy-start | bytes 3538948
  263.8 2.2 copy-start.1
  265.9 1.8 copy-start.3

commit v11 on v9

--- a/solution.py
+++ b/solution.py
@@ -863,14 +863,18 @@
         return carry
 
     lax.fori_loop(0, 2 * PIECES + 2, backward, 0)
-    backward_result(0)
-
     @pl.when(second)
     def _():
+        backward_result(0)
         down_grads()
         up_grads()
 
     head_grads()
+
+    @pl.when(first)
+    def _():
+        backward_result(0)
+
 
     def emit_stage(run):
         @pl.when(first)

time: 270 us -> 269 us (level)
  no operation moved by 1% of the time
where the time goes in v11:
time: 269 us; the launch traced here: 268 us
  Pallas kernels  255 us (95%)
  local copies, waits for them, and re-layouts  12.1 us (4%)
    pallas_call x1, Pallas kernels, run_layers(): pl.pallas_call(functools.partial(layers_kernel, width, depth, inside), ou...  255 us
    unnamed x14, local copies, waits for them, and re-layouts  7.49 us

profile of v11, /device:TPU:0, one launch (start us, length us, event | category | flops | bytes accessed | tf_op | source)
XLA Modules:
  0.0 268.2 jit_solution(13922195432949286567)
XLA Ops:
  0.6 0.0 copy-start
  0.7 1.0 copy-done
  1.7 0.1 constant_dynamic-slice_fusion
  1.7 0.1 constant_dynamic-slice_fusion.1
  1.8 1.0 copy.17
  2.9 1.0 copy.21
  3.9 0.8 concatenate.3.refs_3_
  4.7 255.2 %layers.1 = (bf16[2,4,256,768]{3,2,1,0:T(8,128)(2,1)}, f32[192,1536]{1,0:T(8,128)}, f32[8,768]{1,0:T(8,128)}, f32[3,192,192]{2,1,0:T(8,128)}, f32[2,192]{1,0:T(2,128)}, /*index=5*/f32[192,1152]{1,0:T(8,128)}) custom-call(s32[2,8]{1,0:T(2,128)} %refs_0_.1, bf16[2,4,256,768]{3,2,1,0:T(8,128)(2,1)} %bitcast.37, bf16[2,192]{1,0:T(2,128)(2,1)} %bitcast.44, ...), custom_call_target="tpu_custom_call" | custom-call | tf_op jit(solution)/shard_map/layers/pallas_call | solution.py:1061
  260.0 0.0 copy-start.2
  260.0 1.3 fusion
  261.3 1.2 slice_bitcast_fusion.2
  262.5 0.8 copy.19
  263.3 0.0 copy-start.1
  263.3 1.1 copy.18
  264.4 0.0 copy-done.2
  264.4 1.1 slice_bitcast_fusion
  265.5 0.0 copy-done.1
  265.5 0.0 copy-start.3
  265.5 1.7 copy.24
  267.1 0.1 copy-done.3
  267.2 0.9 copy.25
  (8 shorter events, 0.1 us)
Async XLA Ops:
  0.6 1.0 copy-start
  260.0 4.4 %copy-start.2 = (f32[192,1536]{1,0:T(8,128)S(1)}, f32[192,1536]{1,0:T(8,128)}, u32[]{:S(2)}) copy-start(f32[192,1536]{1,0:T(8,128)} %get-tuple-element.17) | copy-start | bytes 3538948
  263.3 2.2 copy-start.1
  265.5 1.8 copy-start.3
